TPU v7x, 256 devices: a whole 4x4x8 slice. The times are simulated.
256 devices in a mesh: seq: 64 (over z_hi, y, x, core), kv: 4 (over z_lo).
Axes of the slice: x: 4, y: 4, z: 8 (z_hi: 2, z_lo: 4; z = z_hi * 4 + z_lo), core: 2. Of those that a mesh axis runs over, the one named last changes fastest.
Arguments:
- queries: bfloat16 [32768, 4096], P('seq', 'kv'), may hold values from -8 to 8, as said below
- keys: bfloat16 [32768, 1024], P('seq', 'kv'), may hold values from -8 to 8, as said below
- values: bfloat16 [32768, 1024], P('seq', 'kv'), may hold values from -6 to 6
- kept_index: int32 [64, 32, 4], P('seq', 'kv'), may hold values from 0 to 3
- kept_count: int32 [64, 32], P('seq', 'kv'), may hold values from 3 to 4
- owner: int32 [64, 32, 4], P('seq', 'kv'), may hold values from 0 to 63, as said below
Outputs:
- attended: bfloat16 [32768, 4096], P('seq', 'kv')
- block_scores: float32 [32, 256], P('kv', 'seq')
- recv_keys: bfloat16 [64, 4, 64, 1, 128, 128], P('seq', 'kv')
- recv_values: bfloat16 [64, 4, 64, 1, 128, 128], P('seq', 'kv')
- recv_scores: bfloat16 [64, 4, 64, 1], P('seq', 'kv')
Inputs may be any that keep to these rules, and one draw needn't show every extreme that they name: `queries`: entries of order one. `keys`: entries of order one. `kept_index`: a list may repeat a block. Entries c >= kept_count are padding and are not delivered. Within one shard and one lane no owner is named by more than 1 entries, valid or not; in each lane one owner is named by the first entry of the lane's first head in every shard.
All inputs are finite; a program needn't handle non-finite values.
Results may differ from a plain program's by a relative error of at most 0.0075.
Values may be sent and summed in bfloat16 or wider, within the bound.
No kernel may reach another device: no remote copies, remote signals or barrier semaphores. Data moves between devices by JAX's collectives and lax.ppermute only.
A program may use at most 128 MiB of HBM per device.

v0:
```python
import math

import jax
import jax.numpy as jnp
from jax import lax
from jax.sharding import PartitionSpec as P

HD = 128
CYCLE = 4
OBS = 64
BLOCK = 128


def shifted(shard, axis, by):
    length = lax.axis_size(axis)
    pairs = [(i, i + by) for i in range(length) if 0 <= i + by < length]
    return lax.ppermute(shard, axis, pairs)


def from_root(shard, axis, root):
    mine = lax.axis_index(axis) == root
    return lax.psum(jnp.where(mine, shard, jnp.zeros_like(shard)), axis)


def joined(value, axis, join):
    pieces = jax.tree.map(lambda part: lax.all_gather(part, axis), value)
    head = jax.tree.map(lambda part: part[0], pieces)
    tail = jax.tree.map(lambda part: part[1:], pieces)
    subtotal, _ = lax.scan(lambda subtotal, piece: (join(subtotal, piece), None), head, tail)
    return subtotal


def merge_totals(first, second):
    peak = jnp.maximum(first[0], second[0])
    mass = first[1] * jnp.exp(first[0] - peak) + second[1] * jnp.exp(second[0] - peak)
    return (peak, mass)


def attend_block(state, query_rows, key_piece, value_piece, seen, scale):
    peak, mass, accum = state
    shard_len, lane_kv = (key_piece.shape[0], key_piece.shape[1] // HD)
    key_rows = key_piece.reshape(shard_len, lane_kv, HD)
    value_rows = value_piece.reshape(shard_len, lane_kv, HD)
    score = (
        jnp.einsum("tkgd,jkd->kgtj", query_rows, key_rows, preferred_element_type=jnp.float32)
        * scale
    )
    score = jnp.where(seen, score, -1e30)
    new_peak = jnp.maximum(peak, jnp.max(score, axis=-1))
    fading = jnp.exp(peak - new_peak)
    weights = jnp.exp(score - new_peak[..., None])
    mass = mass * fading + jnp.sum(weights, axis=-1)
    update = jnp.einsum(
        "kgtj,jkd->kgtd",
        weights.astype(jnp.bfloat16),
        value_rows,
        preferred_element_type=jnp.float32,
    )
    accum = accum * fading[..., None] + update
    return (new_peak, mass, accum)


def shards(queries, keys, values, kept_index, kept_count, owner):
    shard_len = keys.shape[0]
    lane_kv = keys.shape[1] // HD
    lane_heads = queries.shape[1] // HD
    group = lane_heads // lane_kv
    blocks_here = shard_len // BLOCK
    seq_count = lax.axis_size("seq")
    position = lax.axis_index("seq")
    scale = 1.0 / math.sqrt(HD)
    query_rows = queries.reshape(shard_len, lane_kv, group, HD)
    row_ids = jnp.arange(shard_len, dtype=jnp.int32)
    causal = row_ids[None, :] <= row_ids[:, None]
    start_state = (
        jnp.full((lane_kv, group, shard_len), -1e30, jnp.float32),
        jnp.zeros((lane_kv, group, shard_len), jnp.float32),
        jnp.zeros((lane_kv, group, shard_len, HD), jnp.float32),
    )
    state = attend_block(start_state, query_rows, keys, values, causal, scale)
    carried_keys = keys
    carried_values = values
    for distance in range(1, CYCLE):
        carried_keys, carried_values = shifted((carried_keys, carried_values), "seq", 1)
        seen = jnp.broadcast_to(position >= distance, (shard_len, shard_len))
        state = attend_block(state, query_rows, carried_keys, carried_values, seen, scale)
    final_mass = state[1]
    final_accum = state[2]
    mixed = final_accum / final_mass[..., None]
    attended = (
        jnp.transpose(mixed, (2, 0, 1, 3)).reshape(shard_len, lane_heads * HD).astype(jnp.bfloat16)
    )
    tail = queries[shard_len - OBS :]
    observers = from_root(tail, "seq", seq_count - 1)
    observer_rows = observers.reshape(OBS, lane_kv, group, HD)
    key_rows = keys.reshape(shard_len, lane_kv, HD)
    score = (
        jnp.einsum("okgd,tkd->kgot", observer_rows, key_rows, preferred_element_type=jnp.float32)
        * scale
    )
    key_pos = position * shard_len + row_ids
    obs_pos = shard_len * seq_count - OBS + jnp.arange(OBS, dtype=jnp.int32)
    visible = key_pos[None, :] <= obs_pos[:, None]
    score = jnp.where(visible, score, -jnp.inf)
    local_peak = jnp.max(score, axis=-1)
    local_mass = jnp.sum(jnp.exp(score - local_peak[..., None]), axis=-1)
    top_peak, top_mass = joined((local_peak, local_mass), "seq", merge_totals)
    prob = jnp.exp(score - top_peak[..., None]) / top_mass[..., None]
    per_key = jnp.sum(prob, axis=2)
    scores_here = jnp.sum(per_key.reshape(lane_heads, blocks_here, BLOCK), axis=-1) * (
        blocks_here * seq_count / OBS
    )
    keep_len = kept_index.shape[2]
    capacity = (lane_heads * keep_len + seq_count - 1) // seq_count
    entries = lane_heads * keep_len
    entry_ids = jnp.arange(entries, dtype=jnp.int32)
    entry_head = entry_ids // keep_len
    entry_slot = entry_ids % keep_len
    counts = jnp.repeat(kept_count.reshape(lane_heads), keep_len)
    valid = entry_slot < counts
    owners = owner.reshape(entries)
    picks = kept_index.reshape(entries)
    earlier = (
        (owners[:, None] == owners[None, :])
        & valid[None, :]
        & (entry_ids[None, :] < entry_ids[:, None])
    )
    ranks = jnp.sum(earlier.astype(jnp.int32), axis=1)
    target = owners * capacity + ranks
    seat_ids = jnp.arange(seq_count * capacity, dtype=jnp.int32)
    placing = (valid[:, None] & (target[:, None] == seat_ids[None, :])).astype(jnp.float32)
    unit = picks * lane_kv + entry_head // group
    unit_ids = jnp.arange(blocks_here * lane_kv, dtype=jnp.int32)
    source_pick = (unit[:, None] == unit_ids[None, :]).astype(jnp.float32)
    selector = jnp.dot(placing.T, source_pick, precision=lax.Precision.HIGHEST).astype(jnp.bfloat16)
    key_flat = jnp.transpose(keys.reshape(blocks_here, BLOCK, lane_kv, HD), (0, 2, 1, 3)).reshape(
        blocks_here * lane_kv, BLOCK * HD
    )
    value_flat = jnp.transpose(
        values.reshape(blocks_here, BLOCK, lane_kv, HD), (0, 2, 1, 3)
    ).reshape(blocks_here * lane_kv, BLOCK * HD)
    send_keys = (
        jnp.dot(selector, key_flat, preferred_element_type=jnp.float32)
        .astype(jnp.bfloat16)
        .reshape(seq_count, capacity, BLOCK, HD)
    )
    send_values = (
        jnp.dot(selector, value_flat, preferred_element_type=jnp.float32)
        .astype(jnp.bfloat16)
        .reshape(seq_count, capacity, BLOCK, HD)
    )
    head_pick = (entry_head[:, None] == jnp.arange(lane_heads, dtype=jnp.int32)[None, :]).astype(
        jnp.float32
    )
    block_pick = (picks[:, None] == jnp.arange(blocks_here, dtype=jnp.int32)[None, :]).astype(
        jnp.float32
    )
    head_rows = jnp.dot(head_pick, scores_here, precision=lax.Precision.HIGHEST)
    entry_score = jnp.sum(head_rows * block_pick, axis=1)
    send_scores = jnp.dot(placing.T, entry_score[:, None], precision=lax.Precision.HIGHEST).astype(
        jnp.bfloat16
    )
    got_keys = lax.all_to_all(send_keys, "seq", split_axis=0, concat_axis=0, tiled=True)
    got_values = lax.all_to_all(send_values, "seq", split_axis=0, concat_axis=0, tiled=True)
    got_scores = lax.all_to_all(send_scores, "seq", split_axis=0, concat_axis=0, tiled=True)
    delivered = (
        got_keys.reshape(1, 1, seq_count, capacity, BLOCK, HD),
        got_values.reshape(1, 1, seq_count, capacity, BLOCK, HD),
        got_scores.reshape(1, 1, seq_count, capacity),
    )
    scores_here, delivered = (scores_here, delivered)
    return (attended, scores_here, delivered[0], delivered[1], delivered[2])


def solution(mesh):
    placed = (
        P("seq", "kv"),
        P("seq", "kv"),
        P("seq", "kv"),
        P("seq", "kv", None),
        P("seq", "kv"),
        P("seq", "kv", None),
    )
    return jax.shard_map(
        shards,
        mesh=mesh,
        in_specs=placed,
        out_specs=(
            P("seq", "kv"),
            P("kv", "seq"),
            P("seq", "kv", None, None, None, None),
            P("seq", "kv", None, None, None, None),
            P("seq", "kv", None, None),
        ),
        check_vma=False,
    )
```

profile of v0, /device:TPU:192, one launch (start us, length us, event | category | flops | bytes accessed | tf_op | source)
XLA Modules:
  0.0 1156.0 jit_solution(5159661450096377449)
XLA Ops:
  7.2 0.9 slice_select_fusion
  8.9 0.8 copy.160
  10.6 0.8 copy.159
  12.0 1.0 reshape.254
  13.0 1.1 reshape.269
  14.2 713.9 %all-reduce.2.cloned.1.call-done = bf16[64,2,4,128]{3,0,2,1:T(8,128)(2,1)} async-done(((bf16[64,2,4,128]{3,0,2,1:T(8,128)(2,1)}), bf16[64,2,4,128]{3,0,2,1:T(8,128)(2,1)}) %all-reduce.2.cloned.1.call-update) | async-done | bytes 131088 | tf_op jit(solution)/shard_map/psum | solution.py:22
  728.1 1.3 fusion.87
  729.8 112.9 %all-gather.1 = f32[128,4,64]{2,1,0:T(4,128)S(1)} all-gather(f32[2,4,64]{2,1,0:T(4,128)S(1)} %exponential_reduce_fusion), channel_id=3, replica_groups=mesh['seq'=64,'kv'=4] {'seq'}, dimensions={0}, use_global_device_ids=true | all-gather | bytes 133120 | tf_op jit(solution)/shard_map/all_gather | solution.py:26
  842.7 108.4 %all-gather = f32[128,4,64]{2,1,0:T(4,128)S(1)} all-gather(f32[2,4,64]{2,1,0:T(4,128)S(1)} %get-tuple-element.94), channel_id=2, replica_groups=mesh['seq'=64,'kv'=4] {'seq'}, dimensions={0}, use_global_device_ids=true | all-gather | bytes 133120 | tf_op jit(solution)/shard_map/all_gather | solution.py:26
  951.2 2.8 while.12
  955.6 9.0 all-to-all-start.2
  965.4 1.9 copy.195
  967.3 4.5 all-to-all-done.2
  971.7 9.5 all-to-all-start
  981.2 0.8 copy.143
  982.1 2.0 collective-permute-start
  984.1 3.4 collective-permute-start.1
  987.5 1.8 reshape.255
  989.3 1.8 copy.184
  991.1 1.0 reshape.273
  992.9 1.9 copy.197
  994.9 5.8 fusion.7
  1000.8 1.1 reduce
  1001.8 41.1 %collective-permute-done.1 = bf16[512,256]{1,0:T(8,128)(2,1)} collective-permute-done((bf16[512,256]{1,0:T(8,128)(2,1)}, bf16[512,256]{1,0:T(8,128)(2,1)}, u32[]{:S(2)}, u32[]{:S(2)}) %collective-permute-start.1) | collective-permute-done | bytes 262176 | tf_op jit(solution)/shard_map/ppermute | solution.py:17
  1042.9 1.9 collective-permute-start.3
  1044.9 1.8 copy.146
  1046.7 1.9 collective-permute-start.2
  1048.6 5.6 bitcast_reduce_fusion.2
  1054.2 5.9 collective-permute-done.3
  1060.2 1.8 copy.150
  1062.0 1.9 collective-permute-start.5
  1063.9 2.1 collective-permute-start.4
  1066.0 5.6 bitcast_reduce_fusion.1
  1071.6 6.5 collective-permute-done.5
  1078.1 1.8 copy.154
  1079.9 1.0 collective-permute-done.4
  1080.9 5.6 bitcast_reduce_fusion
  1086.5 7.6 fusion.5
  1094.1 8.1 all-to-all-start.1
  1102.3 7.7 fusion.10
  1110.0 6.2 fusion.16
  1116.3 2.2 fusion.18
  1118.5 2.5 fusion.20
  1121.0 2.6 fusion.27
  1123.6 1.3 copy.166
  1124.9 19.7 %all-to-all-done.1 = bf16[64,1,128,128]{3,2,1,0:T(8,128)(2,1)} async-done(((bf16[64,1,128,128]{3,2,1,0:T(8,128)(2,1)}), bf16[64,1,128,128]{3,2,1,0:T(8,128)(2,1)}, u32[]{:S(2)}, u32[]{:S(2)}) %all-to-all-start.1) | async-done | bytes 2097184 | tf_op jit(solution)/shard_map/all_to_all | solution.py:164
  1144.7 1.3 copy.244
  1146.0 3.2 copy.245
  (132 shorter events, 8.0 us)
Async XLA Ops:
  7.2 721.0 %all-reduce.2.cloned.1.call-start = ((), (), s32[]{:S(2)}) async-start(), calls=%async_computation.3 | async-start | bytes 262144 | tf_op jit(solution)/shard_map/psum | solution.py:22
  13.0 716.4 %copy-start.1 = (bf16[512,2,128]{2,1,0:T(2,128)(2,1)}, bf16[512,2,128]{2,1,0:T(2,128)(2,1)S(1)}, u32[]{:S(2)}) copy-start(bf16[512,2,128]{2,1,0:T(2,128)(2,1)S(1)} %reshape.254) | copy-start | bytes 786436
  14.2 967.0 %copy-start = (bf16[512,256]{1,0:T(8,128)(2,1)S(1)}, bf16[512,256]{1,0:T(8,128)(2,1)}, u32[]{:S(2)}) copy-start(bf16[512,256]{1,0:T(8,128)(2,1)} %param.9) | copy-start | bytes 786436
  954.4 38.5 %copy-start.6 = (f32[8,4]{0,1:T(4,128)}, f32[8,4]{0,1:T(4,128)S(1)}, u32[]{:S(2)}) copy-start(f32[8,4]{0,1:T(4,128)S(1)} %broadcast_multiply_fusion) | copy-start | bytes 388
  955.6 16.1 %all-to-all-start.2 = ((bf16[64,1,1]{2,1,0:T(2,128)(2,1)}), bf16[64,1,1]{2,1,0:T(2,128)(2,1)S(1)}, u32[]{:S(2)}, u32[]{:S(2)}) async-start(bf16[64,1,1]{2,1,0:T(2,128)(2,1)} %copy.165), calls=%async_computation.2 | async-start | bytes 65536 | tf_op jit(solution)/shard_map/all_to_all | solution.py:165
  971.7 122.4 %all-to-all-start = ((bf16[64,1,128,128]{3,2,1,0:T(8,128)(2,1)}), bf16[64,1,128,128]{3,2,1,0:T(8,128)(2,1)S(1)}, u32[]{:S(2)}, u32[]{:S(2)}) async-start(bf16[64,1,128,128]{3,2,1,0:T(8,128)(2,1)} %bitcast.250), calls=%async_computation | async-start | bytes 4194304 | tf_op jit(solution)/shard_map/all_to_all | solution.py:163
  982.1 64.6 %collective-permute-start = (bf16[512,256]{0,1:T(8,128)(2,1)}, bf16[512,256]{0,1:T(8,128)(2,1)}, u32[]{:S(2)}, u32[]{:S(2)}) collective-permute-start(bf16[512,256]{0,1:T(8,128)(2,1)} %copy.143), channel_id=1, source_target_pairs={{0,4},{4,8},{8,12},{12,16},{16,20},{20,24},{24,28},{28,32},{32,36}... | collective-permute-start | bytes 786440 | tf_op jit(solution)/shard_map/ppermute | solution.py:17
  984.1 58.8 %collective-permute-start.1 = (bf16[512,256]{1,0:T(8,128)(2,1)}, bf16[512,256]{1,0:T(8,128)(2,1)}, u32[]{:S(2)}, u32[]{:S(2)}) collective-permute-start(bf16[512,256]{1,0:T(8,128)(2,1)} %param.10), channel_id=1, source_target_pairs={{0,4},{4,8},{8,12},{12,16},{16,20},{20,24},{24,28},{28,32},{32,36}... | collective-permute-start | bytes 786440 | tf_op jit(solution)/shard_map/ppermute | solution.py:17
  1042.9 17.2 %collective-permute-start.3 = (bf16[512,256]{1,0:T(8,128)(2,1)}, bf16[512,256]{1,0:T(8,128)(2,1)}, u32[]{:S(2)}, u32[]{:S(2)}) collective-permute-start(bf16[512,256]{1,0:T(8,128)(2,1)} %collective-permute-done.1), channel_id=1, source_target_pairs={{0,4},{4,8},{8,12},{12,16},{16,20},{20,24},{24,28},{28,32},{32,36}... | collective-permute-start | bytes 786440 | tf_op jit(solution)/shard_map/ppermute | solution.py:17
  1046.7 17.2 %collective-permute-start.2 = (bf16[512,256]{0,1:T(8,128)(2,1)}, bf16[512,256]{0,1:T(8,128)(2,1)}, u32[]{:S(2)}, u32[]{:S(2)}) collective-permute-start(bf16[512,256]{0,1:T(8,128)(2,1)} %collective-permute-done), channel_id=1, source_target_pairs={{0,4},{4,8},{8,12},{12,16},{16,20},{20,24},{24,28},{28,32},{32,36}... | collective-permute-start | bytes 786440 | tf_op jit(solution)/shard_map/ppermute | solution.py:17
  1062.0 16.1 %collective-permute-start.5 = (bf16[512,256]{1,0:T(8,128)(2,1)}, bf16[512,256]{1,0:T(8,128)(2,1)}, u32[]{:S(2)}, u32[]{:S(2)}) collective-permute-start(bf16[512,256]{1,0:T(8,128)(2,1)} %collective-permute-done.3), channel_id=1, source_target_pairs={{0,4},{4,8},{8,12},{12,16},{16,20},{20,24},{24,28},{28,32},{32,36}... | collective-permute-start | bytes 786440 | tf_op jit(solution)/shard_map/ppermute | solution.py:17
  1063.9 17.0 %collective-permute-start.4 = (bf16[512,256]{0,1:T(8,128)(2,1)}, bf16[512,256]{0,1:T(8,128)(2,1)}, u32[]{:S(2)}, u32[]{:S(2)}) collective-permute-start(bf16[512,256]{0,1:T(8,128)(2,1)} %collective-permute-done.2), channel_id=1, source_target_pairs={{0,4},{4,8},{8,12},{12,16},{16,20},{20,24},{24,28},{28,32},{32,36}... | collective-permute-start | bytes 786440 | tf_op jit(solution)/shard_map/ppermute | solution.py:17
  1094.1 50.5 %all-to-all-start.1 = ((bf16[64,1,128,128]{3,2,1,0:T(8,128)(2,1)}), bf16[64,1,128,128]{3,2,1,0:T(8,128)(2,1)}, u32[]{:S(2)}, u32[]{:S(2)}) async-start(bf16[64,1,128,128]{3,2,1,0:T(8,128)(2,1)} %bitcast.249), calls=%async_computation.1 | async-start | bytes 4194304 | tf_op jit(solution)/shard_map/all_to_all | solution.py:164
  1102.2 14.0 %slice-start = ((s8[8388608]{0:T(1024)(128)(4,1)}), s8[4194304]{0:T(1024)(128)(4,1)S(1)}, s32[]{:S(2)}) async-start(s8[8388608]{0:T(1024)(128)(4,1)} %bitcast.242), calls=%async_computation.4 | async-start | bytes 8388608
  1102.2 7.8 copy-start.4
  1102.2 14.0 %slice-start.1 = ((s8[8388608]{0:T(1024)(128)(4,1)}), s8[4194304]{0:T(1024)(128)(4,1)S(1)}, s32[]{:S(2)}) async-start(s8[8388608]{0:T(1024)(128)(4,1)} %bitcast.242), calls=%async_computation.5 | async-start | bytes 8388608
  1102.2 16.2 %slice-start.4 = ((s8[8388608]{0:T(1024)(128)(4,1)}), s8[4194304]{0:T(1024)(128)(4,1)S(1)}, s32[]{:S(2)}) async-start(s8[8388608]{0:T(1024)(128)(4,1)} %bitcast.246), calls=%async_computation.8 | async-start | bytes 8388608
  1110.0 6.3 copy-start.3
  1110.0 8.4 slice-start.5
  1116.2 2.3 copy-start.2
  1116.2 4.7 slice-start.2
  1118.4 2.5 copy-start.5
  1118.5 2.5 slice-start.3
Sparse Core Ops, SparseCore 0:
  11.2 716.8 all-reduce.1
where the time goes:
time: 1160 us
  waiting for transfers between devices  793 us (68%)
  blocking collectives  221 us (19%)
  starting transfers between devices  39.8 us (3%)
  matrix products  39.5 us (3%)
  local copies, waits for them, and re-layouts  26.8 us (2%)
  other arithmetic  20.3 us (2%)
  between operations  14.6 us (1%)
    psum x1, waiting for transfers between devices, from_root(): return lax.psum(jnp.where(mine, shard, jnp.zeros_like(shard)), axis)  714 us
    all_gather x2, blocking collectives, joined(): pieces = jax.tree.map(lambda part: lax.all_gather(part, axis), value)  221 us
    ppermute x6, waiting for transfers between devices, shifted(): return lax.ppermute(shard, axis, pairs)  54.5 us
  transfers between devices with their start and end apart: 10, of which 7 were waited for; matrix products, arithmetic and copies ran while one was open for 7% of the time, Pallas kernels for 0%

commit v1 on v0

v1 whole, which is shorter than its diff:
```python
import math

import jax
import jax.numpy as jnp
from jax import lax
from jax.experimental import pallas as pl
from jax.experimental.pallas import tpu as pltpu
from jax.sharding import Mesh, PartitionSpec as P

HD = 128
CYCLE = 4
OBS = 64
BLOCK = 128
SHARD = 512
HEADS = 8
KVS = 2
GROUP = 4
KEEP = 4
BLKS = 4
NSEQ = 64
HALF = 32
SEQ = ("zh", "y", "x", "c")
PLANE = ("y", "x", "c")
LOG2E = 1.4426950408889634
COEF = LOG2E / math.sqrt(HD)
SCALE = 1.0 / math.sqrt(HD)
BIG = 1e30
NT = (((1,), (1,)), ((), ()))


def f32dot(a, b, dims):
    return lax.dot_general(a, b, dims, preferred_element_type=jnp.float32)


def attend_kernel(pos_ref, q_ref, k0, k1, k2, k3, v0, v1, v2, v3, o_ref):
    pos = pos_ref[0]
    half = SHARD // 2
    ones = jnp.ones((SHARD, HD), jnp.bfloat16)
    vext = [jnp.concatenate([v[...], ones], axis=1) for v in (v0, v1, v2, v3)]
    row = lax.broadcasted_iota(jnp.int32, (half, half), 0)
    col = lax.broadcasted_iota(jnp.int32, (half, half), 1)
    causal = col <= row
    for tile in range(2):
        q = q_ref[tile * half : (tile + 1) * half, :]
        diag = f32dot(q, k0[tile * half : (tile + 1) * half, :], NT)
        diag = jnp.where(causal, diag, -BIG)
        peak = jnp.max(diag, axis=1, keepdims=True)
        full = []
        if tile == 1:
            own = f32dot(q, k0[:half, :], NT)
            peak = jnp.maximum(peak, jnp.max(own, axis=1, keepdims=True))
            full.append(own)
        past = [f32dot(q, k[...], NT) for k in (k1, k2, k3)]
        for distance, score in enumerate(past, 1):
            here = jnp.max(score, axis=1, keepdims=True)
            peak = jnp.where(pos >= distance, jnp.maximum(peak, here), peak)
        shift = peak * COEF
        weight = jnp.exp2(diag * COEF - shift).astype(jnp.bfloat16)
        acc = f32dot(weight, vext[0][tile * half : (tile + 1) * half], (((1,), (0,)), ((), ())))
        if tile == 1:
            weight = jnp.exp2(full[0] * COEF - shift).astype(jnp.bfloat16)
            acc += f32dot(weight, vext[0][:half], (((1,), (0,)), ((), ())))
        for distance, score in enumerate(past, 1):
            lift = jnp.where(pos >= distance, shift, BIG)
            weight = jnp.exp2(score * COEF - lift).astype(jnp.bfloat16)
            acc += f32dot(weight, vext[distance], (((1,), (0,)), ((), ())))
        mixed = acc[:, :HD] / acc[:, HD:]
        o_ref[tile * half : (tile + 1) * half, :] = mixed.astype(jnp.bfloat16)


def attend(position, queries, ks, vs):
    kv_spec = pl.BlockSpec((SHARD, HD), lambda h: (0, h // GROUP))
    return pl.pallas_call(
        attend_kernel,
        grid=(HEADS,),
        out_shape=jax.ShapeDtypeStruct((SHARD, HEADS * HD), jnp.bfloat16),
        in_specs=[
            pl.BlockSpec(memory_space=pltpu.SMEM),
            pl.BlockSpec((SHARD, HD), lambda h: (0, h)),
        ]
        + [kv_spec] * 8,
        out_specs=pl.BlockSpec((SHARD, HD), lambda h: (0, h)),
        compiler_params=pltpu.CompilerParams(vmem_limit_bytes=32 * 1024 * 1024),
        cost_estimate=pl.CostEstimate(
            flops=HEADS * SHARD * SHARD * 4 * HD * 4,
            bytes_accessed=4 * 1024 * 1024,
            transcendentals=HEADS * SHARD * SHARD * 4,
        ),
        name="attend",
    )(position, queries, *ks, *vs)


def pack_kernel(base_ref, meta_ref, k_ref, v_ref, out_ref):
    base = base_ref[0]
    out_ref[...] = jnp.zeros_like(out_ref)
    for head in range(HEADS):
        lo = (head // GROUP) * HD
        for c in range(KEEP):
            seat = meta_ref[c, head] - base
            rows = pl.ds(pl.multiple_of(meta_ref[KEEP + c, head] * BLOCK, BLOCK), BLOCK)

            @pl.when((seat >= 0) & (seat < HALF))
            def _():
                out_ref[seat, 0] = k_ref[rows, lo : lo + HD]
                out_ref[seat, 1] = v_ref[rows, lo : lo + HD]


def pack(base, meta, keys, values):
    return pl.pallas_call(
        pack_kernel,
        out_shape=jax.ShapeDtypeStruct((HALF, 2, BLOCK, HD), jnp.bfloat16),
        in_specs=[
            pl.BlockSpec(memory_space=pltpu.SMEM),
            pl.BlockSpec(memory_space=pltpu.SMEM),
            pl.BlockSpec(memory_space=pltpu.VMEM),
            pl.BlockSpec(memory_space=pltpu.VMEM),
        ],
        out_specs=pl.BlockSpec(memory_space=pltpu.VMEM),
        compiler_params=pltpu.CompilerParams(vmem_limit_bytes=16 * 1024 * 1024),
        cost_estimate=pl.CostEstimate(flops=0, bytes_accessed=5 * 1024 * 1024, transcendentals=0),
        name="pack",
    )(base, meta, keys, values)


def observe_kernel(pos_ref, meta_ref, q_ref, k_ref, msg_ref, frac_ref, level_ref):
    pos = pos_ref[0]
    levels = []
    fracs = [[] for _ in range(BLKS)]
    for kv in range(KVS):
        rows = [
            q_ref[:, (kv * GROUP + g) * HD : (kv * GROUP + g + 1) * HD] for g in range(GROUP)
        ]
        stacked = jnp.concatenate(rows, axis=0)
        score = f32dot(k_ref[:, kv * HD : (kv + 1) * HD], stacked, NT) * SCALE
        key = lax.broadcasted_iota(jnp.int32, score.shape, 0)
        lane = lax.broadcasted_iota(jnp.int32, score.shape, 1)
        limit = (NSEQ - pos) * SHARD - OBS + lax.rem(lane, OBS)
        score = jnp.where(key <= limit, score, -jnp.inf)
        peak = jnp.max(score, axis=0, keepdims=True)
        expo = jnp.exp(score - peak)
        sums = [
            jnp.sum(expo[b * BLOCK : (b + 1) * BLOCK], axis=0, keepdims=True) for b in range(BLKS)
        ]
        mass = (sums[0] + sums[1]) + (sums[2] + sums[3])
        level = peak + jnp.log(mass)
        for side in range(2):
            cut = slice(side * 128, (side + 1) * 128)
            levels.append(level[:, cut])
            for b in range(BLKS):
                fracs[b].append((sums[b] / mass)[:, cut])
    level4 = jnp.concatenate(levels, axis=0)
    level_ref[...] = level4
    for b in range(BLKS):
        frac_ref[b] = jnp.concatenate(fracs[b], axis=0)
    blank = jnp.concatenate([level4, jnp.zeros_like(level4)], axis=0)
    msg_ref[...] = jnp.broadcast_to(blank[None], msg_ref.shape)
    which = lax.broadcasted_iota(jnp.int32, (4, 128), 0) * 2 + (
        lax.broadcasted_iota(jnp.int32, (4, 128), 1) // OBS
    )
    for head in range(HEADS):
        for c in range(KEEP):
            target = meta_ref[c, head]
            unit = meta_ref[KEEP + c, head]

            @pl.when(target >= 0)
            def _():
                msg_ref[target, 4:8, :] = jnp.where(which == head, frac_ref[unit], 0.0)


def observe(position, meta, observers, keys):
    smem = pl.BlockSpec(memory_space=pltpu.SMEM)
    vmem = pl.BlockSpec(memory_space=pltpu.VMEM)
    return pl.pallas_call(
        observe_kernel,
        out_shape=(
            jax.ShapeDtypeStruct((NSEQ, 8, 128), jnp.float32),
            jax.ShapeDtypeStruct((BLKS, 4, 128), jnp.float32),
            jax.ShapeDtypeStruct((4, 128), jnp.float32),
        ),
        in_specs=[smem, smem, vmem, vmem],
        out_specs=(vmem, vmem, vmem),
        compiler_params=pltpu.CompilerParams(vmem_limit_bytes=16 * 1024 * 1024),
        name="observe",
    )(position, meta, observers, keys)


def finish_kernel(got_ref, frac_ref, level_ref, recv_ref, block_ref):
    level = got_ref[:, 0:4, :]
    top = jnp.max(level, axis=0)
    total = top + jnp.log(jnp.sum(jnp.exp(level - top[None]), axis=0))
    share = got_ref[:, 4:8, :] * jnp.exp(level - total[None])
    factor = BLKS * NSEQ / OBS
    recv = jnp.sum(jnp.sum(share, axis=1), axis=1, keepdims=True) * factor
    recv_ref[...] = recv.astype(jnp.bfloat16)
    own = jnp.exp(level_ref[...] - total)
    side = lax.broadcasted_iota(jnp.int32, (HEADS, 128), 1) // OBS
    odd = lax.rem(lax.broadcasted_iota(jnp.int32, (HEADS, 128), 0), 2)
    columns = []
    for b in range(BLKS):
        part = frac_ref[b] * own
        twice = jnp.concatenate([part[h // 2 : h // 2 + 1] for h in range(HEADS)], axis=0)
        picked = jnp.where(side == odd, twice, 0.0)
        columns.append(jnp.sum(picked, axis=1, keepdims=True))
    block_ref[...] = jnp.concatenate(columns, axis=1) * factor


def finish(got, frac, level):
    vmem = pl.BlockSpec(memory_space=pltpu.VMEM)
    return pl.pallas_call(
        finish_kernel,
        out_shape=(
            jax.ShapeDtypeStruct((NSEQ, 1), jnp.bfloat16),
            jax.ShapeDtypeStruct((HEADS, BLKS), jnp.float32),
        ),
        in_specs=[vmem] * 3,
        out_specs=(vmem, vmem),
        name="finish",
    )(got, frac, level)


def place_kernel(half_ref, got_ref, *refs):
    key_ref, value_ref, sems = refs[-3:]
    half = half_ref[0]
    one = pltpu.make_async_copy(got_ref.at[:, 0], key_ref.at[pl.ds(half * HALF, HALF)], sems.at[0])
    two = pltpu.make_async_copy(
        got_ref.at[:, 1], value_ref.at[pl.ds(half * HALF, HALF)], sems.at[1]
    )
    one.start()
    two.start()
    one.wait()
    two.wait()


def place(half, got, earlier=None):
    any_ = pl.BlockSpec(memory_space=pl.ANY)
    shape = jax.ShapeDtypeStruct((NSEQ, BLOCK, HD), jnp.bfloat16)
    operands = (half, got) if earlier is None else (half, got) + tuple(earlier)
    return pl.pallas_call(
        place_kernel,
        out_shape=(shape, shape),
        in_specs=[pl.BlockSpec(memory_space=pltpu.SMEM)] + [any_] * (len(operands) - 1),
        out_specs=(any_, any_),
        scratch_shapes=[pltpu.SemaphoreType.DMA((2,))],
        input_output_aliases={} if earlier is None else {2: 0, 3: 1},
        cost_estimate=pl.CostEstimate(flops=0, bytes_accessed=4 * 1024 * 1024, transcendentals=0),
        name="place",
    )(*operands)


def spread(tail):
    me = lax.axis_index(SEQ)
    held = jnp.where(me == NSEQ - 1, tail, jnp.zeros_like(tail))

    def index(zh, y, x, c):
        return ((zh * 4 + y) * 4 + x) * 2 + c

    steps = (
        [[(index(1, 3, 3, 1), index(1, y, 3, 1))] for y in range(3)],
        [[(index(1, y, 3, 1), index(1, y, x, 1)) for y in range(4)] for x in range(3)],
        [
            [(index(1, y, x, 1), index(zh, y, x, c)) for y in range(4) for x in range(4)]
            for zh, c in ((0, 1), (0, 0), (1, 0))
        ],
    )
    for step in steps:
        came = [lax.ppermute(held, SEQ, pairs) for pairs in step]
        held = held + ((came[0] + came[1]) + came[2])
    return held


def shards(queries, keys, values, kept_index, kept_count, owner):
    position = lax.axis_index(SEQ)
    zh = lax.axis_index("zh")
    pos = position.reshape(1).astype(jnp.int32)
    base = (zh * HALF).reshape(1).astype(jnp.int32)
    slot_ids = jnp.arange(KEEP, dtype=jnp.int32)[:, None]
    owners = jnp.transpose(owner, (0, 2, 1))[0]
    picks = jnp.transpose(kept_index, (0, 2, 1))[0]
    meta = jnp.concatenate([jnp.where(slot_ids < kept_count, owners, -1), picks], axis=0)

    observers = spread(queries[SHARD - OBS :])

    swap = [(0, 1), (1, 0)]
    other_meta = lax.ppermute(meta, "zh", swap)
    other_keys = lax.ppermute(keys, "zh", swap)
    other_values = lax.ppermute(values, "zh", swap)

    def exchange(packed):
        return lax.all_to_all(packed, PLANE, split_axis=0, concat_axis=0, tiled=True)

    near = exchange(pack(base, meta, keys, values))

    pairs = [(i, i + 1) for i in range(NSEQ - 1)]
    ks, vs = [keys], [values]
    for _ in range(1, CYCLE):
        ks.append(lax.ppermute(ks[-1], SEQ, pairs))
        vs.append(lax.ppermute(vs[-1], SEQ, pairs))

    msg, frac, level = observe(pos, meta, observers, keys)
    got = lax.all_to_all(msg, SEQ, split_axis=0, concat_axis=0, tiled=True)
    attended = attend(pos, queries, ks, vs)
    recv_scores, scores_here = finish(got, frac, level)

    far = exchange(pack(base, other_meta, other_keys, other_values))
    first = place(zh.reshape(1).astype(jnp.int32), near)
    recv_keys, recv_values = place((1 - zh).reshape(1).astype(jnp.int32), far, first)
    return (
        attended,
        scores_here,
        recv_keys.reshape(1, 1, NSEQ, 1, BLOCK, HD),
        recv_values.reshape(1, 1, NSEQ, 1, BLOCK, HD),
        recv_scores.reshape(1, 1, NSEQ, 1),
    )


def solution(mesh):
    fine = Mesh(mesh.devices.reshape(2, 4, 4, 2, 4), SEQ + ("kv",))
    placed = (
        P(SEQ, "kv"),
        P(SEQ, "kv"),
        P(SEQ, "kv"),
        P(SEQ, "kv", None),
        P(SEQ, "kv"),
        P(SEQ, "kv", None),
    )
    return jax.shard_map(
        shards,
        mesh=fine,
        in_specs=placed,
        out_specs=(
            P(SEQ, "kv"),
            P("kv", SEQ),
            P(SEQ, "kv", None, None, None, None),
            P(SEQ, "kv", None, None, None, None),
            P(SEQ, "kv", None, None),
        ),
        check_vma=False,
    )
```

time: 1160 us -> 312 us (0.27)
  waiting for transfers between devices: 793 us -> 86.6 us
  blocking collectives: 221 us -> 0 us
  Pallas kernels: 0 us -> 158 us
  matrix products: 39.5 us -> 0 us
  local copies, waits for them, and re-layouts: 26.8 us -> 2.51 us
  starting transfers between devices: 39.8 us -> 59.2 us
  other arithmetic: 20.3 us -> 4.7 us
  between operations: 14.6 us -> 0.93 us
    psum x1 -> x0, waiting for transfers between devices: 714 us -> none  [from_root(): return lax.psum(jnp.where(mine, shard, jnp.zeros_like(shard)), axis)]
    all_gather x2 -> x0, blocking collectives: 221 us -> none  [joined(): pieces = jax.tree.map(lambda part: lax.all_gather(part, axis), value)]
    pallas_call x0 -> x7, Pallas kernels: none -> 158 us  [the longest x2 129 us: place(): pl.pallas_call(place_kernel, out_shape=(shape, shape), in_specs=[pl.Block...]
    dot_general x14 -> x0, matrix products: 39.5 us -> none  [the longest x4 22.7 us: attend_block(): jnp.einsum('tkgd,jkd->kgtj', query_rows, key_rows, preferred_element_type...]
    ppermute x6 -> x18, waiting for transfers between devices: 54.5 us -> 80.1 us  [the longest x3 45.5 us: shards(): ks.append(lax.ppermute(ks[-1], SEQ, pairs))]
    ppermute x6 -> x18, starting transfers between devices: 13.2 us -> 31.5 us  [the longest x3 7.46 us: shards(): vs.append(lax.ppermute(vs[-1], SEQ, pairs))]
    all_to_all x3, waiting for transfers between devices: 24.2 us -> 6.53 us  [the longest x1 6.52 us: shards(): got = lax.all_to_all(msg, SEQ, split_axis=0, concat_axis=0, tiled=True)]
    reduce_sum x6 -> x0, other arithmetic: 16.2 us -> none  [the longest x2 15.3 us: attend_block(): mass = mass * fading + jnp.sum(weights, axis=-1)]
  transfers between devices with their start and end apart: 10 -> 21, of which waited for: 7 -> 9; matrix products, arithmetic and copies ran while one was open for 7% -> 1% of each run, Pallas kernels for 0% -> 29%
where the time goes in v1:
time: 312 us
  Pallas kernels  158 us (51%)
  waiting for transfers between devices  86.6 us (28%)
  starting transfers between devices  59.2 us (19%)
  other arithmetic  4.7 us (2%)
    pallas_call x2, Pallas kernels, place(): pl.pallas_call(place_kernel, out_shape=(shape, shape), in_specs=[pl.Block...  129 us
    ppermute x3, waiting for transfers between devices, shards(): ks.append(lax.ppermute(ks[-1], SEQ, pairs))  45.5 us
    pallas_call x1, Pallas kernels, attend(): pl.pallas_call(attend_kernel, grid=(HEADS,), out_shape=jax.ShapeDtypeStru...  19.1 us
    ppermute x1, waiting for transfers between devices, shards(): other_meta = lax.ppermute(meta, 'zh', swap)  16.8 us
    all_to_all x1, starting transfers between devices, shards(): got = lax.all_to_all(msg, SEQ, split_axis=0, concat_axis=0, tiled=True)  15.4 us
    all_to_all x2, starting transfers between devices, exchange(): lax.all_to_all(packed, PLANE, split_axis=0, concat_axis=0, tiled=True)  12.3 us
    ppermute x9, waiting for transfers between devices, spread(): came = [lax.ppermute(held, SEQ, pairs) for pairs in step]  12.1 us
    ppermute x3, starting transfers between devices, shards(): vs.append(lax.ppermute(vs[-1], SEQ, pairs))  7.46 us
  transfers between devices with their start and end apart: 21, of which 9 were waited for; matrix products, arithmetic and copies ran while one was open for 1% of the time, Pallas kernels for 29%

profile of v1, /device:TPU:192, one launch (start us, length us, event | category | flops | bytes accessed | tf_op | source)
XLA Modules:
  0.0 311.6 jit_solution(3593447979313262158)
XLA Ops:
  0.7 1.0 slice_select_fusion
  1.6 0.7 collective-permute-start.6
  2.3 0.7 collective-permute-start.7
  3.0 0.7 collective-permute-start.8
  3.7 0.0 collective-permute-done.6
  3.7 0.9 add_add_fusion.2
  4.7 0.7 collective-permute-start.10
  5.3 0.7 collective-permute-start.11
  6.0 0.7 collective-permute-start.9
  6.7 0.0 collective-permute-done.11
  6.7 0.0 collective-permute-done.9
  6.8 0.7 collective-permute-start.12
  7.4 0.7 collective-permute-start.13
  8.1 1.3 collective-permute-start.14
  9.4 0.7 bitcast_select_fusion
  10.1 0.7 pad_add_fusion.meta_ref
  10.8 12.0 %collective-permute-done.14 = bf16[64,1024]{1,0:T(8,128)(2,1)S(1)} collective-permute-done((bf16[64,1024]{1,0:T(8,128)(2,1)S(1)}, bf16[64,1024]{1,0:T(8,128)(2,1)S(1)}, u32[]{:S(2)}, u32[]{:S(2)}) %collective-permute-start.14) | collective-permute-done | bytes 131104 | tf_op jit(solution)/shard_map/ppermute | solution.py:266
  22.9 2.0 observe.1
  24.9 0.6 copy-done.3
  25.5 0.6 copy-done.4
  26.1 15.4 %all-to-all-start = ((f32[64,8,128]{2,1,0:T(8,128)}), f32[64,8,128]{2,1,0:T(8,128)S(1)}, u32[]{:S(2)}, u32[]{:S(2)}) async-start(f32[64,8,128]{2,1,0:T(8,128)} %get-tuple-element.14), calls=%async_computation | async-start | bytes 524288 | tf_op jit(solution)/shard_map/all_to_all | solution.py:300
  41.5 2.6 pack.3
  44.1 6.5 %all-to-all-done.got_ref = f32[64,8,128]{2,1,0:T(8,128)S(1)} async-done(((f32[64,8,128]{2,1,0:T(8,128)}), f32[64,8,128]{2,1,0:T(8,128)S(1)}, u32[]{:S(2)}, u32[]{:S(2)}) %all-to-all-start) | async-done | bytes 262176 | tf_op jit(solution)/shard_map/all_to_all | solution.py:300
  50.7 4.8 %all-to-all-start.2 = ((bf16[32,2,128,128]{3,2,1,0:T(8,128)(2,1)}), bf16[32,2,128,128]{3,2,1,0:T(8,128)(2,1)}, u32[]{:S(2)}, u32[]{:S(2)}) async-start(bf16[32,2,128,128]{3,2,1,0:T(8,128)(2,1)} %pack.3), calls=%async_computation.2 | async-start | bytes 4194304 | tf_op jit(solution)/shard_map/all_to_all | solution.py:289
  55.4 5.5 %collective-permute-start.16 = (bf16[512,256]{1,0:T(8,128)(2,1)S(1)}, bf16[512,256]{1,0:T(8,128)(2,1)S(1)}, u32[]{:S(2)}, u32[]{:S(2)}) collective-permute-start(bf16[512,256]{1,0:T(8,128)(2,1)S(1)} %copy-done), channel_id=1, source_target_pairs={{0,128},{128,0},{1,129},{129,1},{2,130},{130,2},{3,131},{131,3},{4... | collective-permute-start | bytes 786440 | tf_op jit(solution)/shard_map/ppermute | solution.py:285
  61.0 0.5 collective-permute-start.17
  61.5 5.4 %collective-permute-start.15 = (s32[8,8]{1,0:T(8,128)S(1)}, s32[8,8]{1,0:T(8,128)S(1)}, u32[]{:S(2)}, u32[]{:S(2)}) collective-permute-start(s32[8,8]{1,0:T(8,128)S(1)} %pad_add_fusion.meta_ref), channel_id=1, source_target_pairs={{0,128},{128,0},{1,129},{129,1},{2,130},{130,2},{3,131},{131,3},{4... | collective-permute-start | bytes 776 | tf_op jit(solution)/shard_map/ppermute | solution.py:284
  66.9 16.8 %collective-permute-done.15.meta_ref = s32[8,8]{1,0:T(8,128)S(1)} collective-permute-done((s32[8,8]{1,0:T(8,128)S(1)}, s32[8,8]{1,0:T(8,128)S(1)}, u32[]{:S(2)}, u32[]{:S(2)}) %collective-permute-start.15) | collective-permute-done | bytes 288 | tf_op jit(solution)/shard_map/ppermute | solution.py:284
  83.7 2.7 pack.2
  86.4 7.6 %all-to-all-start.1 = ((bf16[32,2,128,128]{3,2,1,0:T(8,128)(2,1)}), bf16[32,2,128,128]{3,2,1,0:T(8,128)(2,1)}, u32[]{:S(2)}, u32[]{:S(2)}) async-start(bf16[32,2,128,128]{3,2,1,0:T(8,128)(2,1)} %pack.2), calls=%async_computation.1 | async-start | bytes 4194304 | tf_op jit(solution)/shard_map/all_to_all | solution.py:289
  94.0 2.1 collective-permute-start
  96.1 3.5 %collective-permute-start.3 = (bf16[512,256]{1,0:T(8,128)(2,1)S(1)}, bf16[512,256]{1,0:T(8,128)(2,1)S(1)}, u32[]{:S(2)}, u32[]{:S(2)}) collective-permute-start(bf16[512,256]{1,0:T(8,128)(2,1)S(1)} %copy-done.1), channel_id=1, source_target_pairs={{0,4},{4,8},{8,12},{12,16},{16,20},{20,24},{24,28},{28,32},{32,36}... | collective-permute-start | bytes 786440 | tf_op jit(solution)/shard_map/ppermute | solution.py:297
  99.7 20.8 %collective-permute-done.k1 = bf16[512,256]{1,0:T(8,128)(2,1)S(1)} collective-permute-done((bf16[512,256]{1,0:T(8,128)(2,1)S(1)}, bf16[512,256]{1,0:T(8,128)(2,1)S(1)}, u32[]{:S(2)}, u32[]{:S(2)}) %collective-permute-start) | collective-permute-done | bytes 262176 | tf_op jit(solution)/shard_map/ppermute | solution.py:296
  120.5 1.9 collective-permute-start.1
  122.4 1.9 collective-permute-done.3.v1
  124.4 2.0 collective-permute-start.4
  126.4 12.7 %collective-permute-done.1.k2 = bf16[512,256]{1,0:T(8,128)(2,1)S(1)} collective-permute-done((bf16[512,256]{1,0:T(8,128)(2,1)S(1)}, bf16[512,256]{1,0:T(8,128)(2,1)S(1)}, u32[]{:S(2)}, u32[]{:S(2)}) %collective-permute-start.1) | collective-permute-done | bytes 262176 | tf_op jit(solution)/shard_map/ppermute | solution.py:296
  139.1 1.9 collective-permute-start.2
  141.0 0.9 collective-permute-done.4.v2
  141.9 1.9 collective-permute-start.5
  143.8 12.0 %collective-permute-done.2.k3 = bf16[512,256]{1,0:T(8,128)(2,1)S(1)} collective-permute-done((bf16[512,256]{1,0:T(8,128)(2,1)S(1)}, bf16[512,256]{1,0:T(8,128)(2,1)S(1)}, u32[]{:S(2)}, u32[]{:S(2)}) %collective-permute-start.2) | collective-permute-done | bytes 262176 | tf_op jit(solution)/shard_map/ppermute | solution.py:296
  155.8 2.8 collective-permute-done.5.v3
  158.6 19.1 %attend.1 = bf16[512,1024]{1,0:T(8,128)(2,1)} custom-call(s32[1]{0:T(128)} %bitcast.pos_ref, bf16[512,1024]{1,0:T(8,128)(2,1)S(1)} %copy-done.2, bf16[512,256]{1,0:T(8,128)(2,1)S(1)} %copy-done, bf16[512,256]{1,0:T(8,128)(2,1)S(1)} %collective-permute-done.k1, bf16[512,256]{1,0:T(8,128)(2,1)S(1)} %collective-permute-done.1.k2, ...), custom_call_target="tpu_custom_call" | custom-call | flops 4294967296 | bytes 4194304 | tf_op jit(solution)/shard_map/attend/pallas_call | solution.py:73
  177.8 1.9 finish.1
  179.6 1.3 copy.16
  181.0 1.3 reduce
  182.3 64.6 %place.2 = (bf16[64,128,128]{2,1,0:T(8,128)(2,1)}, bf16[64,128,128]{2,1,0:T(8,128)(2,1)}) custom-call(s32[1]{0:T(128)} %bitcast.8.half_ref, bf16[32,2,128,128]{3,2,1,0:T(8,128)(2,1)} %all-to-all-done.2.got_ref), custom_call_target="tpu_custom_call" | custom-call | bytes 4194304 | tf_op jit(solution)/shard_map/place/pallas_call | solution.py:238
  247.0 64.7 %place.3 = (bf16[64,128,128]{2,1,0:T(8,128)(2,1)}, bf16[64,128,128]{2,1,0:T(8,128)(2,1)}) custom-call(s32[1]{0:T(128)} %bitcast.6.half_ref, bf16[32,2,128,128]{3,2,1,0:T(8,128)(2,1)} %all-to-all-done.1.got_ref, bf16[64,128,128]{2,1,0:T(8,128)(2,1)} %get-tuple-element.18.refs_0_, ...), custom_call_target="tpu_custom_call", output_to_operand_aliasing={{0}: (2, {}), {1}: (3, {})} | custom-call | bytes 4194304 | tf_op jit(solution)/shard_map/place/pallas_call | solution.py:238
  (21 shorter events, 0.1 us)
Async XLA Ops:
  0.6 22.2 %copy-start = (bf16[512,256]{1,0:T(8,128)(2,1)S(1)}, bf16[512,256]{1,0:T(8,128)(2,1)}, u32[]{:S(2)}) copy-start(bf16[512,256]{1,0:T(8,128)(2,1)} %k_ref.3) | copy-start | bytes 786436
  0.6 40.9 %copy-start.1 = (bf16[512,256]{1,0:T(8,128)(2,1)S(1)}, bf16[512,256]{1,0:T(8,128)(2,1)}, u32[]{:S(2)}) copy-start(bf16[512,256]{1,0:T(8,128)(2,1)} %v_ref.1) | copy-start | bytes 786436
  1.6 2.0 collective-permute-start.6
  2.3 1.4 collective-permute-start.7
  3.0 0.7 collective-permute-start.8
  4.7 2.0 collective-permute-start.10
  5.3 1.4 collective-permute-start.11
  6.0 0.7 collective-permute-start.9
  6.8 4.0 %collective-permute-start.12 = (bf16[64,1024]{1,0:T(8,128)(2,1)S(1)}, bf16[64,1024]{1,0:T(8,128)(2,1)S(1)}, u32[]{:S(2)}, u32[]{:S(2)}) collective-permute-start(bf16[64,1024]{1,0:T(8,128)(2,1)S(1)} %add_add_fusion.1), channel_id=1, source_target_pairs={{132,4},{140,12},{148,20},{156,28},{164,36},{172,44},{180,52},{188... | collective-permute-start | bytes 393224 | tf_op jit(solution)/shard_map/ppermute | solution.py:266
  7.4 3.4 %collective-permute-start.13 = (bf16[64,1024]{1,0:T(8,128)(2,1)S(1)}, bf16[64,1024]{1,0:T(8,128)(2,1)S(1)}, u32[]{:S(2)}, u32[]{:S(2)}) collective-permute-start(bf16[64,1024]{1,0:T(8,128)(2,1)S(1)} %add_add_fusion.1), channel_id=1, source_target_pairs={{132,0},{140,8},{148,16},{156,24},{164,32},{172,40},{180,48},{188,... | collective-permute-start | bytes 393224 | tf_op jit(solution)/shard_map/ppermute | solution.py:266
  8.1 14.7 %collective-permute-start.14 = (bf16[64,1024]{1,0:T(8,128)(2,1)S(1)}, bf16[64,1024]{1,0:T(8,128)(2,1)S(1)}, u32[]{:S(2)}, u32[]{:S(2)}) collective-permute-start(bf16[64,1024]{1,0:T(8,128)(2,1)S(1)} %add_add_fusion.1), channel_id=1, source_target_pairs={{132,128},{140,136},{148,144},{156,152},{164,160},{172,168},{180,1... | collective-permute-start | bytes 393224 | tf_op jit(solution)/shard_map/ppermute | solution.py:266
  24.9 0.6 copy-start.3
  25.5 0.6 copy-start.4
  26.1 24.6 %all-to-all-start = ((f32[64,8,128]{2,1,0:T(8,128)}), f32[64,8,128]{2,1,0:T(8,128)S(1)}, u32[]{:S(2)}, u32[]{:S(2)}) async-start(f32[64,8,128]{2,1,0:T(8,128)} %get-tuple-element.14), calls=%async_computation | async-start | bytes 524288 | tf_op jit(solution)/shard_map/all_to_all | solution.py:300
  50.7 35.8 %copy-start.5 = (f32[64,8,128]{2,1,0:T(8,128)}, f32[64,8,128]{2,1,0:T(8,128)S(1)}, u32[]{:S(2)}) copy-start(f32[64,8,128]{2,1,0:T(8,128)S(1)} %all-to-all-done.got_ref) | copy-start | bytes 786436
  50.7 35.8 %all-to-all-start.2 = ((bf16[32,2,128,128]{3,2,1,0:T(8,128)(2,1)}), bf16[32,2,128,128]{3,2,1,0:T(8,128)(2,1)}, u32[]{:S(2)}, u32[]{:S(2)}) async-start(bf16[32,2,128,128]{3,2,1,0:T(8,128)(2,1)} %pack.3), calls=%async_computation.2 | async-start | bytes 4194304 | tf_op jit(solution)/shard_map/all_to_all | solution.py:289
  55.4 28.3 %collective-permute-start.16 = (bf16[512,256]{1,0:T(8,128)(2,1)S(1)}, bf16[512,256]{1,0:T(8,128)(2,1)S(1)}, u32[]{:S(2)}, u32[]{:S(2)}) collective-permute-start(bf16[512,256]{1,0:T(8,128)(2,1)S(1)} %copy-done), channel_id=1, source_target_pairs={{0,128},{128,0},{1,129},{129,1},{2,130},{130,2},{3,131},{131,3},{4... | collective-permute-start | bytes 786440 | tf_op jit(solution)/shard_map/ppermute | solution.py:285
  61.0 22.8 %collective-permute-start.17 = (bf16[512,256]{1,0:T(8,128)(2,1)S(1)}, bf16[512,256]{1,0:T(8,128)(2,1)S(1)}, u32[]{:S(2)}, u32[]{:S(2)}) collective-permute-start(bf16[512,256]{1,0:T(8,128)(2,1)S(1)} %copy-done.1), channel_id=1, source_target_pairs={{0,128},{128,0},{1,129},{129,1},{2,130},{130,2},{3,131},{131,3},{4... | collective-permute-start | bytes 786440 | tf_op jit(solution)/shard_map/ppermute | solution.py:286
  61.5 22.3 %collective-permute-start.15 = (s32[8,8]{1,0:T(8,128)S(1)}, s32[8,8]{1,0:T(8,128)S(1)}, u32[]{:S(2)}, u32[]{:S(2)}) collective-permute-start(s32[8,8]{1,0:T(8,128)S(1)} %pad_add_fusion.meta_ref), channel_id=1, source_target_pairs={{0,128},{128,0},{1,129},{129,1},{2,130},{130,2},{3,131},{131,3},{4... | collective-permute-start | bytes 776 | tf_op jit(solution)/shard_map/ppermute | solution.py:284
  86.4 72.2 %copy-start.2 = (bf16[512,1024]{1,0:T(8,128)(2,1)S(1)}, bf16[512,1024]{1,0:T(8,128)(2,1)}, u32[]{:S(2)}) copy-start(bf16[512,1024]{1,0:T(8,128)(2,1)} %q_ref.1) | copy-start | bytes 3145732
  86.4 160.5 %all-to-all-start.1 = ((bf16[32,2,128,128]{3,2,1,0:T(8,128)(2,1)}), bf16[32,2,128,128]{3,2,1,0:T(8,128)(2,1)}, u32[]{:S(2)}, u32[]{:S(2)}) async-start(bf16[32,2,128,128]{3,2,1,0:T(8,128)(2,1)} %pack.2), calls=%async_computation.1 | async-start | bytes 4194304 | tf_op jit(solution)/shard_map/all_to_all | solution.py:289
  94.0 26.5 %collective-permute-start = (bf16[512,256]{1,0:T(8,128)(2,1)S(1)}, bf16[512,256]{1,0:T(8,128)(2,1)S(1)}, u32[]{:S(2)}, u32[]{:S(2)}) collective-permute-start(bf16[512,256]{1,0:T(8,128)(2,1)S(1)} %copy-done), channel_id=1, source_target_pairs={{0,4},{4,8},{8,12},{12,16},{16,20},{20,24},{24,28},{28,32},{32,36}... | collective-permute-start | bytes 786440 | tf_op jit(solution)/shard_map/ppermute | solution.py:296
  96.1 28.3 %collective-permute-start.3 = (bf16[512,256]{1,0:T(8,128)(2,1)S(1)}, bf16[512,256]{1,0:T(8,128)(2,1)S(1)}, u32[]{:S(2)}, u32[]{:S(2)}) collective-permute-start(bf16[512,256]{1,0:T(8,128)(2,1)S(1)} %copy-done.1), channel_id=1, source_target_pairs={{0,4},{4,8},{8,12},{12,16},{16,20},{20,24},{24,28},{28,32},{32,36}... | collective-permute-start | bytes 786440 | tf_op jit(solution)/shard_map/ppermute | solution.py:297
  120.5 18.6 %collective-permute-start.1 = (bf16[512,256]{1,0:T(8,128)(2,1)S(1)}, bf16[512,256]{1,0:T(8,128)(2,1)S(1)}, u32[]{:S(2)}, u32[]{:S(2)}) collective-permute-start(bf16[512,256]{1,0:T(8,128)(2,1)S(1)} %collective-permute-done.k1), channel_id=1, source_target_pairs={{0,4},{4,8},{8,12},{12,16},{16,20},{20,24},{24,28},{28,32},{32,36}... | collective-permute-start | bytes 786440 | tf_op jit(solution)/shard_map/ppermute | solution.py:296
  124.4 17.6 %collective-permute-start.4 = (bf16[512,256]{1,0:T(8,128)(2,1)S(1)}, bf16[512,256]{1,0:T(8,128)(2,1)S(1)}, u32[]{:S(2)}, u32[]{:S(2)}) collective-permute-start(bf16[512,256]{1,0:T(8,128)(2,1)S(1)} %collective-permute-done.3.v1), channel_id=1, source_target_pairs={{0,4},{4,8},{8,12},{12,16},{16,20},{20,24},{24,28},{28,32},{32,36}... | collective-permute-start | bytes 786440 | tf_op jit(solution)/shard_map/ppermute | solution.py:297
  139.1 16.7 %collective-permute-start.2 = (bf16[512,256]{1,0:T(8,128)(2,1)S(1)}, bf16[512,256]{1,0:T(8,128)(2,1)S(1)}, u32[]{:S(2)}, u32[]{:S(2)}) collective-permute-start(bf16[512,256]{1,0:T(8,128)(2,1)S(1)} %collective-permute-done.1.k2), channel_id=1, source_target_pairs={{0,4},{4,8},{8,12},{12,16},{16,20},{20,24},{24,28},{28,32},{32,36}... | collective-permute-start | bytes 786440 | tf_op jit(solution)/shard_map/ppermute | solution.py:296
  141.9 16.7 %collective-permute-start.5 = (bf16[512,256]{1,0:T(8,128)(2,1)S(1)}, bf16[512,256]{1,0:T(8,128)(2,1)S(1)}, u32[]{:S(2)}, u32[]{:S(2)}) collective-permute-start(bf16[512,256]{1,0:T(8,128)(2,1)S(1)} %collective-permute-done.4.v2), channel_id=1, source_target_pairs={{0,4},{4,8},{8,12},{12,16},{16,20},{20,24},{24,28},{28,32},{32,36}... | collective-permute-start | bytes 786440 | tf_op jit(solution)/shard_map/ppermute | solution.py:297

commit v2 on v1

v2 whole, which is shorter than its diff:
```python
import functools
import math

import jax
import jax.numpy as jnp
from jax import lax
from jax.experimental import pallas as pl
from jax.experimental.pallas import tpu as pltpu
from jax.sharding import Mesh, PartitionSpec as P

HD = 128
CYCLE = 4
OBS = 64
BLOCK = 128
SHARD = 512
HEADS = 8
KVS = 2
GROUP = 4
KEEP = 4
BLKS = 4
NSEQ = 64
HALF = 32
SEQ = ("zh", "y", "x", "c")
PLANE = ("y", "x", "c")
LOG2E = 1.4426950408889634
COEF = LOG2E / math.sqrt(HD)
SCALE = 1.0 / math.sqrt(HD)
BIG = 1e30
NT = (((1,), (1,)), ((), ()))


def f32dot(a, b, dims):
    return lax.dot_general(a, b, dims, preferred_element_type=jnp.float32)


def attend_kernel(pos_ref, q_ref, k0, v0, k1, v1, k2, v2, k3, v3, o_ref):
    pos = pos_ref[0]
    half = SHARD // 2
    ones = jnp.ones((SHARD, HD), jnp.bfloat16)
    vext = [jnp.concatenate([v[...], ones], axis=1) for v in (v0, v1, v2, v3)]
    row = lax.broadcasted_iota(jnp.int32, (half, half), 0)
    col = lax.broadcasted_iota(jnp.int32, (half, half), 1)
    causal = col <= row
    for tile in range(2):
        q = q_ref[tile * half : (tile + 1) * half, :]
        diag = f32dot(q, k0[tile * half : (tile + 1) * half, :], NT)
        diag = jnp.where(causal, diag, -BIG)
        peak = jnp.max(diag, axis=1, keepdims=True)
        full = []
        if tile == 1:
            own = f32dot(q, k0[:half, :], NT)
            peak = jnp.maximum(peak, jnp.max(own, axis=1, keepdims=True))
            full.append(own)
        past = [f32dot(q, k[...], NT) for k in (k1, k2, k3)]
        for distance, score in enumerate(past, 1):
            here = jnp.max(score, axis=1, keepdims=True)
            peak = jnp.where(pos >= distance, jnp.maximum(peak, here), peak)
        shift = peak * COEF
        weight = jnp.exp2(diag * COEF - shift).astype(jnp.bfloat16)
        acc = f32dot(weight, vext[0][tile * half : (tile + 1) * half], (((1,), (0,)), ((), ())))
        if tile == 1:
            weight = jnp.exp2(full[0] * COEF - shift).astype(jnp.bfloat16)
            acc += f32dot(weight, vext[0][:half], (((1,), (0,)), ((), ())))
        for distance, score in enumerate(past, 1):
            lift = jnp.where(pos >= distance, shift, BIG)
            weight = jnp.exp2(score * COEF - lift).astype(jnp.bfloat16)
            acc += f32dot(weight, vext[distance], (((1,), (0,)), ((), ())))
        mixed = acc[:, :HD] / acc[:, HD:]
        o_ref[tile * half : (tile + 1) * half, :] = mixed.astype(jnp.bfloat16)


def attend(position, queries, pairs):
    key_spec = pl.BlockSpec((SHARD, HD), lambda h: (0, h // GROUP))
    value_spec = pl.BlockSpec((SHARD, HD), lambda h: (1, h // GROUP))
    return pl.pallas_call(
        attend_kernel,
        grid=(HEADS,),
        out_shape=jax.ShapeDtypeStruct((SHARD, HEADS * HD), jnp.bfloat16),
        in_specs=[
            pl.BlockSpec(memory_space=pltpu.SMEM),
            pl.BlockSpec((SHARD, HD), lambda h: (0, h)),
        ]
        + [key_spec, value_spec] * CYCLE,
        out_specs=pl.BlockSpec((SHARD, HD), lambda h: (0, h)),
        compiler_params=pltpu.CompilerParams(vmem_limit_bytes=32 * 1024 * 1024),
        cost_estimate=pl.CostEstimate(
            flops=HEADS * SHARD * SHARD * 4 * HD * 4,
            bytes_accessed=4 * 1024 * 1024,
            transcendentals=HEADS * SHARD * SHARD * 4,
        ),
        name="attend",
    )(position, queries, *[pair for pair in pairs for _ in range(2)])


SMEM = pl.BlockSpec(memory_space=pltpu.SMEM)
VMEM = pl.BlockSpec(memory_space=pltpu.VMEM)
ANY = pl.BlockSpec(memory_space=pl.ANY)


def seats(base, meta_ref, put):
    for head in range(HEADS):
        for c in range(KEEP):
            seat = meta_ref[c, head] - base
            unit = meta_ref[KEEP + c, head]
            pl.when((seat >= 0) & (seat < HALF))(functools.partial(put, seat, unit, head))


def block_rows(unit, start):
    return pl.ds(pl.multiple_of(unit * BLOCK + start, BLOCK), BLOCK)


def near_kernel(base_ref, meta_ref, k_ref, v_ref, out_ref, pair_ref):
    pair_ref[:SHARD] = k_ref[...]
    pair_ref[SHARD:] = v_ref[...]
    out_ref[...] = jnp.zeros_like(out_ref)

    def put(seat, unit, head):
        cols = slice((head // GROUP) * HD, (head // GROUP + 1) * HD)
        out_ref[seat, :BLOCK] = k_ref[block_rows(unit, 0), cols]
        out_ref[seat, BLOCK:] = v_ref[block_rows(unit, 0), cols]

    seats(base_ref[0], meta_ref, put)


def pack_near(base, meta, keys, values):
    return pl.pallas_call(
        near_kernel,
        out_shape=(
            jax.ShapeDtypeStruct((HALF, 2 * BLOCK, HD), jnp.bfloat16),
            jax.ShapeDtypeStruct((2 * SHARD, KVS * HD), jnp.bfloat16),
        ),
        in_specs=[SMEM, SMEM, VMEM, VMEM],
        out_specs=(VMEM, VMEM),
        compiler_params=pltpu.CompilerParams(vmem_limit_bytes=16 * 1024 * 1024),
        cost_estimate=pl.CostEstimate(flops=0, bytes_accessed=3 * 1024 * 1024, transcendentals=0),
        name="pack_near",
    )(base, meta, keys, values)


def terms(value, count):
    parts = []
    for _ in range(count):
        part = value.astype(jnp.bfloat16)
        parts.append(part)
        value = value - part.astype(jnp.float32)
    return parts


def far_kernel(
    base_ref, meta_ref, other_meta_ref, pair_ref, stats_ref, other_ref, out_ref, tile_ref
):
    level, other_level = stats_ref[0:4], other_ref[0:4]
    top = jnp.maximum(level, other_level)
    both = top + jnp.log(jnp.exp(level - top) + jnp.exp(other_level - top))
    part, other_part = jnp.exp(level - both), jnp.exp(other_level - both)
    blank = jnp.zeros((4, 128), jnp.float32)
    as_rows = lambda pieces: jnp.concatenate([p.astype(jnp.float32) for p in pieces], axis=0)
    for b in range(BLKS):
        rows = slice(4 + 4 * b, 8 + 4 * b)
        tile_ref[0, b] = as_rows(terms(stats_ref[rows] * part, 2) + [blank, blank])
        tile_ref[1, b] = as_rows([blank, blank] + terms(other_ref[rows] * other_part, 2))
    out_ref[:, : 2 * BLOCK, :] = jnp.zeros((HALF, 2 * BLOCK, HD), jnp.bfloat16)
    lead = as_rows(terms(both, 3) + [blank]).astype(jnp.bfloat16)
    out_ref[:, 2 * BLOCK : 2 * BLOCK + 16, :] = jnp.broadcast_to(lead[None], (HALF, 16, HD))
    out_ref[:, 2 * BLOCK + 16 :, :] = jnp.zeros((HALF, 16, HD), jnp.bfloat16)
    row = lax.broadcasted_iota(jnp.int32, (16, 128), 0)
    lane = lax.broadcasted_iota(jnp.int32, (16, 128), 1)
    which = lax.rem(row, 4) * 2 + lane // OBS
    tail = slice(2 * BLOCK + 16, 2 * BLOCK + 32)

    def add_score(source, seat, unit, head):
        picked = jnp.where(which == head, tile_ref[source, unit], 0.0).astype(jnp.bfloat16)
        out_ref[seat, tail] = out_ref[seat, tail] + picked

    def put(seat, unit, head):
        cols = slice((head // GROUP) * HD, (head // GROUP + 1) * HD)
        out_ref[seat, :BLOCK] = pair_ref[block_rows(unit, 0), cols]
        out_ref[seat, BLOCK : 2 * BLOCK] = pair_ref[block_rows(unit, SHARD), cols]
        add_score(1, seat, unit, head)

    seats(base_ref[0], meta_ref, functools.partial(add_score, 0))
    seats(base_ref[0], other_meta_ref, put)


def pack_far(base, meta, other_meta, other_pair, stats, other_stats):
    return pl.pallas_call(
        far_kernel,
        out_shape=jax.ShapeDtypeStruct((HALF, 2 * BLOCK + 32, HD), jnp.bfloat16),
        in_specs=[SMEM, SMEM, SMEM, VMEM, VMEM, VMEM],
        out_specs=VMEM,
        scratch_shapes=[pltpu.VMEM((2, BLKS, 16, 128), jnp.float32)],
        compiler_params=pltpu.CompilerParams(vmem_limit_bytes=16 * 1024 * 1024),
        cost_estimate=pl.CostEstimate(flops=0, bytes_accessed=3 * 1024 * 1024, transcendentals=0),
        name="pack_far",
    )(base, meta, other_meta, other_pair, stats, other_stats)


def observe_kernel(pos_ref, q_ref, k_ref, stats_ref):
    pos = pos_ref[0]
    rows = [[] for _ in range(1 + BLKS)]
    for kv in range(KVS):
        heads = [
            q_ref[:, (kv * GROUP + g) * HD : (kv * GROUP + g + 1) * HD] for g in range(GROUP)
        ]
        stacked = jnp.concatenate(heads, axis=0)
        score = f32dot(k_ref[:, kv * HD : (kv + 1) * HD], stacked, NT) * SCALE
        key = lax.broadcasted_iota(jnp.int32, score.shape, 0)
        lane = lax.broadcasted_iota(jnp.int32, score.shape, 1)
        limit = (NSEQ - pos) * SHARD - OBS + lax.rem(lane, OBS)
        score = jnp.where(key <= limit, score, -jnp.inf)
        peak = jnp.max(score, axis=0, keepdims=True)
        expo = jnp.exp(score - peak)
        sums = [
            jnp.sum(expo[b * BLOCK : (b + 1) * BLOCK], axis=0, keepdims=True) for b in range(BLKS)
        ]
        mass = (sums[0] + sums[1]) + (sums[2] + sums[3])
        level = peak + jnp.log(mass)
        for side in range(2):
            cut = slice(side * 128, (side + 1) * 128)
            rows[0].append(level[:, cut])
            for b in range(BLKS):
                rows[1 + b].append((sums[b] / mass)[:, cut])
    for place_, pieces in enumerate(rows):
        stats_ref[4 * place_ : 4 * place_ + 4] = jnp.concatenate(pieces, axis=0)
    stats_ref[20:24] = jnp.zeros((4, 128), jnp.float32)


def observe(position, observers, keys):
    return pl.pallas_call(
        observe_kernel,
        out_shape=jax.ShapeDtypeStruct((24, 128), jnp.float32),
        in_specs=[SMEM, VMEM, VMEM],
        out_specs=VMEM,
        compiler_params=pltpu.CompilerParams(vmem_limit_bytes=16 * 1024 * 1024),
        name="observe",
    )(position, observers, keys)


CHUNK = 4


def place_kernel(half_ref, got_ref, key_ref, value_ref):
    key_ref[...] = got_ref[:, :BLOCK]
    value_ref[...] = got_ref[:, BLOCK : 2 * BLOCK]


def place_near(half, got):
    shape = jax.ShapeDtypeStruct((NSEQ, BLOCK, HD), jnp.bfloat16)
    out_spec = pl.BlockSpec((CHUNK, BLOCK, HD), lambda i, half: (half[0] * (HALF // CHUNK) + i, 0, 0))
    return pl.pallas_call(
        place_kernel,
        out_shape=(shape, shape),
        grid_spec=pltpu.PrefetchScalarGridSpec(
            num_scalar_prefetch=1,
            grid=(HALF // CHUNK,),
            in_specs=[pl.BlockSpec((CHUNK, 2 * BLOCK, HD), lambda i, half: (i, 0, 0))],
            out_specs=(out_spec, out_spec),
        ),
        cost_estimate=pl.CostEstimate(flops=0, bytes_accessed=4 * 1024 * 1024, transcendentals=0),
        name="place_near",
    )(half, got)


def last_kernel(
    half_ref, got_ref, mail_ref, stats_ref, _k, _v, key_ref, value_ref, recv_ref, block_ref
):
    key_ref[...] = got_ref[:, :BLOCK]
    value_ref[...] = got_ref[:, BLOCK : 2 * BLOCK]

    @pl.when(pl.program_id(0) == 0)
    def _():
        factor = BLKS * NSEQ / OBS
        lead = mail_ref[:, :16].astype(jnp.float32)
        level = (lead[:, 8:12] + lead[:, 4:8]) + lead[:, 0:4]
        top = jnp.max(level, axis=0)
        total = top + jnp.log(jnp.sum(jnp.exp(level - top[None]), axis=0))
        share = jnp.exp(level - total[None])
        tail = mail_ref[:, 16:].astype(jnp.float32)
        own = jnp.sum((tail[:, 4:8] + tail[:, 0:4]) * share, axis=1)
        other = jnp.sum((tail[:, 12:16] + tail[:, 8:12]) * share, axis=1)
        far = half_ref[0] == 0
        rows = jnp.concatenate(
            [jnp.where(far, other, own), jnp.where(far, own, other)], axis=0
        )
        lined = lax.dot_general(
            jnp.ones((8, 128), jnp.float32),
            rows,
            NT,
            precision=lax.Precision.HIGHEST,
            preferred_element_type=jnp.float32,
        )
        recv_ref[...] = (lined[0:1] * factor).astype(jnp.bfloat16)
        mine = jnp.exp(stats_ref[0:4] - total)
        row = lax.broadcasted_iota(jnp.int32, (HEADS, 4 * 128), 0)
        lane = lax.broadcasted_iota(jnp.int32, (HEADS, 4 * 128), 1)
        chosen = (lane // OBS == row).astype(jnp.float32)
        parts = []
        for b in range(BLKS):
            part = stats_ref[4 + 4 * b : 8 + 4 * b] * mine
            parts.append(jnp.concatenate([part[r : r + 1] for r in range(4)], axis=1))
        table = jnp.concatenate(parts + parts, axis=0)
        scores = lax.dot_general(
            table,
            chosen,
            NT,
            precision=lax.Precision.HIGHEST,
            preferred_element_type=jnp.float32,
        )
        block_ref[...] = scores[:BLKS] * factor


def place_last(half, got, stats, earlier):
    shape = jax.ShapeDtypeStruct((NSEQ, BLOCK, HD), jnp.bfloat16)
    out_spec = pl.BlockSpec((CHUNK, BLOCK, HD), lambda i, half: (half[0] * (HALF // CHUNK) + i, 0, 0))
    return pl.pallas_call(
        last_kernel,
        out_shape=(
            shape,
            shape,
            jax.ShapeDtypeStruct((1, NSEQ), jnp.bfloat16),
            jax.ShapeDtypeStruct((BLKS, HEADS), jnp.float32),
        ),
        grid_spec=pltpu.PrefetchScalarGridSpec(
            num_scalar_prefetch=1,
            grid=(HALF // CHUNK,),
            in_specs=[
                pl.BlockSpec((CHUNK, 2 * BLOCK, HD), lambda i, half: (i, 0, 0)),
                pl.BlockSpec((HALF, 32, HD), lambda i, half: (0, 2 * BLOCK // 32, 0)),
                pl.BlockSpec((24, 128), lambda i, half: (0, 0)),
                ANY,
                ANY,
            ],
            out_specs=(
                out_spec,
                out_spec,
                pl.BlockSpec((1, NSEQ), lambda i, half: (0, 0)),
                pl.BlockSpec((BLKS, HEADS), lambda i, half: (0, 0)),
            ),
        ),
        input_output_aliases={4: 0, 5: 1},
        cost_estimate=pl.CostEstimate(flops=0, bytes_accessed=4 * 1024 * 1024, transcendentals=0),
        name="place_last",
    )(half, got, got, stats, *earlier)


def spread(tail):
    me = lax.axis_index(SEQ)
    held = jnp.where(me == NSEQ - 1, tail, jnp.zeros_like(tail))

    def at(zh, y, x, c):
        return ((zh * 4 + y) * 4 + x) * 2 + c

    four, two = range(4), range(2)
    steps = (
        [[(at(1, 3, 3, 1), at(0, 3, 3, 1))]],
        [[(at(z, 3, 3, 1), at(z, y, 3, 1)) for z in two] for y in range(3)],
        [[(at(z, y, 3, 1), at(z, y, x, 1)) for z in two for y in four] for x in range(3)],
        [[(at(z, y, x, 1), at(z, y, x, 0)) for z in two for y in four for x in four]],
    )
    for step in steps:
        came = [lax.ppermute(held, SEQ, pairs) for pairs in step]
        for part in came:
            held = held + part
    return held


def shards(queries, keys, values, kept_index, kept_count, owner):
    position = lax.axis_index(SEQ)
    zh = lax.axis_index("zh")
    pos = position.reshape(1).astype(jnp.int32)
    near_half = zh.reshape(1).astype(jnp.int32)
    base = near_half * HALF
    slot_ids = jnp.arange(KEEP, dtype=jnp.int32)[:, None]
    owners = jnp.transpose(owner, (0, 2, 1))[0]
    picks = jnp.transpose(kept_index, (0, 2, 1))[0]
    meta = jnp.concatenate([jnp.where(slot_ids < kept_count, owners, -1), picks], axis=0)

    def exchange(packed):
        return lax.all_to_all(packed, PLANE, split_axis=0, concat_axis=0, tiled=True)

    swap = [(0, 1), (1, 0)]
    observers = spread(queries[SHARD - OBS :])
    packed, pair = pack_near(base, meta, keys, values)
    near = exchange(packed)
    other_meta = lax.ppermute(meta, "zh", swap)
    other_pair = lax.ppermute(pair, "zh", swap)

    hops = [(i, i + 1) for i in range(NSEQ - 1)]
    held = [pair]
    for _ in range(1, CYCLE):
        held.append(lax.ppermute(held[-1], SEQ, hops))

    stats = observe(pos, observers, keys)
    other_stats = lax.ppermute(stats, "zh", swap)
    far = exchange(pack_far(base, meta, other_meta, other_pair, stats, other_stats))
    attended = attend(pos, queries, held)
    first = place_near(near_half, near)
    recv_keys, recv_values, recv_scores, scores_here = place_last(1 - near_half, far, stats, first)
    return (
        attended,
        scores_here.T,
        recv_keys.reshape(1, 1, NSEQ, 1, BLOCK, HD),
        recv_values.reshape(1, 1, NSEQ, 1, BLOCK, HD),
        recv_scores.reshape(1, 1, NSEQ, 1),
    )


def solution(mesh):
    fine = Mesh(mesh.devices.reshape(2, 4, 4, 2, 4), SEQ + ("kv",))
    placed = (
        P(SEQ, "kv"),
        P(SEQ, "kv"),
        P(SEQ, "kv"),
        P(SEQ, "kv", None),
        P(SEQ, "kv"),
        P(SEQ, "kv", None),
    )
    return jax.shard_map(
        shards,
        mesh=fine,
        in_specs=placed,
        out_specs=(
            P(SEQ, "kv"),
            P("kv", SEQ),
            P(SEQ, "kv", None, None, None, None),
            P(SEQ, "kv", None, None, None, None),
            P(SEQ, "kv", None, None),
        ),
        check_vma=False,
    )
```

time: 312 us -> 171 us (0.55)
  Pallas kernels: 158 us -> 37.3 us
  starting transfers between devices: 59.2 us -> 31.6 us
  waiting for transfers between devices: 86.6 us -> 96.8 us
  other arithmetic: 4.7 us -> 1.51 us
    pallas_call x6 -> x5, Pallas kernels: 139 us -> 18.1 us  [the longest x1 6.13 us: place_last(): pl.pallas_call(last_kernel, out_shape=(shape, shape, jax.ShapeDtypeStruct...]
    ppermute x9 -> x8, waiting for transfers between devices: 12.1 us -> 32 us  [spread(): came = [lax.ppermute(held, SEQ, pairs) for pairs in step]]
    all_to_all x1 -> x0, starting transfers between devices: 15.4 us -> none  [shards(): got = lax.all_to_all(msg, SEQ, split_axis=0, concat_axis=0, tiled=True)]
    ppermute x1, waiting for transfers between devices: 16.8 us -> 2.47 us  [shards(): other_meta = lax.ppermute(meta, 'zh', swap)]
    ppermute x8 -> x5, starting transfers between devices: 19.4 us -> 8 us  [the longest x3 6.39 us: shards(): held.append(lax.ppermute(held[-1], SEQ, hops))]
    ppermute x8 -> x5, waiting for transfers between devices: 51.2 us -> 62.3 us  [the longest x3 62.3 us: shards(): held.append(lax.ppermute(held[-1], SEQ, hops))]
    all_to_all x1 -> x0, waiting for transfers between devices: 6.52 us -> none  [shards(): got = lax.all_to_all(msg, SEQ, split_axis=0, concat_axis=0, tiled=True)]
    ppermute x9 -> x8, starting transfers between devices: 6.64 us -> 6.11 us  [spread(): came = [lax.ppermute(held, SEQ, pairs) for pairs in step]]
  transfers between devices with their start and end apart: 21 -> 16, of which waited for: 9 -> 5; matrix products, arithmetic and copies ran while one was open for 1% -> 0% of each run, Pallas kernels for 29% -> 17%
where the time goes in v2:
time: 171 us; the launch traced here: 170 us
  waiting for transfers between devices  96.8 us (57%)
  Pallas kernels  37.3 us (22%)
  starting transfers between devices  31.6 us (18%)
  local copies, waits for them, and re-layouts  1.91 us (1%)
    ppermute x3, waiting for transfers between devices, shards(): held.append(lax.ppermute(held[-1], SEQ, hops))  62.3 us
    ppermute x8, waiting for transfers between devices, spread(): came = [lax.ppermute(held, SEQ, pairs) for pairs in step]  32 us
    pallas_call x1, Pallas kernels, attend(): pl.pallas_call(attend_kernel, grid=(HEADS,), out_shape=jax.ShapeDtypeStru...  19.1 us
    all_to_all x2, starting transfers between devices, exchange(): lax.all_to_all(packed, PLANE, split_axis=0, concat_axis=0, tiled=True)  12.4 us
    ppermute x3, starting transfers between devices, shards(): held.append(lax.ppermute(held[-1], SEQ, hops))  6.39 us
    pallas_call x1, Pallas kernels, place_last(): pl.pallas_call(last_kernel, out_shape=(shape, shape, jax.ShapeDtypeStruct...  6.13 us
    ppermute x8, starting transfers between devices, spread(): came = [lax.ppermute(held, SEQ, pairs) for pairs in step]  6.11 us
    pallas_call x1, Pallas kernels, place_near(): pl.pallas_call(place_kernel, out_shape=(shape, shape), grid_spec=pltpu.Pr...  5.63 us
  transfers between devices with their start and end apart: 16, of which 5 were waited for; matrix products, arithmetic and copies ran while one was open for 0% of the time, Pallas kernels for 17%

profile of v2, /device:TPU:192, one launch (start us, length us, event | category | flops | bytes accessed | tf_op | source)
XLA Modules:
  0.0 169.9 jit_solution(582461856977154745)
XLA Ops:
  0.6 0.7 bitcast_select_fusion
  1.3 0.7 pad_add_fusion.meta_ref
  2.0 0.9 copy-done
  3.0 0.0 copy-start.2
  3.0 0.9 copy-done.2
  3.9 2.7 %pack_near.1 = (bf16[32,256,128]{2,1,0:T(8,128)(2,1)}, bf16[1024,256]{1,0:T(8,128)(2,1)S(1)}) custom-call(s32[1]{0:T(128)S(6)} %mul.18.base_ref, s32[8,8]{1,0:T(8,128)S(1)} %pad_add_fusion.meta_ref, bf16[512,256]{1,0:T(8,128)(2,1)S(1)} %copy-done, bf16[512,256]{1,0:T(8,128)(2,1)S(1)} %copy-done.2), custom_call_target="tpu_custom_call" | custom-call | bytes 3145728 | tf_op jit(solution)/shard_map/pack_near/pallas_call | solution.py:126
  6.6 7.6 %all-to-all-start.1 = ((bf16[32,256,128]{2,1,0:T(8,128)(2,1)}), bf16[32,256,128]{2,1,0:T(8,128)(2,1)}, u32[]{:S(2)}, u32[]{:S(2)}) async-start(bf16[32,256,128]{2,1,0:T(8,128)(2,1)} %get-tuple-element.14), calls=%async_computation.1 | async-start | bytes 4194304 | tf_op jit(solution)/shard_map/all_to_all | solution.py:379
  14.2 0.0 copy-start.1
  14.2 0.0 copy-done.4
  14.2 0.8 collective-permute-start.5
  15.0 0.0 collective-permute-done.5
  15.1 0.7 collective-permute-start.6
  15.7 0.7 collective-permute-start.7
  16.4 0.7 collective-permute-start.8
  17.1 0.6 collective-permute-start.4
  17.7 0.0 collective-permute-done.6
  17.7 0.0 collective-permute-done.7
  17.7 0.0 collective-permute-done.8
  17.8 0.7 collective-permute-start.10
  18.4 0.7 collective-permute-start.11
  19.1 0.7 collective-permute-start.9
  19.8 0.0 collective-permute-done.10
  19.8 0.0 collective-permute-done.11
  19.8 0.0 collective-permute-done.9
  19.9 1.3 collective-permute-start.12
  21.2 32.0 %collective-permute-done.12 = bf16[64,1024]{1,0:T(8,128)(2,1)S(1)} collective-permute-done((bf16[64,1024]{1,0:T(8,128)(2,1)S(1)}, bf16[64,1024]{1,0:T(8,128)(2,1)S(1)}, u32[]{:S(2)}, u32[]{:S(2)}) %collective-permute-start.12) | collective-permute-done | bytes 131104 | tf_op jit(solution)/shard_map/ppermute | solution.py:361
  53.2 0.0 copy-done.1
  53.2 0.5 observe.1.stats_ref
  53.7 0.0 copy-start.3
  53.7 1.0 collective-permute-start.13
  54.7 5.0 %collective-permute-start.3 = (s32[8,8]{1,0:T(8,128)S(1)}, s32[8,8]{1,0:T(8,128)S(1)}, u32[]{:S(2)}, u32[]{:S(2)}) collective-permute-start(s32[8,8]{1,0:T(8,128)S(1)} %pad_add_fusion.meta_ref), channel_id=1, source_target_pairs={{0,128},{128,0},{1,129},{129,1},{2,130},{130,2},{3,131},{131,3},{4... | collective-permute-start | bytes 776 | tf_op jit(solution)/shard_map/ppermute | solution.py:385
  59.8 2.5 %collective-permute-done.3.other_meta_ref = s32[8,8]{1,0:T(8,128)S(1)} collective-permute-done((s32[8,8]{1,0:T(8,128)S(1)}, s32[8,8]{1,0:T(8,128)S(1)}, u32[]{:S(2)}, u32[]{:S(2)}) %collective-permute-start.3) | collective-permute-done | bytes 288 | tf_op jit(solution)/shard_map/ppermute | solution.py:385
  62.2 0.0 collective-permute-done.4.pair_ref
  62.2 0.0 collective-permute-done.13.other_ref
  62.2 3.2 %pack_far.1 = bf16[32,288,128]{2,1,0:T(8,128)(2,1)} custom-call(s32[1]{0:T(128)S(6)} %mul.18.base_ref, s32[8,8]{1,0:T(8,128)S(1)} %pad_add_fusion.meta_ref, s32[8,8]{1,0:T(8,128)S(1)} %collective-permute-done.3.other_meta_ref, bf16[1024,256]{1,0:T(8,128)(2,1)S(1)} %collective-permute-done.4.pair_ref, f32[24,128]{1,0:T(8,128)S(1)} %observe.1.stats_ref, ...), custom_call_target="tpu_custom_call" | custom-call | bytes 3145728 | tf_op jit(solution)/shard_map/pack_far/pallas_call | solution.py:186
  65.4 0.0 all-to-all-done.1.got_ref
  65.4 0.0 copy-done.3
  65.4 4.9 %all-to-all-start = ((bf16[32,288,128]{2,1,0:T(8,128)(2,1)}), bf16[32,288,128]{2,1,0:T(8,128)(2,1)}, u32[]{:S(2)}, u32[]{:S(2)}) async-start(bf16[32,288,128]{2,1,0:T(8,128)(2,1)} %pack_far.1), calls=%async_computation | async-start | bytes 4718592 | tf_op jit(solution)/shard_map/all_to_all | solution.py:379
  70.3 2.1 %collective-permute-start = (bf16[1024,256]{1,0:T(8,128)(2,1)S(1)}, bf16[1024,256]{1,0:T(8,128)(2,1)S(1)}, u32[]{:S(2)}, u32[]{:S(2)}) collective-permute-start(bf16[1024,256]{1,0:T(8,128)(2,1)S(1)} %get-tuple-element.13.k0.v0), channel_id=1, source_target_pairs={{0,4},{4,8},{8,12},{12,16},{16,20},{20,24},{24,28},{28,32},{32,36}... | collective-permute-start | bytes 1572872 | tf_op jit(solution)/shard_map/ppermute | solution.py:391
  72.5 29.3 %collective-permute-done.k1.v1 = bf16[1024,256]{1,0:T(8,128)(2,1)S(1)} collective-permute-done((bf16[1024,256]{1,0:T(8,128)(2,1)S(1)}, bf16[1024,256]{1,0:T(8,128)(2,1)S(1)}, u32[]{:S(2)}, u32[]{:S(2)}) %collective-permute-start) | collective-permute-done | bytes 524320 | tf_op jit(solution)/shard_map/ppermute | solution.py:391
  101.8 2.4 %collective-permute-start.1 = (bf16[1024,256]{1,0:T(8,128)(2,1)S(1)}, bf16[1024,256]{1,0:T(8,128)(2,1)S(1)}, u32[]{:S(2)}, u32[]{:S(2)}) collective-permute-start(bf16[1024,256]{1,0:T(8,128)(2,1)S(1)} %collective-permute-done.k1.v1), channel_id=1, source_target_pairs={{0,4},{4,8},{8,12},{12,16},{16,20},{20,24},{24,28},{28,32},{32,36}... | collective-permute-start | bytes 1572872 | tf_op jit(solution)/shard_map/ppermute | solution.py:391
  104.2 16.2 %collective-permute-done.1.k2.v2 = bf16[1024,256]{1,0:T(8,128)(2,1)S(1)} collective-permute-done((bf16[1024,256]{1,0:T(8,128)(2,1)S(1)}, bf16[1024,256]{1,0:T(8,128)(2,1)S(1)}, u32[]{:S(2)}, u32[]{:S(2)}) %collective-permute-start.1) | collective-permute-done | bytes 524320 | tf_op jit(solution)/shard_map/ppermute | solution.py:391
  120.4 1.9 %collective-permute-start.2 = (bf16[1024,256]{1,0:T(8,128)(2,1)S(1)}, bf16[1024,256]{1,0:T(8,128)(2,1)S(1)}, u32[]{:S(2)}, u32[]{:S(2)}) collective-permute-start(bf16[1024,256]{1,0:T(8,128)(2,1)S(1)} %collective-permute-done.1.k2.v2), channel_id=1, source_target_pairs={{0,4},{4,8},{8,12},{12,16},{16,20},{20,24},{24,28},{28,32},{32,36}... | collective-permute-start | bytes 1572872 | tf_op jit(solution)/shard_map/ppermute | solution.py:391
  122.3 16.7 %collective-permute-done.2.k3.v3 = bf16[1024,256]{1,0:T(8,128)(2,1)S(1)} collective-permute-done((bf16[1024,256]{1,0:T(8,128)(2,1)S(1)}, bf16[1024,256]{1,0:T(8,128)(2,1)S(1)}, u32[]{:S(2)}, u32[]{:S(2)}) %collective-permute-start.2) | collective-permute-done | bytes 524320 | tf_op jit(solution)/shard_map/ppermute | solution.py:391
  139.0 19.1 %attend.1 = bf16[512,1024]{1,0:T(8,128)(2,1)} custom-call(s32[1]{0:T(128)} %bitcast.pos_ref, bf16[512,1024]{1,0:T(8,128)(2,1)S(1)} %copy-done.4, bf16[1024,256]{1,0:T(8,128)(2,1)S(1)} %get-tuple-element.13.k0.v0, bf16[1024,256]{1,0:T(8,128)(2,1)S(1)} %get-tuple-element.13.k0.v0, bf16[1024,256]{1,0:T(8,128)(2,1)S(1)} %collective-permute-done.k1.v1, ...), custom_call_target="tpu_custom_call" | custom-call | flops 4294967296 | bytes 4194304 | tf_op jit(solution)/shard_map/attend/pallas_call | solution.py:75
  158.2 5.6 %place_near.1 = (bf16[64,128,128]{2,1,0:T(8,128)(2,1)}, bf16[64,128,128]{2,1,0:T(8,128)(2,1)}) custom-call(s32[1]{0:T(128)} %bitcast.1.half_ref, bf16[32,256,128]{2,1,0:T(8,128)(2,1)} %all-to-all-done.1.got_ref), custom_call_target="tpu_custom_call" | custom-call | bytes 4194304 | tf_op jit(solution)/shard_map/place_near/pallas_call | solution.py:250
  163.8 0.0 all-to-all-done.got_ref.mail_ref
  163.8 6.1 %place_last.1 = (bf16[64,128,128]{2,1,0:T(8,128)(2,1)}, bf16[64,128,128]{2,1,0:T(8,128)(2,1)}, bf16[1,64]{1,0:T(2,128)(2,1)}, f32[4,8]{1,0:T(4,128)}) custom-call(s32[1]{0:T(128)S(6)} %sub.3.half_ref, bf16[32,288,128]{2,1,0:T(8,128)(2,1)} %all-to-all-done.got_ref.mail_ref, ...), custom_call_target="tpu_custom_call", output_to_operand_aliasing={{0}: (4, {}), {1}: (5, {})} | custom-call | bytes 4194304 | tf_op jit(solution)/shard_map/place_last/pallas_call | solution.py:315
  (7 shorter events, 0.1 us)
Async XLA Ops:
  2.0 0.9 copy-start
  3.0 0.9 copy-start.2
  6.6 7.6 %copy-start.4 = (bf16[512,1024]{1,0:T(8,128)(2,1)S(1)}, bf16[512,1024]{1,0:T(8,128)(2,1)}, u32[]{:S(2)}) copy-start(bf16[512,1024]{1,0:T(8,128)(2,1)} %q_ref.1) | copy-start | bytes 3145732
  6.6 58.9 %all-to-all-start.1 = ((bf16[32,256,128]{2,1,0:T(8,128)(2,1)}), bf16[32,256,128]{2,1,0:T(8,128)(2,1)}, u32[]{:S(2)}, u32[]{:S(2)}) async-start(bf16[32,256,128]{2,1,0:T(8,128)(2,1)} %get-tuple-element.14), calls=%async_computation.1 | async-start | bytes 4194304 | tf_op jit(solution)/shard_map/all_to_all | solution.py:379
  14.2 39.1 %copy-start.1 = (bf16[512,256]{1,0:T(8,128)(2,1)S(1)}, bf16[512,256]{1,0:T(8,128)(2,1)}, u32[]{:S(2)}) copy-start(bf16[512,256]{1,0:T(8,128)(2,1)} %k_ref.3) | copy-start | bytes 786436
  14.2 0.8 collective-permute-start.5
  15.1 2.7 %collective-permute-start.6 = (bf16[64,1024]{1,0:T(8,128)(2,1)S(1)}, bf16[64,1024]{1,0:T(8,128)(2,1)S(1)}, u32[]{:S(2)}, u32[]{:S(2)}) collective-permute-start(bf16[64,1024]{1,0:T(8,128)(2,1)S(1)} %fusion), channel_id=1, source_target_pairs={{124,28},{252,156},{125,29},{253,157},{126,30},{254,158},{127,31},... | collective-permute-start | bytes 393224 | tf_op jit(solution)/shard_map/ppermute | solution.py:361
  15.7 2.0 %collective-permute-start.7 = (bf16[64,1024]{1,0:T(8,128)(2,1)S(1)}, bf16[64,1024]{1,0:T(8,128)(2,1)S(1)}, u32[]{:S(2)}, u32[]{:S(2)}) collective-permute-start(bf16[64,1024]{1,0:T(8,128)(2,1)S(1)} %fusion), channel_id=1, source_target_pairs={{124,60},{252,188},{125,61},{253,189},{126,62},{254,190},{127,63},... | collective-permute-start | bytes 393224 | tf_op jit(solution)/shard_map/ppermute | solution.py:361
  16.4 1.3 collective-permute-start.8
  17.1 45.2 %collective-permute-start.4 = (bf16[1024,256]{1,0:T(8,128)(2,1)S(1)}, bf16[1024,256]{1,0:T(8,128)(2,1)S(1)}, u32[]{:S(2)}, u32[]{:S(2)}) collective-permute-start(bf16[1024,256]{1,0:T(8,128)(2,1)S(1)} %get-tuple-element.13.k0.v0), channel_id=1, source_target_pairs={{0,128},{128,0},{1,129},{129,1},{2,130},{130,2},{3,131},{131,3},{4... | collective-permute-start | bytes 1572872 | tf_op jit(solution)/shard_map/ppermute | solution.py:386
  17.8 2.0 %collective-permute-start.10 = (bf16[64,1024]{1,0:T(8,128)(2,1)S(1)}, bf16[64,1024]{1,0:T(8,128)(2,1)S(1)}, u32[]{:S(2)}, u32[]{:S(2)}) collective-permute-start(bf16[64,1024]{1,0:T(8,128)(2,1)S(1)} %add_add_fusion.1), channel_id=1, source_target_pairs={{28,12},{60,44},{92,76},{124,108},{156,140},{188,172},{220,204},{2... | collective-permute-start | bytes 393224 | tf_op jit(solution)/shard_map/ppermute | solution.py:361
  18.4 1.4 collective-permute-start.11
  19.1 0.7 collective-permute-start.9
  19.9 33.3 %collective-permute-start.12 = (bf16[64,1024]{1,0:T(8,128)(2,1)S(1)}, bf16[64,1024]{1,0:T(8,128)(2,1)S(1)}, u32[]{:S(2)}, u32[]{:S(2)}) collective-permute-start(bf16[64,1024]{1,0:T(8,128)(2,1)S(1)} %add_add_fusion), channel_id=1, source_target_pairs={{4,0},{12,8},{20,16},{28,24},{36,32},{44,40},{52,48},{60,56},{68,6... | collective-permute-start | bytes 393224 | tf_op jit(solution)/shard_map/ppermute | solution.py:361
  53.7 11.7 %copy-start.3 = (f32[24,128]{1,0:T(8,128)}, f32[24,128]{1,0:T(8,128)S(1)}, u32[]{:S(2)}) copy-start(f32[24,128]{1,0:T(8,128)S(1)} %observe.1.stats_ref) | copy-start | bytes 36868
  53.7 8.5 %collective-permute-start.13 = (f32[24,128]{1,0:T(8,128)S(1)}, f32[24,128]{1,0:T(8,128)S(1)}, u32[]{:S(2)}, u32[]{:S(2)}) collective-permute-start(f32[24,128]{1,0:T(8,128)S(1)} %observe.1.stats_ref), channel_id=1, source_target_pairs={{0,128},{128,0},{1,129},{129,1},{2,130},{130,2},{3,131},{131,3},{4... | collective-permute-start | bytes 36872 | tf_op jit(solution)/shard_map/ppermute | solution.py:394
  54.7 7.5 %collective-permute-start.3 = (s32[8,8]{1,0:T(8,128)S(1)}, s32[8,8]{1,0:T(8,128)S(1)}, u32[]{:S(2)}, u32[]{:S(2)}) collective-permute-start(s32[8,8]{1,0:T(8,128)S(1)} %pad_add_fusion.meta_ref), channel_id=1, source_target_pairs={{0,128},{128,0},{1,129},{129,1},{2,130},{130,2},{3,131},{131,3},{4... | collective-permute-start | bytes 776 | tf_op jit(solution)/shard_map/ppermute | solution.py:385
  65.4 98.4 %all-to-all-start = ((bf16[32,288,128]{2,1,0:T(8,128)(2,1)}), bf16[32,288,128]{2,1,0:T(8,128)(2,1)}, u32[]{:S(2)}, u32[]{:S(2)}) async-start(bf16[32,288,128]{2,1,0:T(8,128)(2,1)} %pack_far.1), calls=%async_computation | async-start | bytes 4718592 | tf_op jit(solution)/shard_map/all_to_all | solution.py:379
  70.3 31.5 %collective-permute-start = (bf16[1024,256]{1,0:T(8,128)(2,1)S(1)}, bf16[1024,256]{1,0:T(8,128)(2,1)S(1)}, u32[]{:S(2)}, u32[]{:S(2)}) collective-permute-start(bf16[1024,256]{1,0:T(8,128)(2,1)S(1)} %get-tuple-element.13.k0.v0), channel_id=1, source_target_pairs={{0,4},{4,8},{8,12},{12,16},{16,20},{20,24},{24,28},{28,32},{32,36}... | collective-permute-start | bytes 1572872 | tf_op jit(solution)/shard_map/ppermute | solution.py:391
  101.8 18.6 %collective-permute-start.1 = (bf16[1024,256]{1,0:T(8,128)(2,1)S(1)}, bf16[1024,256]{1,0:T(8,128)(2,1)S(1)}, u32[]{:S(2)}, u32[]{:S(2)}) collective-permute-start(bf16[1024,256]{1,0:T(8,128)(2,1)S(1)} %collective-permute-done.k1.v1), channel_id=1, source_target_pairs={{0,4},{4,8},{8,12},{12,16},{16,20},{20,24},{24,28},{28,32},{32,36}... | collective-permute-start | bytes 1572872 | tf_op jit(solution)/shard_map/ppermute | solution.py:391
  120.4 18.6 %collective-permute-start.2 = (bf16[1024,256]{1,0:T(8,128)(2,1)S(1)}, bf16[1024,256]{1,0:T(8,128)(2,1)S(1)}, u32[]{:S(2)}, u32[]{:S(2)}) collective-permute-start(bf16[1024,256]{1,0:T(8,128)(2,1)S(1)} %collective-permute-done.1.k2.v2), channel_id=1, source_target_pairs={{0,4},{4,8},{8,12},{12,16},{16,20},{20,24},{24,28},{28,32},{32,36}... | collective-permute-start | bytes 1572872 | tf_op jit(solution)/shard_map/ppermute | solution.py:391

commit v3 on v2

--- a/solution.py
+++ b/solution.py
@@ -70,8 +70,7 @@
 
 
 def attend(position, queries, pairs):
-    key_spec = pl.BlockSpec((SHARD, HD), lambda h: (0, h // GROUP))
-    value_spec = pl.BlockSpec((SHARD, HD), lambda h: (1, h // GROUP))
+    kv_spec = pl.BlockSpec((SHARD, HD), lambda h: (0, h // GROUP))
     return pl.pallas_call(
         attend_kernel,
         grid=(HEADS,),
@@ -80,7 +79,7 @@
             pl.BlockSpec(memory_space=pltpu.SMEM),
             pl.BlockSpec((SHARD, HD), lambda h: (0, h)),
         ]
-        + [key_spec, value_spec] * CYCLE,
+        + [kv_spec] * (2 * CYCLE),
         out_specs=pl.BlockSpec((SHARD, HD), lambda h: (0, h)),
         compiler_params=pltpu.CompilerParams(vmem_limit_bytes=32 * 1024 * 1024),
         cost_estimate=pl.CostEstimate(
@@ -89,7 +88,7 @@
             transcendentals=HEADS * SHARD * SHARD * 4,
         ),
         name="attend",
-    )(position, queries, *[pair for pair in pairs for _ in range(2)])
+    )(position, queries, *[part for pair in pairs for part in pair])
 
 
 SMEM = pl.BlockSpec(memory_space=pltpu.SMEM)
@@ -147,7 +146,7 @@
 
 
 def far_kernel(
-    base_ref, meta_ref, other_meta_ref, pair_ref, stats_ref, other_ref, out_ref, tile_ref
+    base_ref, meta_ref, other_meta_ref, pair_ref, stats_ref, other_ref, _k, _v, out_ref, tile_ref
 ):
     level, other_level = stats_ref[0:4], other_ref[0:4]
     top = jnp.maximum(level, other_level)
@@ -182,17 +181,17 @@
     seats(base_ref[0], other_meta_ref, put)
 
 
-def pack_far(base, meta, other_meta, other_pair, stats, other_stats):
+def pack_far(base, meta, other_meta, other_pair, stats, other_stats, last):
     return pl.pallas_call(
         far_kernel,
         out_shape=jax.ShapeDtypeStruct((HALF, 2 * BLOCK + 32, HD), jnp.bfloat16),
-        in_specs=[SMEM, SMEM, SMEM, VMEM, VMEM, VMEM],
+        in_specs=[SMEM, SMEM, SMEM, VMEM, VMEM, VMEM, ANY, ANY],
         out_specs=VMEM,
         scratch_shapes=[pltpu.VMEM((2, BLKS, 16, 128), jnp.float32)],
         compiler_params=pltpu.CompilerParams(vmem_limit_bytes=16 * 1024 * 1024),
         cost_estimate=pl.CostEstimate(flops=0, bytes_accessed=3 * 1024 * 1024, transcendentals=0),
         name="pack_far",
-    )(base, meta, other_meta, other_pair, stats, other_stats)
+    )(base, meta, other_meta, other_pair, stats, other_stats, *last)
 
 
 def observe_kernel(pos_ref, q_ref, k_ref, stats_ref):
@@ -236,82 +235,86 @@
     )(position, observers, keys)
 
 
-CHUNK = 4
-
-
-def place_kernel(half_ref, got_ref, key_ref, value_ref):
-    key_ref[...] = got_ref[:, :BLOCK]
-    value_ref[...] = got_ref[:, BLOCK : 2 * BLOCK]
+def deliver(half, got_ref, key_ref, value_ref, sems):
+    rows = pl.ds(half * HALF, HALF)
+    return (
+        pltpu.make_async_copy(got_ref.at[:, :BLOCK], key_ref.at[rows], sems.at[0]),
+        pltpu.make_async_copy(got_ref.at[:, BLOCK : 2 * BLOCK], value_ref.at[rows], sems.at[1]),
+    )
+
+
+def place_kernel(half_ref, got_ref, key_ref, value_ref, sems):
+    copies = deliver(half_ref[0], got_ref, key_ref, value_ref, sems)
+    for copy in copies:
+        copy.start()
+    for copy in copies:
+        copy.wait()
 
 
 def place_near(half, got):
     shape = jax.ShapeDtypeStruct((NSEQ, BLOCK, HD), jnp.bfloat16)
-    out_spec = pl.BlockSpec((CHUNK, BLOCK, HD), lambda i, half: (half[0] * (HALF // CHUNK) + i, 0, 0))
     return pl.pallas_call(
         place_kernel,
         out_shape=(shape, shape),
-        grid_spec=pltpu.PrefetchScalarGridSpec(
-            num_scalar_prefetch=1,
-            grid=(HALF // CHUNK,),
-            in_specs=[pl.BlockSpec((CHUNK, 2 * BLOCK, HD), lambda i, half: (i, 0, 0))],
-            out_specs=(out_spec, out_spec),
-        ),
+        in_specs=[SMEM, VMEM],
+        out_specs=(ANY, ANY),
+        scratch_shapes=[pltpu.SemaphoreType.DMA((2,))],
+        compiler_params=pltpu.CompilerParams(vmem_limit_bytes=16 * 1024 * 1024),
         cost_estimate=pl.CostEstimate(flops=0, bytes_accessed=4 * 1024 * 1024, transcendentals=0),
         name="place_near",
     )(half, got)
 
 
 def last_kernel(
-    half_ref, got_ref, mail_ref, stats_ref, _k, _v, key_ref, value_ref, recv_ref, block_ref
+    half_ref, got_ref, stats_ref, _k, _v, key_ref, value_ref, recv_ref, block_ref, sems
 ):
-    key_ref[...] = got_ref[:, :BLOCK]
-    value_ref[...] = got_ref[:, BLOCK : 2 * BLOCK]
-
-    @pl.when(pl.program_id(0) == 0)
-    def _():
-        factor = BLKS * NSEQ / OBS
-        lead = mail_ref[:, :16].astype(jnp.float32)
-        level = (lead[:, 8:12] + lead[:, 4:8]) + lead[:, 0:4]
-        top = jnp.max(level, axis=0)
-        total = top + jnp.log(jnp.sum(jnp.exp(level - top[None]), axis=0))
-        share = jnp.exp(level - total[None])
-        tail = mail_ref[:, 16:].astype(jnp.float32)
-        own = jnp.sum((tail[:, 4:8] + tail[:, 0:4]) * share, axis=1)
-        other = jnp.sum((tail[:, 12:16] + tail[:, 8:12]) * share, axis=1)
-        far = half_ref[0] == 0
-        rows = jnp.concatenate(
-            [jnp.where(far, other, own), jnp.where(far, own, other)], axis=0
-        )
-        lined = lax.dot_general(
-            jnp.ones((8, 128), jnp.float32),
-            rows,
-            NT,
-            precision=lax.Precision.HIGHEST,
-            preferred_element_type=jnp.float32,
-        )
-        recv_ref[...] = (lined[0:1] * factor).astype(jnp.bfloat16)
-        mine = jnp.exp(stats_ref[0:4] - total)
-        row = lax.broadcasted_iota(jnp.int32, (HEADS, 4 * 128), 0)
-        lane = lax.broadcasted_iota(jnp.int32, (HEADS, 4 * 128), 1)
-        chosen = (lane // OBS == row).astype(jnp.float32)
-        parts = []
-        for b in range(BLKS):
-            part = stats_ref[4 + 4 * b : 8 + 4 * b] * mine
-            parts.append(jnp.concatenate([part[r : r + 1] for r in range(4)], axis=1))
-        table = jnp.concatenate(parts + parts, axis=0)
-        scores = lax.dot_general(
-            table,
-            chosen,
-            NT,
-            precision=lax.Precision.HIGHEST,
-            preferred_element_type=jnp.float32,
-        )
-        block_ref[...] = scores[:BLKS] * factor
+    copies = deliver(half_ref[0], got_ref, key_ref, value_ref, sems)
+    for copy in copies:
+        copy.start()
+    factor = BLKS * NSEQ / OBS
+    lead = got_ref[:, 2 * BLOCK : 2 * BLOCK + 16].astype(jnp.float32)
+    level = (lead[:, 8:12] + lead[:, 4:8]) + lead[:, 0:4]
+    top = jnp.max(level, axis=0)
+    total = top + jnp.log(jnp.sum(jnp.exp(level - top[None]), axis=0))
+    share = jnp.exp(level - total[None])
+    tail = got_ref[:, 2 * BLOCK + 16 :].astype(jnp.float32)
+    own = jnp.sum((tail[:, 4:8] + tail[:, 0:4]) * share, axis=1)
+    other = jnp.sum((tail[:, 12:16] + tail[:, 8:12]) * share, axis=1)
+    far = half_ref[0] == 0
+    rows = jnp.concatenate(
+        [jnp.where(far, other, own), jnp.where(far, own, other)], axis=0
+    )
+    lined = lax.dot_general(
+        jnp.ones((8, 128), jnp.float32),
+        rows,
+        NT,
+        precision=lax.Precision.HIGHEST,
+        preferred_element_type=jnp.float32,
+    )
+    recv_ref[...] = (lined[0:1] * factor).astype(jnp.bfloat16)
+    mine = jnp.exp(stats_ref[0:4] - total)
+    row = lax.broadcasted_iota(jnp.int32, (HEADS, 4 * 128), 0)
+    lane = lax.broadcasted_iota(jnp.int32, (HEADS, 4 * 128), 1)
+    chosen = (lane // OBS == row).astype(jnp.float32)
+    parts = []
+    for b in range(BLKS):
+        part = stats_ref[4 + 4 * b : 8 + 4 * b] * mine
+        parts.append(jnp.concatenate([part[r : r + 1] for r in range(4)], axis=1))
+    table = jnp.concatenate(parts + parts, axis=0)
+    scores = lax.dot_general(
+        table,
+        chosen,
+        NT,
+        precision=lax.Precision.HIGHEST,
+        preferred_element_type=jnp.float32,
+    )
+    block_ref[...] = scores[:BLKS] * factor
+    for copy in copies:
+        copy.wait()
 
 
 def place_last(half, got, stats, earlier):
     shape = jax.ShapeDtypeStruct((NSEQ, BLOCK, HD), jnp.bfloat16)
-    out_spec = pl.BlockSpec((CHUNK, BLOCK, HD), lambda i, half: (half[0] * (HALF // CHUNK) + i, 0, 0))
     return pl.pallas_call(
         last_kernel,
         out_shape=(
@@ -320,27 +323,14 @@
             jax.ShapeDtypeStruct((1, NSEQ), jnp.bfloat16),
             jax.ShapeDtypeStruct((BLKS, HEADS), jnp.float32),
         ),
-        grid_spec=pltpu.PrefetchScalarGridSpec(
-            num_scalar_prefetch=1,
-            grid=(HALF // CHUNK,),
-            in_specs=[
-                pl.BlockSpec((CHUNK, 2 * BLOCK, HD), lambda i, half: (i, 0, 0)),
-                pl.BlockSpec((HALF, 32, HD), lambda i, half: (0, 2 * BLOCK // 32, 0)),
-                pl.BlockSpec((24, 128), lambda i, half: (0, 0)),
-                ANY,
-                ANY,
-            ],
-            out_specs=(
-                out_spec,
-                out_spec,
-                pl.BlockSpec((1, NSEQ), lambda i, half: (0, 0)),
-                pl.BlockSpec((BLKS, HEADS), lambda i, half: (0, 0)),
-            ),
-        ),
-        input_output_aliases={4: 0, 5: 1},
+        in_specs=[SMEM, VMEM, VMEM, ANY, ANY],
+        out_specs=(ANY, ANY, VMEM, VMEM),
+        scratch_shapes=[pltpu.SemaphoreType.DMA((2,))],
+        input_output_aliases={3: 0, 4: 1},
+        compiler_params=pltpu.CompilerParams(vmem_limit_bytes=16 * 1024 * 1024),
         cost_estimate=pl.CostEstimate(flops=0, bytes_accessed=4 * 1024 * 1024, transcendentals=0),
         name="place_last",
-    )(half, got, got, stats, *earlier)
+    )(half, got, stats, *earlier)
 
 
 def spread(tail):
@@ -386,13 +376,15 @@
     other_pair = lax.ppermute(pair, "zh", swap)
 
     hops = [(i, i + 1) for i in range(NSEQ - 1)]
-    held = [pair]
+    held = [(keys, values)]
     for _ in range(1, CYCLE):
-        held.append(lax.ppermute(held[-1], SEQ, hops))
+        held.append(tuple(lax.ppermute(part, SEQ, hops) for part in held[-1]))
 
     stats = observe(pos, observers, keys)
     other_stats = lax.ppermute(stats, "zh", swap)
-    far = exchange(pack_far(base, meta, other_meta, other_pair, stats, other_stats))
+    far = exchange(
+        pack_far(base, meta, other_meta, other_pair, stats, other_stats, held[-1])
+    )
     attended = attend(pos, queries, held)
     first = place_near(near_half, near)
     recv_keys, recv_values, recv_scores, scores_here = place_last(1 - near_half, far, stats, first)

time: 171 us -> 142 us (0.83)
  waiting for transfers between devices: 96.8 us -> 60.8 us
  Pallas kernels: 37.3 us -> 26.8 us
  local copies, waits for them, and re-layouts: 1.91 us -> 11 us
  starting transfers between devices: 31.6 us -> 37.7 us
  other arithmetic: 1.51 us -> 3.32 us
    ppermute x8, waiting for transfers between devices: 32 us -> 1.96 us  [spread(): came = [lax.ppermute(held, SEQ, pairs) for pairs in step]]
    ppermute x3 -> x6, waiting for transfers between devices: 62.3 us -> 47.6 us  [shards(): held.append(tuple((lax.ppermute(part, SEQ, hops) for part in held[-1])))]
    unnamed x10 -> x34, local copies, waits for them, and re-layouts: 1.91 us -> 11 us
    all_to_all x2, waiting for transfers between devices: 0.01 us -> 7.58 us  [exchange(): lax.all_to_all(packed, PLANE, split_axis=0, concat_axis=0, tiled=True)]
    ppermute x3 -> x6, starting transfers between devices: 6.39 us -> 13.6 us  [shards(): held.append(tuple((lax.ppermute(part, SEQ, hops) for part in held[-1])))]
    pallas_call x1, Pallas kernels: 5.63 us -> 1.33 us  [place_near(): pl.pallas_call(place_kernel, out_shape=(shape, shape), in_specs=[SMEM, VM...]
    pallas_call x1, Pallas kernels: 6.13 us -> 1.92 us  [place_last(): pl.pallas_call(last_kernel, out_shape=(shape, shape, jax.ShapeDtypeStruct...]
  transfers between devices with their start and end apart: 16 -> 19, of which waited for: 5 -> 9; matrix products, arithmetic and copies ran while one was open for 0% -> 1% of each run, Pallas kernels for 17% -> 16%
where the time goes in v3:
time: 142 us; the launch traced here: 141 us
  waiting for transfers between devices  60.8 us (43%)
  starting transfers between devices  37.7 us (27%)
  Pallas kernels  26.8 us (19%)
  local copies, waits for them, and re-layouts  11 us (8%)
  other arithmetic  3.32 us (2%)
    ppermute x6, waiting for transfers between devices, shards(): held.append(tuple((lax.ppermute(part, SEQ, hops) for part in held[-1])))  47.6 us
    pallas_call x1, Pallas kernels, attend(): pl.pallas_call(attend_kernel, grid=(HEADS,), out_shape=jax.ShapeDtypeStru...  19.1 us
    ppermute x6, starting transfers between devices, shards(): held.append(tuple((lax.ppermute(part, SEQ, hops) for part in held[-1])))  13.6 us
    all_to_all x2, starting transfers between devices, exchange(): lax.all_to_all(packed, PLANE, split_axis=0, concat_axis=0, tiled=True)  11.5 us
    unnamed x34, local copies, waits for them, and re-layouts  11 us
    all_to_all x2, waiting for transfers between devices, exchange(): lax.all_to_all(packed, PLANE, split_axis=0, concat_axis=0, tiled=True)  7.58 us
    ppermute x8, starting transfers between devices, spread(): came = [lax.ppermute(held, SEQ, pairs) for pairs in step]  5.96 us
    ppermute x1, starting transfers between devices, shards(): other_meta = lax.ppermute(meta, 'zh', swap)  5.92 us
  transfers between devices with their start and end apart: 19, of which 9 were waited for; matrix products, arithmetic and copies ran while one was open for 1% of the time, Pallas kernels for 16%

profile of v3, /device:TPU:192, one launch (start us, length us, event | category | flops | bytes accessed | tf_op | source)
XLA Modules:
  0.0 140.5 jit_solution(14475485551921117765)
XLA Ops:
  0.6 0.7 bitcast_select_fusion
  1.3 0.7 pad_add_fusion.meta_ref
  2.0 0.9 copy-done.4
  3.0 0.9 copy-done.6
  3.9 2.1 %pack_near.1 = (bf16[32,256,128]{2,1,0:T(8,128)(2,1)S(1)}, bf16[1024,256]{1,0:T(8,128)(2,1)}) custom-call(s32[1]{0:T(128)S(6)} %mul.18.base_ref, s32[8,8]{1,0:T(8,128)S(1)} %pad_add_fusion.meta_ref, bf16[512,256]{1,0:T(8,128)(2,1)S(1)} %copy-done.4, bf16[512,256]{1,0:T(8,128)(2,1)S(1)} %copy-done.6), custom_call_target="tpu_custom_call" | custom-call | bytes 3145728 | tf_op jit(solution)/shard_map/pack_near/pallas_call | solution.py:125
  6.1 1.3 copy-done.3
  7.4 7.4 %all-to-all-start.1 = ((bf16[32,256,128]{2,1,0:T(8,128)(2,1)}), bf16[32,256,128]{2,1,0:T(8,128)(2,1)S(1)}, u32[]{:S(2)}, u32[]{:S(2)}) async-start(bf16[32,256,128]{2,1,0:T(8,128)(2,1)} %copy-done.3), calls=%async_computation.1 | async-start | bytes 4194304 | tf_op jit(solution)/shard_map/all_to_all | solution.py:369
  14.8 0.9 slice_select_fusion
  15.7 0.7 collective-permute-start.8
  16.4 2.2 %collective-permute-start.1 = (bf16[512,256]{1,0:T(8,128)(2,1)S(1)}, bf16[512,256]{1,0:T(8,128)(2,1)S(1)}, u32[]{:S(2)}, u32[]{:S(2)}) collective-permute-start(bf16[512,256]{1,0:T(8,128)(2,1)S(1)} %copy-done.7), channel_id=1, source_target_pairs={{0,4},{4,8},{8,12},{12,16},{16,20},{20,24},{24,28},{28,32},{32,36}... | collective-permute-start | bytes 786440 | tf_op jit(solution)/shard_map/ppermute | solution.py:381
  18.6 3.5 %collective-permute-start = (bf16[512,256]{1,0:T(8,128)(2,1)S(1)}, bf16[512,256]{1,0:T(8,128)(2,1)S(1)}, u32[]{:S(2)}, u32[]{:S(2)}) collective-permute-start(bf16[512,256]{1,0:T(8,128)(2,1)S(1)} %copy-done.5), channel_id=1, source_target_pairs={{0,4},{4,8},{8,12},{12,16},{16,20},{20,24},{24,28},{28,32},{32,36}... | collective-permute-start | bytes 786440 | tf_op jit(solution)/shard_map/ppermute | solution.py:381
  22.2 0.9 fusion
  23.1 0.7 collective-permute-start.11
  23.8 0.7 collective-permute-start.10
  24.5 0.7 collective-permute-start.9
  25.1 16.0 %collective-permute-done.1.v1 = bf16[512,256]{1,0:T(8,128)(2,1)S(1)} collective-permute-done((bf16[512,256]{1,0:T(8,128)(2,1)S(1)}, bf16[512,256]{1,0:T(8,128)(2,1)S(1)}, u32[]{:S(2)}, u32[]{:S(2)}) %collective-permute-start.1) | collective-permute-done | bytes 262176 | tf_op jit(solution)/shard_map/ppermute | solution.py:381
  41.1 1.9 %collective-permute-start.3 = (bf16[512,256]{1,0:T(8,128)(2,1)S(1)}, bf16[512,256]{1,0:T(8,128)(2,1)S(1)}, u32[]{:S(2)}, u32[]{:S(2)}) collective-permute-start(bf16[512,256]{1,0:T(8,128)(2,1)S(1)} %collective-permute-done.1.v1), channel_id=1, source_target_pairs={{0,4},{4,8},{8,12},{12,16},{16,20},{20,24},{24,28},{28,32},{32,36}... | collective-permute-start | bytes 786440 | tf_op jit(solution)/shard_map/ppermute | solution.py:381
  43.0 2.1 %collective-permute-done.k1 = bf16[512,256]{1,0:T(8,128)(2,1)S(1)} collective-permute-done((bf16[512,256]{1,0:T(8,128)(2,1)S(1)}, bf16[512,256]{1,0:T(8,128)(2,1)S(1)}, u32[]{:S(2)}, u32[]{:S(2)}) %collective-permute-start) | collective-permute-done | bytes 262176 | tf_op jit(solution)/shard_map/ppermute | solution.py:381
  45.2 2.2 %collective-permute-start.2 = (bf16[512,256]{1,0:T(8,128)(2,1)S(1)}, bf16[512,256]{1,0:T(8,128)(2,1)S(1)}, u32[]{:S(2)}, u32[]{:S(2)}) collective-permute-start(bf16[512,256]{1,0:T(8,128)(2,1)S(1)} %collective-permute-done.k1), channel_id=1, source_target_pairs={{0,4},{4,8},{8,12},{12,16},{16,20},{20,24},{24,28},{28,32},{32,36}... | collective-permute-start | bytes 786440 | tf_op jit(solution)/shard_map/ppermute | solution.py:381
  47.4 0.7 collective-permute-start.14
  48.1 0.6 collective-permute-start.7
  48.7 0.7 collective-permute-start.13
  49.4 0.7 collective-permute-start.12
  50.1 6.9 %collective-permute-done.3.v2 = bf16[512,256]{1,0:T(8,128)(2,1)S(1)} collective-permute-done((bf16[512,256]{1,0:T(8,128)(2,1)S(1)}, bf16[512,256]{1,0:T(8,128)(2,1)S(1)}, u32[]{:S(2)}, u32[]{:S(2)}) %collective-permute-start.3) | collective-permute-done | bytes 262176 | tf_op jit(solution)/shard_map/ppermute | solution.py:381
  57.0 1.9 %collective-permute-start.5 = (bf16[512,256]{1,0:T(8,128)(2,1)S(1)}, bf16[512,256]{1,0:T(8,128)(2,1)S(1)}, u32[]{:S(2)}, u32[]{:S(2)}) collective-permute-start(bf16[512,256]{1,0:T(8,128)(2,1)S(1)} %collective-permute-done.3.v2), channel_id=1, source_target_pairs={{0,4},{4,8},{8,12},{12,16},{16,20},{20,24},{24,28},{28,32},{32,36}... | collective-permute-start | bytes 786440 | tf_op jit(solution)/shard_map/ppermute | solution.py:381
  58.9 4.0 %collective-permute-done.2.k2 = bf16[512,256]{1,0:T(8,128)(2,1)S(1)} collective-permute-done((bf16[512,256]{1,0:T(8,128)(2,1)S(1)}, bf16[512,256]{1,0:T(8,128)(2,1)S(1)}, u32[]{:S(2)}, u32[]{:S(2)}) %collective-permute-start.2) | collective-permute-done | bytes 262176 | tf_op jit(solution)/shard_map/ppermute | solution.py:381
  62.9 1.9 %collective-permute-start.4 = (bf16[512,256]{1,0:T(8,128)(2,1)S(1)}, bf16[512,256]{1,0:T(8,128)(2,1)S(1)}, u32[]{:S(2)}, u32[]{:S(2)}) collective-permute-start(bf16[512,256]{1,0:T(8,128)(2,1)S(1)} %collective-permute-done.2.k2), channel_id=1, source_target_pairs={{0,4},{4,8},{8,12},{12,16},{16,20},{20,24},{24,28},{28,32},{32,36}... | collective-permute-start | bytes 786440 | tf_op jit(solution)/shard_map/ppermute | solution.py:381
  64.9 1.3 collective-permute-start.15
  66.2 1.9 %collective-permute-done.15 = bf16[64,1024]{1,0:T(8,128)(2,1)S(1)} collective-permute-done((bf16[64,1024]{1,0:T(8,128)(2,1)S(1)}, bf16[64,1024]{1,0:T(8,128)(2,1)S(1)}, u32[]{:S(2)}, u32[]{:S(2)}) %collective-permute-start.15) | collective-permute-done | bytes 131104 | tf_op jit(solution)/shard_map/ppermute | solution.py:351
  68.2 0.5 observe.1.stats_ref
  68.7 0.1 collective-permute-start.16
  68.8 5.9 %collective-permute-start.6 = (s32[8,8]{1,0:T(8,128)S(1)}, s32[8,8]{1,0:T(8,128)S(1)}, u32[]{:S(2)}, u32[]{:S(2)}) collective-permute-start(s32[8,8]{1,0:T(8,128)S(1)} %pad_add_fusion.meta_ref), channel_id=1, source_target_pairs={{0,128},{128,0},{1,129},{129,1},{2,130},{130,2},{3,131},{131,3},{4... | collective-permute-start | bytes 776 | tf_op jit(solution)/shard_map/ppermute | solution.py:375
  74.7 3.7 %collective-permute-done.6.other_meta_ref = s32[8,8]{1,0:T(8,128)S(1)} collective-permute-done((s32[8,8]{1,0:T(8,128)S(1)}, s32[8,8]{1,0:T(8,128)S(1)}, u32[]{:S(2)}, u32[]{:S(2)}) %collective-permute-start.6) | collective-permute-done | bytes 288 | tf_op jit(solution)/shard_map/ppermute | solution.py:375
  78.3 15.8 %collective-permute-done.5.v3._v = bf16[512,256]{1,0:T(8,128)(2,1)S(1)} collective-permute-done((bf16[512,256]{1,0:T(8,128)(2,1)S(1)}, bf16[512,256]{1,0:T(8,128)(2,1)S(1)}, u32[]{:S(2)}, u32[]{:S(2)}) %collective-permute-start.5) | collective-permute-done | bytes 262176 | tf_op jit(solution)/shard_map/ppermute | solution.py:381
  94.1 2.8 %collective-permute-done.4.k3._k = bf16[512,256]{1,0:T(8,128)(2,1)S(1)} collective-permute-done((bf16[512,256]{1,0:T(8,128)(2,1)S(1)}, bf16[512,256]{1,0:T(8,128)(2,1)S(1)}, u32[]{:S(2)}, u32[]{:S(2)}) %collective-permute-start.4) | collective-permute-done | bytes 262176 | tf_op jit(solution)/shard_map/ppermute | solution.py:381
  96.9 1.8 %pack_far.1 = bf16[32,288,128]{2,1,0:T(8,128)(2,1)S(1)} custom-call(s32[1]{0:T(128)S(6)} %mul.18.base_ref, s32[8,8]{1,0:T(8,128)S(1)} %pad_add_fusion.meta_ref, s32[8,8]{1,0:T(8,128)S(1)} %collective-permute-done.6.other_meta_ref, bf16[1024,256]{1,0:T(8,128)(2,1)S(1)} %collective-permute-done.7.pair_ref, f32[24,128]{1,0:T(8,128)S(1)} %observe.1.stats_ref, ...), custom_call_target="tpu_custom_call" | custom-call | bytes 3145728 | tf_op jit(solution)/shard_map/pack_far/pallas_call | solution.py:185
  98.7 1.4 %copy-done = bf16[32,288,128]{2,1,0:T(8,128)(2,1)} copy-done((bf16[32,288,128]{2,1,0:T(8,128)(2,1)}, bf16[32,288,128]{2,1,0:T(8,128)(2,1)S(1)}, u32[]{:S(2)}) %copy-start) | copy-done | bytes 2359320
  100.1 1.3 copy-done.1
  101.4 4.1 %all-to-all-start = ((bf16[32,288,128]{2,1,0:T(8,128)(2,1)}), bf16[32,288,128]{2,1,0:T(8,128)(2,1)S(1)}, u32[]{:S(2)}, u32[]{:S(2)}) async-start(bf16[32,288,128]{2,1,0:T(8,128)(2,1)} %copy-done), calls=%async_computation | async-start | bytes 4718592 | tf_op jit(solution)/shard_map/all_to_all | solution.py:369
  105.5 1.2 copy-done.8
  106.7 0.9 copy-done.10
  107.7 0.9 copy-done.12
  108.6 0.9 copy-done.14
  109.6 0.9 copy-done.16
  110.5 19.1 %attend.1 = bf16[512,1024]{1,0:T(8,128)(2,1)} custom-call(s32[1]{0:T(128)} %bitcast.pos_ref, bf16[512,1024]{1,0:T(8,128)(2,1)S(1)} %copy-done.8, bf16[512,256]{1,0:T(8,128)(2,1)S(1)} %copy-done.5, bf16[512,256]{1,0:T(8,128)(2,1)S(1)} %copy-done.7, bf16[512,256]{1,0:T(8,128)(2,1)S(1)} %copy-done.12, bf16[512,256]{1,0:T(8,128)(2,1)S(1)} %copy-done.10, ...), custom_call_target="tpu_custom_call" | custom-call | flops 4294967296 | bytes 4194304 | tf_op jit(solution)/shard_map/attend/pallas_call | solution.py:74
  129.7 1.3 place_near.1
  131.0 7.6 %all-to-all-done.got_ref = bf16[32,288,128]{2,1,0:T(8,128)(2,1)S(1)} async-done(((bf16[32,288,128]{2,1,0:T(8,128)(2,1)}), bf16[32,288,128]{2,1,0:T(8,128)(2,1)S(1)}, u32[]{:S(2)}, u32[]{:S(2)}) %all-to-all-start) | async-done | bytes 2359328 | tf_op jit(solution)/shard_map/all_to_all | solution.py:369
  138.6 1.9 %place_last.1 = (bf16[64,128,128]{2,1,0:T(8,128)(2,1)}, bf16[64,128,128]{2,1,0:T(8,128)(2,1)}, bf16[1,64]{1,0:T(2,128)(2,1)}, f32[4,8]{1,0:T(4,128)}) custom-call(s32[1]{0:T(128)S(6)} %sub.3.half_ref, bf16[32,288,128]{2,1,0:T(8,128)(2,1)S(1)} %all-to-all-done.got_ref, f32[24,128]{1,0:T(8,128)S(1)} %observe.1.stats_ref, ...), custom_call_target="tpu_custom_call", output_to_operand_aliasing={{0}: (3, {}), {1}: (4, {})} | custom-call | bytes 4194304 | tf_op jit(solution)/shard_map/place_last/pallas_call | solution.py:318
  (37 shorter events, 0.2 us)
Async XLA Ops:
  2.0 0.9 copy-start.4
  3.0 0.9 copy-start.6
  6.0 1.3 copy-start.3
  7.4 9.0 %copy-start.7 = (bf16[512,256]{1,0:T(8,128)(2,1)S(1)}, bf16[512,256]{1,0:T(8,128)(2,1)}, u32[]{:S(2)}) copy-start(bf16[512,256]{1,0:T(8,128)(2,1)} %v_ref.1) | copy-start | bytes 786436
  7.4 11.2 %copy-start.5 = (bf16[512,256]{1,0:T(8,128)(2,1)S(1)}, bf16[512,256]{1,0:T(8,128)(2,1)}, u32[]{:S(2)}) copy-start(bf16[512,256]{1,0:T(8,128)(2,1)} %k_ref.3) | copy-start | bytes 786436
  7.4 92.7 %all-to-all-start.1 = ((bf16[32,256,128]{2,1,0:T(8,128)(2,1)}), bf16[32,256,128]{2,1,0:T(8,128)(2,1)S(1)}, u32[]{:S(2)}, u32[]{:S(2)}) async-start(bf16[32,256,128]{2,1,0:T(8,128)(2,1)} %copy-done.3), calls=%async_computation.1 | async-start | bytes 4194304 | tf_op jit(solution)/shard_map/all_to_all | solution.py:369
  15.7 6.4 %collective-permute-start.8 = (bf16[64,1024]{1,0:T(8,128)(2,1)S(1)}, bf16[64,1024]{1,0:T(8,128)(2,1)S(1)}, u32[]{:S(2)}, u32[]{:S(2)}) collective-permute-start(bf16[64,1024]{1,0:T(8,128)(2,1)S(1)} %slice_select_fusion), channel_id=1, source_target_pairs={{252,124},{253,125},{254,126},{255,127}} | collective-permute-start | bytes 393224 | tf_op jit(solution)/shard_map/ppermute | solution.py:351
  16.4 24.7 %collective-permute-start.1 = (bf16[512,256]{1,0:T(8,128)(2,1)S(1)}, bf16[512,256]{1,0:T(8,128)(2,1)S(1)}, u32[]{:S(2)}, u32[]{:S(2)}) collective-permute-start(bf16[512,256]{1,0:T(8,128)(2,1)S(1)} %copy-done.7), channel_id=1, source_target_pairs={{0,4},{4,8},{8,12},{12,16},{16,20},{20,24},{24,28},{28,32},{32,36}... | collective-permute-start | bytes 786440 | tf_op jit(solution)/shard_map/ppermute | solution.py:381
  18.6 26.5 %collective-permute-start = (bf16[512,256]{1,0:T(8,128)(2,1)S(1)}, bf16[512,256]{1,0:T(8,128)(2,1)S(1)}, u32[]{:S(2)}, u32[]{:S(2)}) collective-permute-start(bf16[512,256]{1,0:T(8,128)(2,1)S(1)} %copy-done.5), channel_id=1, source_target_pairs={{0,4},{4,8},{8,12},{12,16},{16,20},{20,24},{24,28},{28,32},{32,36}... | collective-permute-start | bytes 786440 | tf_op jit(solution)/shard_map/ppermute | solution.py:381
  23.1 24.2 %collective-permute-start.11 = (bf16[64,1024]{1,0:T(8,128)(2,1)S(1)}, bf16[64,1024]{1,0:T(8,128)(2,1)S(1)}, u32[]{:S(2)}, u32[]{:S(2)}) collective-permute-start(bf16[64,1024]{1,0:T(8,128)(2,1)S(1)} %fusion), channel_id=1, source_target_pairs={{124,92},{252,220},{125,93},{253,221},{126,94},{254,222},{127,95},... | collective-permute-start | bytes 393224 | tf_op jit(solution)/shard_map/ppermute | solution.py:351
  23.8 23.6 %collective-permute-start.10 = (bf16[64,1024]{1,0:T(8,128)(2,1)S(1)}, bf16[64,1024]{1,0:T(8,128)(2,1)S(1)}, u32[]{:S(2)}, u32[]{:S(2)}) collective-permute-start(bf16[64,1024]{1,0:T(8,128)(2,1)S(1)} %fusion), channel_id=1, source_target_pairs={{124,60},{252,188},{125,61},{253,189},{126,62},{254,190},{127,63},... | collective-permute-start | bytes 393224 | tf_op jit(solution)/shard_map/ppermute | solution.py:351
  24.5 22.9 %collective-permute-start.9 = (bf16[64,1024]{1,0:T(8,128)(2,1)S(1)}, bf16[64,1024]{1,0:T(8,128)(2,1)S(1)}, u32[]{:S(2)}, u32[]{:S(2)}) collective-permute-start(bf16[64,1024]{1,0:T(8,128)(2,1)S(1)} %fusion), channel_id=1, source_target_pairs={{124,28},{252,156},{125,29},{253,157},{126,30},{254,158},{127,31},... | collective-permute-start | bytes 393224 | tf_op jit(solution)/shard_map/ppermute | solution.py:351
  41.1 8.9 %copy-start.9 = (bf16[512,256]{1,0:T(8,128)(2,1)}, bf16[512,256]{1,0:T(8,128)(2,1)S(1)}, u32[]{:S(2)}) copy-start(bf16[512,256]{1,0:T(8,128)(2,1)S(1)} %collective-permute-done.1.v1) | copy-start | bytes 786436
  41.1 15.8 %collective-permute-start.3 = (bf16[512,256]{1,0:T(8,128)(2,1)S(1)}, bf16[512,256]{1,0:T(8,128)(2,1)S(1)}, u32[]{:S(2)}, u32[]{:S(2)}) collective-permute-start(bf16[512,256]{1,0:T(8,128)(2,1)S(1)} %collective-permute-done.1.v1), channel_id=1, source_target_pairs={{0,4},{4,8},{8,12},{12,16},{16,20},{20,24},{24,28},{28,32},{32,36}... | collective-permute-start | bytes 786440 | tf_op jit(solution)/shard_map/ppermute | solution.py:381
  45.2 13.7 %copy-start.11 = (bf16[512,256]{1,0:T(8,128)(2,1)}, bf16[512,256]{1,0:T(8,128)(2,1)S(1)}, u32[]{:S(2)}) copy-start(bf16[512,256]{1,0:T(8,128)(2,1)S(1)} %collective-permute-done.k1) | copy-start | bytes 786436
  45.2 17.7 %collective-permute-start.2 = (bf16[512,256]{1,0:T(8,128)(2,1)S(1)}, bf16[512,256]{1,0:T(8,128)(2,1)S(1)}, u32[]{:S(2)}, u32[]{:S(2)}) collective-permute-start(bf16[512,256]{1,0:T(8,128)(2,1)S(1)} %collective-permute-done.k1), channel_id=1, source_target_pairs={{0,4},{4,8},{8,12},{12,16},{16,20},{20,24},{24,28},{28,32},{32,36}... | collective-permute-start | bytes 786440 | tf_op jit(solution)/shard_map/ppermute | solution.py:381
  47.4 2.0 %collective-permute-start.14 = (bf16[64,1024]{1,0:T(8,128)(2,1)S(1)}, bf16[64,1024]{1,0:T(8,128)(2,1)S(1)}, u32[]{:S(2)}, u32[]{:S(2)}) collective-permute-start(bf16[64,1024]{1,0:T(8,128)(2,1)S(1)} %add_add_fusion.1), channel_id=1, source_target_pairs={{28,20},{60,52},{92,84},{124,116},{156,148},{188,180},{220,212},{2... | collective-permute-start | bytes 393224 | tf_op jit(solution)/shard_map/ppermute | solution.py:351
  48.1 30.3 %collective-permute-start.7 = (bf16[1024,256]{1,0:T(8,128)(2,1)}, bf16[1024,256]{1,0:T(8,128)(2,1)S(1)}, u32[]{:S(2)}, u32[]{:S(2)}) collective-permute-start(bf16[1024,256]{1,0:T(8,128)(2,1)} %get-tuple-element.13), channel_id=1, source_target_pairs={{0,128},{128,0},{1,129},{129,1},{2,130},{130,2},{3,131},{131,3},{4... | collective-permute-start | bytes 1572872 | tf_op jit(solution)/shard_map/ppermute | solution.py:376
  48.7 16.1 %collective-permute-start.13 = (bf16[64,1024]{1,0:T(8,128)(2,1)S(1)}, bf16[64,1024]{1,0:T(8,128)(2,1)S(1)}, u32[]{:S(2)}, u32[]{:S(2)}) collective-permute-start(bf16[64,1024]{1,0:T(8,128)(2,1)S(1)} %add_add_fusion.1), channel_id=1, source_target_pairs={{28,12},{60,44},{92,76},{124,108},{156,140},{188,172},{220,204},{2... | collective-permute-start | bytes 393224 | tf_op jit(solution)/shard_map/ppermute | solution.py:351
  49.4 15.4 %collective-permute-start.12 = (bf16[64,1024]{1,0:T(8,128)(2,1)S(1)}, bf16[64,1024]{1,0:T(8,128)(2,1)S(1)}, u32[]{:S(2)}, u32[]{:S(2)}) collective-permute-start(bf16[64,1024]{1,0:T(8,128)(2,1)S(1)} %add_add_fusion.1), channel_id=1, source_target_pairs={{28,4},{60,36},{92,68},{124,100},{156,132},{188,164},{220,196},{25... | collective-permute-start | bytes 393224 | tf_op jit(solution)/shard_map/ppermute | solution.py:351
  56.9 37.2 %copy-start.13 = (bf16[512,256]{1,0:T(8,128)(2,1)}, bf16[512,256]{1,0:T(8,128)(2,1)S(1)}, u32[]{:S(2)}) copy-start(bf16[512,256]{1,0:T(8,128)(2,1)S(1)} %collective-permute-done.3.v2) | copy-start | bytes 786436
  57.0 37.2 %collective-permute-start.5 = (bf16[512,256]{1,0:T(8,128)(2,1)S(1)}, bf16[512,256]{1,0:T(8,128)(2,1)S(1)}, u32[]{:S(2)}, u32[]{:S(2)}) collective-permute-start(bf16[512,256]{1,0:T(8,128)(2,1)S(1)} %collective-permute-done.3.v2), channel_id=1, source_target_pairs={{0,4},{4,8},{8,12},{12,16},{16,20},{20,24},{24,28},{28,32},{32,36}... | collective-permute-start | bytes 786440 | tf_op jit(solution)/shard_map/ppermute | solution.py:381
  62.9 31.2 %copy-start.15 = (bf16[512,256]{1,0:T(8,128)(2,1)}, bf16[512,256]{1,0:T(8,128)(2,1)S(1)}, u32[]{:S(2)}) copy-start(bf16[512,256]{1,0:T(8,128)(2,1)S(1)} %collective-permute-done.2.k2) | copy-start | bytes 786436
  62.9 34.0 %collective-permute-start.4 = (bf16[512,256]{1,0:T(8,128)(2,1)S(1)}, bf16[512,256]{1,0:T(8,128)(2,1)S(1)}, u32[]{:S(2)}, u32[]{:S(2)}) collective-permute-start(bf16[512,256]{1,0:T(8,128)(2,1)S(1)} %collective-permute-done.2.k2), channel_id=1, source_target_pairs={{0,4},{4,8},{8,12},{12,16},{16,20},{20,24},{24,28},{28,32},{32,36}... | collective-permute-start | bytes 786440 | tf_op jit(solution)/shard_map/ppermute | solution.py:381
  64.9 3.2 %collective-permute-start.15 = (bf16[64,1024]{1,0:T(8,128)(2,1)S(1)}, bf16[64,1024]{1,0:T(8,128)(2,1)S(1)}, u32[]{:S(2)}, u32[]{:S(2)}) collective-permute-start(bf16[64,1024]{1,0:T(8,128)(2,1)S(1)} %add_add_fusion), channel_id=1, source_target_pairs={{4,0},{12,8},{20,16},{28,24},{36,32},{44,40},{52,48},{60,56},{68,6... | collective-permute-start | bytes 393224 | tf_op jit(solution)/shard_map/ppermute | solution.py:351
  68.7 9.7 %collective-permute-start.16 = (f32[24,128]{1,0:T(8,128)S(1)}, f32[24,128]{1,0:T(8,128)S(1)}, u32[]{:S(2)}, u32[]{:S(2)}) collective-permute-start(f32[24,128]{1,0:T(8,128)S(1)} %observe.1.stats_ref), channel_id=1, source_target_pairs={{0,128},{128,0},{1,129},{129,1},{2,130},{130,2},{3,131},{131,3},{4... | collective-permute-start | bytes 36872 | tf_op jit(solution)/shard_map/ppermute | solution.py:384
  68.8 9.6 %collective-permute-start.6 = (s32[8,8]{1,0:T(8,128)S(1)}, s32[8,8]{1,0:T(8,128)S(1)}, u32[]{:S(2)}, u32[]{:S(2)}) collective-permute-start(s32[8,8]{1,0:T(8,128)S(1)} %pad_add_fusion.meta_ref), channel_id=1, source_target_pairs={{0,128},{128,0},{1,129},{129,1},{2,130},{130,2},{3,131},{131,3},{4... | collective-permute-start | bytes 776 | tf_op jit(solution)/shard_map/ppermute | solution.py:375
  98.7 1.4 %copy-start = (bf16[32,288,128]{2,1,0:T(8,128)(2,1)}, bf16[32,288,128]{2,1,0:T(8,128)(2,1)S(1)}, u32[]{:S(2)}) copy-start(bf16[32,288,128]{2,1,0:T(8,128)(2,1)S(1)} %pack_far.1) | copy-start | bytes 7077892
  100.1 1.3 copy-start.1
  101.4 37.2 %all-to-all-start = ((bf16[32,288,128]{2,1,0:T(8,128)(2,1)}), bf16[32,288,128]{2,1,0:T(8,128)(2,1)S(1)}, u32[]{:S(2)}, u32[]{:S(2)}) async-start(bf16[32,288,128]{2,1,0:T(8,128)(2,1)} %copy-done), calls=%async_computation | async-start | bytes 4718592 | tf_op jit(solution)/shard_map/all_to_all | solution.py:369
  105.5 1.2 copy-start.8
  106.7 0.9 copy-start.10
  107.7 0.9 copy-start.12
  108.6 0.9 copy-start.14
  109.6 0.9 copy-start.16
  110.5 19.1 %copy-start.2 = (bf16[32,256,128]{2,1,0:T(8,128)(2,1)S(1)}, bf16[32,256,128]{2,1,0:T(8,128)(2,1)}, u32[]{:S(2)}) copy-start(bf16[32,256,128]{2,1,0:T(8,128)(2,1)} %copy-done.1) | copy-start | bytes 6291460

commit v4 on v3

v4 whole, which is shorter than its diff:
```python
import functools
import math

import jax
import jax.numpy as jnp
from jax import lax
from jax.experimental import pallas as pl
from jax.experimental.pallas import tpu as pltpu
from jax.sharding import Mesh, PartitionSpec as P

HD = 128
CYCLE = 4
OBS = 64
BLOCK = 128
SHARD = 512
HEADS = 8
KVS = 2
GROUP = 4
KEEP = 4
BLKS = 4
NSEQ = 64
HALF = 32
SEQ = ("zh", "y", "x", "c")
PLANE = ("y", "x", "c")
LEAD = 4 * BLOCK
SHIFT = 2
LOG2E = 1.4426950408889634
COEF = LOG2E / math.sqrt(HD)
SCALE = 1.0 / math.sqrt(HD)
BIG = 1e30
NT = (((1,), (1,)), ((), ()))
NN = (((1,), (0,)), ((), ()))


def f32dot(a, b, dims):
    return lax.dot_general(a, b, dims, preferred_element_type=jnp.float32)


def attend_kernel(pos_ref, q_ref, *refs):
    o_ref = refs[-1]
    pos = pos_ref[0]
    p0, p1, p2, p3, held, ea, eb = [refs[2 * i : 2 * i + 2] for i in range(7)]
    first = pos - NSEQ // 2
    keys, values = [p0[0][...]], [p0[1][...]]
    for side, out in ((0, keys), (1, values)):
        near = [p[side][...] for p in (p1, p2, p3)]
        other, swapped, edge = [e[side][...] for e in (held, ea, eb)]
        out.append(jnp.where(first == 0, swapped, near[0]))
        out.append(jnp.where((first == 0) | (first == 1), other, near[1]))
        third = jnp.where((first == 0) | (first == 2), edge, near[2])
        out.append(jnp.where(first == 1, swapped, third))
    half = SHARD // 2
    ones = jnp.ones((SHARD, HD), jnp.bfloat16)
    vext = [jnp.concatenate([v, ones], axis=1) for v in values]
    row = lax.broadcasted_iota(jnp.int32, (half, half), 0)
    col = lax.broadcasted_iota(jnp.int32, (half, half), 1)
    causal = col <= row
    for tile in range(2):
        q = q_ref[tile * half : (tile + 1) * half, :]
        diag = f32dot(q, keys[0][tile * half : (tile + 1) * half, :], NT)
        diag = jnp.where(causal, diag, -BIG)
        peak = jnp.max(diag, axis=1, keepdims=True)
        if tile == 1:
            own = f32dot(q, keys[0][:half, :], NT)
            peak = jnp.maximum(peak, jnp.max(own, axis=1, keepdims=True))
        past = [f32dot(q, k, NT) for k in keys[1:]]
        for distance, score in enumerate(past, 1):
            here = jnp.max(score, axis=1, keepdims=True)
            peak = jnp.where(pos >= distance, jnp.maximum(peak, here), peak)
        shift = peak * COEF
        weight = jnp.exp2(diag * COEF - shift).astype(jnp.bfloat16)
        acc = f32dot(weight, vext[0][tile * half : (tile + 1) * half], NN)
        if tile == 1:
            weight = jnp.exp2(own * COEF - shift).astype(jnp.bfloat16)
            acc += f32dot(weight, vext[0][:half], NN)
        for distance, score in enumerate(past, 1):
            lift = jnp.where(pos >= distance, shift, BIG)
            weight = jnp.exp2(score * COEF - lift).astype(jnp.bfloat16)
            acc += f32dot(weight, vext[distance], NN)
        mixed = acc[:, :HD] / acc[:, HD:]
        o_ref[tile * half : (tile + 1) * half, :] = mixed.astype(jnp.bfloat16)


def attend(position, queries, pairs):
    key_spec = pl.BlockSpec((SHARD, HD), lambda h: (0, h // GROUP))
    value_spec = pl.BlockSpec((SHARD, HD), lambda h: (1, h // GROUP))
    return pl.pallas_call(
        attend_kernel,
        grid=(HEADS,),
        out_shape=jax.ShapeDtypeStruct((SHARD, HEADS * HD), jnp.bfloat16),
        in_specs=[
            pl.BlockSpec(memory_space=pltpu.SMEM),
            pl.BlockSpec((SHARD, HD), lambda h: (0, h)),
        ]
        + [key_spec, value_spec] * len(pairs),
        out_specs=pl.BlockSpec((SHARD, HD), lambda h: (0, h)),
        compiler_params=pltpu.CompilerParams(vmem_limit_bytes=32 * 1024 * 1024),
        cost_estimate=pl.CostEstimate(
            flops=HEADS * SHARD * SHARD * 4 * HD * 4,
            bytes_accessed=4 * 1024 * 1024,
            transcendentals=HEADS * SHARD * SHARD * 4,
        ),
        name="attend",
    )(position, queries, *[pair for pair in pairs for _ in range(2)])


SMEM = pl.BlockSpec(memory_space=pltpu.SMEM)
VMEM = pl.BlockSpec(memory_space=pltpu.VMEM)
ANY = pl.BlockSpec(memory_space=pl.ANY)


def join_kernel(k_ref, v_ref, pair_ref, sems):
    copies = (
        pltpu.make_async_copy(k_ref, pair_ref.at[:SHARD], sems.at[0]),
        pltpu.make_async_copy(v_ref, pair_ref.at[SHARD:], sems.at[1]),
    )
    for copy in copies:
        copy.start()
    for copy in copies:
        copy.wait()


def join(keys, values):
    return pl.pallas_call(
        join_kernel,
        out_shape=jax.ShapeDtypeStruct((2 * SHARD, KVS * HD), jnp.bfloat16),
        in_specs=[ANY, ANY],
        out_specs=VMEM,
        scratch_shapes=[pltpu.SemaphoreType.DMA((2,))],
        cost_estimate=pl.CostEstimate(flops=0, bytes_accessed=1024 * 1024, transcendentals=0),
        name="join",
    )(keys, values)


def seats(entry, put):
    for head in range(HEADS):
        for c in range(KEEP):
            seat, unit = entry(c, head)
            pl.when((seat >= 0) & (seat < HALF))(functools.partial(put, seat, unit, head))


def block_rows(unit, start):
    return pl.ds(pl.multiple_of(unit * BLOCK + start, BLOCK), BLOCK)


def terms(value, count):
    parts = []
    for _ in range(count):
        part = value.astype(jnp.bfloat16)
        parts.append(part)
        value = value - part.astype(jnp.float32)
    return parts


def pack_kernel(base_ref, meta_ref, list_ref, pair_ref, other_ref, mail_ref, got_ref, *refs):
    out_ref, stats_ref, tile_ref = refs[-3:]
    last = base_ref[0] > 0
    mine = jnp.where(last, mail_ref[0:24], got_ref[24:48])
    other = jnp.where(last, mail_ref[24:48], got_ref[0:24])
    stats_ref[...] = mine
    level, other_level = mine[0:4], other[0:4]
    top = jnp.maximum(level, other_level)
    both = top + jnp.log(jnp.exp(level - top) + jnp.exp(other_level - top))
    part, other_part = jnp.exp(level - both), jnp.exp(other_level - both)
    blank = jnp.zeros((4, 128), jnp.float32)
    as_rows = lambda pieces: jnp.concatenate([p.astype(jnp.float32) for p in pieces], axis=0)
    for b in range(BLKS):
        rows = slice(4 + 4 * b, 8 + 4 * b)
        tile_ref[0, b] = as_rows(terms(mine[rows] * part, 2) + [blank, blank])
        tile_ref[1, b] = as_rows([blank, blank] + terms(other[rows] * other_part, 2))
    out_ref[:, :LEAD, :] = jnp.zeros((HALF, LEAD, HD), jnp.bfloat16)
    lead = as_rows(terms(both, 3) + [blank]).astype(jnp.bfloat16)
    out_ref[:, LEAD : LEAD + 16, :] = jnp.broadcast_to(lead[None], (HALF, 16, HD))
    out_ref[:, LEAD + 16 :, :] = jnp.zeros((HALF, 16, HD), jnp.bfloat16)
    row = lax.broadcasted_iota(jnp.int32, (16, 128), 0)
    lane = lax.broadcasted_iota(jnp.int32, (16, 128), 1)
    which = lax.rem(row, 4) * 2 + lane // OBS
    tail = slice(LEAD + 16, LEAD + 32)

    def my_entry(c, head):
        return meta_ref[c, head] - base_ref[0], meta_ref[KEEP + c, head]

    def other_entry(c, head):
        seat = list_ref[c, head].astype(jnp.int32) - base_ref[0]
        return seat, list_ref[KEEP + c, head].astype(jnp.int32)

    def add_score(source, seat, unit, head):
        picked = jnp.where(which == head, tile_ref[source, unit], 0.0).astype(jnp.bfloat16)
        out_ref[seat, tail] = out_ref[seat, tail] + picked

    def put(source, held_ref, seat, unit, head):
        cols = slice((head // GROUP) * HD, (head // GROUP + 1) * HD)
        start = 2 * BLOCK * source
        out_ref[seat, start : start + BLOCK] = held_ref[block_rows(unit, 0), cols]
        out_ref[seat, start + BLOCK : start + 2 * BLOCK] = held_ref[block_rows(unit, SHARD), cols]
        add_score(source, seat, unit, head)

    seats(my_entry, functools.partial(put, 0, pair_ref))
    seats(other_entry, functools.partial(put, 1, other_ref))


def pack(base, meta, pair, other_pair, mail, got, after):
    return pl.pallas_call(
        pack_kernel,
        out_shape=(
            jax.ShapeDtypeStruct((HALF, LEAD + 32, HD), jnp.bfloat16),
            jax.ShapeDtypeStruct((24, 128), jnp.float32),
        ),
        in_specs=[SMEM, SMEM, SMEM, VMEM, VMEM, VMEM, VMEM] + [ANY] * len(after),
        out_specs=(VMEM, VMEM),
        scratch_shapes=[pltpu.VMEM((2, BLKS, 16, 128), jnp.float32)],
        compiler_params=pltpu.CompilerParams(vmem_limit_bytes=16 * 1024 * 1024),
        cost_estimate=pl.CostEstimate(flops=0, bytes_accessed=3 * 1024 * 1024, transcendentals=0),
        name="pack",
    )(base, meta, got[48:56], pair, other_pair, mail, got, *after)


def score_keys(pos, q_ref, k_ref, mail_ref, start):
    rows = [[] for _ in range(1 + BLKS)]
    for kv in range(KVS):
        heads = [
            q_ref[:, (kv * GROUP + g) * HD : (kv * GROUP + g + 1) * HD] for g in range(GROUP)
        ]
        stacked = jnp.concatenate(heads, axis=0)
        score = f32dot(k_ref[:SHARD, kv * HD : (kv + 1) * HD], stacked, NT) * SCALE
        key = lax.broadcasted_iota(jnp.int32, score.shape, 0)
        lane = lax.broadcasted_iota(jnp.int32, score.shape, 1)
        limit = (NSEQ - pos) * SHARD - OBS + lax.rem(lane, OBS)
        score = jnp.where(key <= limit, score, -jnp.inf)
        peak = jnp.max(score, axis=0, keepdims=True)
        expo = jnp.exp(score - peak)
        sums = [
            jnp.sum(expo[b * BLOCK : (b + 1) * BLOCK], axis=0, keepdims=True) for b in range(BLKS)
        ]
        mass = (sums[0] + sums[1]) + (sums[2] + sums[3])
        level = peak + jnp.log(mass)
        for side in range(2):
            cut = slice(side * 128, (side + 1) * 128)
            rows[0].append(level[:, cut])
            for b in range(BLKS):
                rows[1 + b].append((sums[b] / mass)[:, cut])
    for place_, pieces in enumerate(rows):
        at = start + 4 * place_
        mail_ref[at : at + 4] = jnp.concatenate(pieces, axis=0)
    mail_ref[start + 20 : start + 24] = jnp.zeros((4, 128), jnp.float32)


def observe_kernel(pos_ref, q_ref, k_ref, other_ref, meta_ref, *refs):
    mail_ref = refs[-1]
    pos = pos_ref[0]
    score_keys(pos, q_ref, k_ref, mail_ref, 0)
    score_keys(0, q_ref, other_ref, mail_ref, 24)
    mail_ref[48:56] = meta_ref[...].astype(jnp.float32)


def observe(position, observers, keys, other_keys, meta, after):
    return pl.pallas_call(
        observe_kernel,
        out_shape=jax.ShapeDtypeStruct((56, 128), jnp.float32),
        in_specs=[SMEM, VMEM, VMEM, VMEM, VMEM] + [ANY] * len(after),
        out_specs=VMEM,
        compiler_params=pltpu.CompilerParams(vmem_limit_bytes=16 * 1024 * 1024),
        name="observe",
    )(position, observers, keys, other_keys, meta, *after)


def sends(half, buf_ref, key_ref, value_ref, sems):
    own, other = half * HALF, (1 - half) * HALF
    most = HALF - SHIFT
    pieces = (
        (0, 0, own, HALF),
        (1, SHIFT * half, other + SHIFT * (1 - half), most),
        (1, most * (1 - half), other + most * half, SHIFT),
    )
    copies = []
    for number, (source, start, row, count) in enumerate(pieces):
        for side, out_ref in enumerate((key_ref, value_ref)):
            at_ = (2 * source + side) * BLOCK
            copies.append(
                pltpu.make_async_copy(
                    buf_ref.at[pl.ds(start, count), at_ : at_ + BLOCK],
                    out_ref.at[pl.ds(row, count)],
                    sems.at[2 * number + side],
                )
            )
    return copies


def last_kernel(
    half_ref, got_ref, stats_ref, key_ref, value_ref, recv_ref, block_ref, sems
):
    copies = sends(half_ref[0], got_ref, key_ref, value_ref, sems)
    for copy in copies:
        copy.start()
    factor = BLKS * NSEQ / OBS
    lead = got_ref[:, LEAD : LEAD + 16].astype(jnp.float32)
    level = (lead[:, 8:12] + lead[:, 4:8]) + lead[:, 0:4]
    top = jnp.max(level, axis=0)
    total = top + jnp.log(jnp.sum(jnp.exp(level - top[None]), axis=0))
    share = jnp.exp(level - total[None])
    tail = got_ref[:, LEAD + 16 :].astype(jnp.float32)
    own = jnp.sum((tail[:, 4:8] + tail[:, 0:4]) * share, axis=1)
    other = jnp.sum((tail[:, 12:16] + tail[:, 8:12]) * share, axis=1)
    low = half_ref[0] == 0
    other = jnp.where(
        low,
        jnp.concatenate([other[HALF - SHIFT :], other[: HALF - SHIFT]], axis=0),
        jnp.concatenate([other[SHIFT:], other[:SHIFT]], axis=0),
    )
    rows = jnp.concatenate(
        [jnp.where(low, own, other), jnp.where(low, other, own)], axis=0
    )
    lined = lax.dot_general(
        jnp.ones((8, 128), jnp.float32),
        rows,
        NT,
        precision=lax.Precision.HIGHEST,
        preferred_element_type=jnp.float32,
    )
    recv_ref[...] = (lined[0:1] * factor).astype(jnp.bfloat16)
    mine = jnp.exp(stats_ref[0:4] - total)
    row = lax.broadcasted_iota(jnp.int32, (HEADS, 4 * 128), 0)
    lane = lax.broadcasted_iota(jnp.int32, (HEADS, 4 * 128), 1)
    chosen = (lane // OBS == row).astype(jnp.float32)
    parts = []
    for b in range(BLKS):
        part = stats_ref[4 + 4 * b : 8 + 4 * b] * mine
        parts.append(jnp.concatenate([part[r : r + 1] for r in range(4)], axis=1))
    table = jnp.concatenate(parts + parts, axis=0)
    scores = lax.dot_general(
        table,
        chosen,
        NT,
        precision=lax.Precision.HIGHEST,
        preferred_element_type=jnp.float32,
    )
    block_ref[...] = scores[:BLKS] * factor
    for copy in copies:
        copy.wait()


def place(half, got, stats):
    shape = jax.ShapeDtypeStruct((NSEQ, BLOCK, HD), jnp.bfloat16)
    return pl.pallas_call(
        last_kernel,
        out_shape=(
            shape,
            shape,
            jax.ShapeDtypeStruct((1, NSEQ), jnp.bfloat16),
            jax.ShapeDtypeStruct((BLKS, HEADS), jnp.float32),
        ),
        in_specs=[SMEM, VMEM, VMEM],
        out_specs=(ANY, ANY, VMEM, VMEM),
        scratch_shapes=[pltpu.SemaphoreType.DMA((6,))],
        compiler_params=pltpu.CompilerParams(vmem_limit_bytes=16 * 1024 * 1024),
        cost_estimate=pl.CostEstimate(flops=0, bytes_accessed=4 * 1024 * 1024, transcendentals=0),
        name="place",
    )(half, got, stats)


def at(zh, y, x, c):
    return ((zh * 4 + y) * 4 + x) * 2 + c


def spread(tail):
    me = lax.axis_index(SEQ)
    held = jnp.where(me == NSEQ - 1, tail, jnp.zeros_like(tail))
    four = range(4)
    steps = (
        [[(at(1, 3, 3, 1), at(1, y, 3, 1))] for y in range(3)],
        [[(at(1, y, 3, 1), at(1, y, x, 1)) for y in four] for x in range(3)],
        [[(at(1, y, x, 1), at(1, y, x, 0)) for y in four for x in four]],
    )
    levels = []
    for step in steps:
        came = [lax.ppermute(held, SEQ, pairs) for pairs in step]
        for part in came:
            held = held + part
        levels.append(held)
    return levels


def shards(queries, keys, values, kept_index, kept_count, owner):
    position = lax.axis_index(SEQ)
    zh = lax.axis_index("zh")
    pos = position.reshape(1).astype(jnp.int32)
    near_half = zh.reshape(1).astype(jnp.int32)
    base = near_half * HALF
    slot_ids = jnp.arange(KEEP, dtype=jnp.int32)[:, None]
    owners = jnp.transpose(owner, (0, 2, 1))[0]
    picks = jnp.transpose(kept_index, (0, 2, 1))[0]
    meta = jnp.concatenate([jnp.where(slot_ids < kept_count, owners, -1), picks], axis=0)
    meta = jnp.pad(meta, ((0, 0), (0, 128 - HEADS)))

    def exchange(packed):
        return lax.all_to_all(packed, PLANE, split_axis=0, concat_axis=0, tiled=True)

    def hop(pair, by):
        steps = [(i, i + by) for i in range(NSEQ) if i // HALF == (i + by) // HALF]
        return lax.ppermute(pair, SEQ, steps)

    swap = []
    for i in range(HALF):
        j = HALF + (i + SHIFT) % HALF
        swap += [(i, j), (j, i)]
    levels = spread(queries[SHARD - OBS :])
    pair = join(keys, values)
    other_pair = lax.ppermute(pair, SEQ, swap)
    one, two = hop(pair, 1), hop(pair, 2)
    three = hop(two, 1)
    edge_a = lax.ppermute(other_pair, SEQ, [(32, 33), (33, 32)])
    edge_b = lax.ppermute(other_pair, SEQ, [(33, 34), (63, 32)])

    mail = observe(pos, levels[-1], pair, other_pair, meta, (one, two))
    got = lax.ppermute(mail, SEQ, swap)
    packed, stats = pack(base, meta, pair, other_pair, mail, got, (three, edge_a, edge_b))
    arrived = exchange(packed)
    attended = attend(pos, queries, [pair, one, two, three, other_pair, edge_a, edge_b])
    recv_keys, recv_values, recv_scores, scores_here = place(near_half, arrived, stats)
    return (
        attended,
        scores_here.T,
        recv_keys.reshape(1, 1, NSEQ, 1, BLOCK, HD),
        recv_values.reshape(1, 1, NSEQ, 1, BLOCK, HD),
        recv_scores.reshape(1, 1, NSEQ, 1),
    )


def solution(mesh):
    fine = Mesh(mesh.devices.reshape(2, 4, 4, 2, 4), SEQ + ("kv",))
    placed = (
        P(SEQ, "kv"),
        P(SEQ, "kv"),
        P(SEQ, "kv"),
        P(SEQ, "kv", None),
        P(SEQ, "kv"),
        P(SEQ, "kv", None),
    )
    return jax.shard_map(
        shards,
        mesh=fine,
        in_specs=placed,
        out_specs=(
            P(SEQ, "kv"),
            P("kv", SEQ),
            P(SEQ, "kv", None, None, None, None),
            P(SEQ, "kv", None, None, None, None),
            P(SEQ, "kv", None, None),
        ),
        check_vma=False,
    )
```

time: 142 us -> 130 us (0.915)
  starting transfers between devices: 37.7 us -> 25.4 us
  local copies, waits for them, and re-layouts: 11 us -> 5.4 us
  waiting for transfers between devices: 60.8 us -> 65.1 us
  Pallas kernels: 26.8 us -> 29.5 us
    all_to_all x2 -> x1, waiting for transfers between devices: 7.58 us -> 34.7 us  [exchange(): lax.all_to_all(packed, PLANE, split_axis=0, concat_axis=0, tiled=True)]
    ppermute x9 -> x7, waiting for transfers between devices: 51.2 us -> 29.8 us  [the longest x1 18.6 us: shards(): other_pair = lax.ppermute(pair, SEQ, swap)]
    all_to_all x2 -> x1, starting transfers between devices: 11.5 us -> 4.85 us  [exchange(): lax.all_to_all(packed, PLANE, split_axis=0, concat_axis=0, tiled=True)]
    unnamed x34 -> x12, local copies, waits for them, and re-layouts: 11 us -> 5.39 us
    ppermute x9 -> x7, starting transfers between devices: 20.3 us -> 15.2 us  [the longest x3 5.86 us: hop(): return lax.ppermute(pair, SEQ, steps)]
    pallas_call x5 -> x4, Pallas kernels: 7.63 us -> 9.76 us  [the longest x1 4.88 us: place(): pl.pallas_call(last_kernel, out_shape=(shape, shape, jax.ShapeDtypeStruct...]
    ppermute x8 -> x7, starting transfers between devices: 5.96 us -> 5.3 us  [spread(): came = [lax.ppermute(held, SEQ, pairs) for pairs in step]]
  transfers between devices with their start and end apart: 19 -> 15, of which waited for: 9 -> 4; matrix products, arithmetic and copies ran while one was open for 1% -> 3% of each run, Pallas kernels for 16% -> 16%
where the time goes in v4:
time: 130 us
  waiting for transfers between devices  65.1 us (50%)
  Pallas kernels  29.5 us (23%)
  starting transfers between devices  25.4 us (20%)
  local copies, waits for them, and re-layouts  5.4 us (4%)
  other arithmetic  3.32 us (3%)
    all_to_all x1, waiting for transfers between devices, exchange(): lax.all_to_all(packed, PLANE, split_axis=0, concat_axis=0, tiled=True)  34.7 us
    pallas_call x1, Pallas kernels, attend(): pl.pallas_call(attend_kernel, grid=(HEADS,), out_shape=jax.ShapeDtypeStru...  19.8 us
    ppermute x1, waiting for transfers between devices, shards(): other_pair = lax.ppermute(pair, SEQ, swap)  18.6 us
    ppermute x1, waiting for transfers between devices, shards(): got = lax.ppermute(mail, SEQ, swap)  11.2 us
    ppermute x3, starting transfers between devices, hop(): return lax.ppermute(pair, SEQ, steps)  5.86 us
    unnamed x12, local copies, waits for them, and re-layouts  5.39 us
    ppermute x7, starting transfers between devices, spread(): came = [lax.ppermute(held, SEQ, pairs) for pairs in step]  5.3 us
    ppermute x1, starting transfers between devices, shards(): other_pair = lax.ppermute(pair, SEQ, swap)  5.27 us
  transfers between devices with their start and end apart: 15, of which 4 were waited for; matrix products, arithmetic and copies ran while one was open for 3% of the time, Pallas kernels for 16%

profile of v4, /device:TPU:192, one launch (start us, length us, event | category | flops | bytes accessed | tf_op | source)
XLA Modules:
  0.0 129.6 jit_solution(18142084928847589358)
XLA Ops:
  0.6 1.8 %join.1.refs_0_.refs_1_.k_ref.pair_ref = bf16[1024,256]{1,0:T(8,128)(2,1)} custom-call(bf16[512,256]{1,0:T(8,128)(2,1)} %k_ref.1, bf16[512,256]{1,0:T(8,128)(2,1)} %v_ref.1), custom_call_target="tpu_custom_call" | custom-call | bytes 1048576 | tf_op jit(solution)/shard_map/join/pallas_call | solution.py:124
  2.5 0.0 copy-start.1
  2.5 5.3 %collective-permute-start.3 = (bf16[1024,256]{1,0:T(8,128)(2,1)}, bf16[1024,256]{1,0:T(8,128)(2,1)S(1)}, u32[]{:S(2)}, u32[]{:S(2)}) collective-permute-start(bf16[1024,256]{1,0:T(8,128)(2,1)} %join.1.refs_0_.refs_1_.k_ref.pair_ref), channel_id=1, source_target_pairs={{0,136},{136,0},{4,140},{140,4},{8,144},{144,8},{12,148},{148,12},... | collective-permute-start | bytes 1572872 | tf_op jit(solution)/shard_map/ppermute | solution.py:408
  7.8 1.3 %collective-permute-start.1 = (bf16[1024,256]{1,0:T(8,128)(2,1)}, bf16[1024,256]{1,0:T(8,128)(2,1)S(1)}, u32[]{:S(2)}, u32[]{:S(2)}) collective-permute-start(bf16[1024,256]{1,0:T(8,128)(2,1)} %join.1.refs_0_.refs_1_.k_ref.pair_ref), channel_id=1, source_target_pairs={{0,8},{4,12},{8,16},{12,20},{16,24},{20,28},{24,32},{28,36},{32,40... | collective-permute-start | bytes 1572872 | tf_op jit(solution)/shard_map/ppermute | solution.py:400
  9.1 0.9 slice_select_fusion
  10.0 0.7 collective-permute-start.7
  10.7 0.7 collective-permute-start.8
  11.4 0.7 collective-permute-start.6
  12.1 0.0 collective-permute-done.7
  12.1 0.0 collective-permute-done.8
  12.1 0.0 collective-permute-done.6
  12.1 1.0 add_add_fusion.1
  13.0 0.7 collective-permute-start.11
  13.7 0.7 collective-permute-start.10
  14.4 0.7 collective-permute-start.9
  15.1 0.0 collective-permute-done.11
  15.1 2.1 %collective-permute-start = (bf16[1024,256]{1,0:T(8,128)(2,1)}, bf16[1024,256]{1,0:T(8,128)(2,1)S(1)}, u32[]{:S(2)}, u32[]{:S(2)}) collective-permute-start(bf16[1024,256]{1,0:T(8,128)(2,1)} %join.1.refs_0_.refs_1_.k_ref.pair_ref), channel_id=1, source_target_pairs={{0,4},{4,8},{8,12},{12,16},{16,20},{20,24},{24,28},{28,32},{32,36}... | collective-permute-start | bytes 1572872 | tf_op jit(solution)/shard_map/ppermute | solution.py:400
  17.2 18.6 %collective-permute-done.3.refs_8_.refs_9_.other_ref = bf16[1024,256]{1,0:T(8,128)(2,1)S(1)} collective-permute-done((bf16[1024,256]{1,0:T(8,128)(2,1)}, bf16[1024,256]{1,0:T(8,128)(2,1)S(1)}, u32[]{:S(2)}, u32[]{:S(2)}) %collective-permute-start.3) | collective-permute-done | bytes 524320 | tf_op jit(solution)/shard_map/ppermute | solution.py:408
  35.8 1.3 collective-permute-start.5
  37.1 0.0 collective-permute-done.10
  37.1 1.9 %collective-permute-start.4 = (bf16[1024,256]{1,0:T(8,128)(2,1)S(1)}, bf16[1024,256]{1,0:T(8,128)(2,1)S(1)}, u32[]{:S(2)}, u32[]{:S(2)}) collective-permute-start(bf16[1024,256]{1,0:T(8,128)(2,1)S(1)} %collective-permute-done.3.refs_8_.refs_9_.other_ref), channel_id=1, source_target_pairs={{128,132},{132,128},{129,133},{133,129},{130,134},{134,130},{131,1... | collective-permute-start | bytes 1572872 | tf_op jit(solution)/shard_map/ppermute | solution.py:411
  39.0 0.0 collective-permute-done.1.refs_4_.refs_5_.refs_1_
  39.0 2.4 %collective-permute-start.2 = (bf16[1024,256]{1,0:T(8,128)(2,1)S(1)}, bf16[1024,256]{1,0:T(8,128)(2,1)S(1)}, u32[]{:S(2)}, u32[]{:S(2)}) collective-permute-start(bf16[1024,256]{1,0:T(8,128)(2,1)S(1)} %collective-permute-done.1.refs_4_.refs_5_.refs_1_), channel_id=1, source_target_pairs={{0,4},{4,8},{8,12},{12,16},{16,20},{20,24},{24,28},{28,32},{32,36}... | collective-permute-start | bytes 1572872 | tf_op jit(solution)/shard_map/ppermute | solution.py:400
  41.5 0.0 collective-permute-done.9
  41.5 1.3 collective-permute-start.12
  42.8 0.7 bitcast_select_fusion
  43.5 0.7 pad_add_fusion
  44.2 0.6 collective-permute-done.12
  44.8 0.0 collective-permute-done.refs_2_.refs_3_.refs_0_
  44.8 0.0 copy-start
  44.8 1.0 copy-done
  45.9 0.8 observe.1.mail_ref
  46.7 0.9 collective-permute-start.13
  47.6 11.2 %collective-permute-done.13.got_ref = f32[56,128]{1,0:T(8,128)S(1)} collective-permute-done((f32[56,128]{1,0:T(8,128)S(1)}, f32[56,128]{1,0:T(8,128)S(1)}, u32[]{:S(2)}, u32[]{:S(2)}) %collective-permute-start.13) | collective-permute-done | bytes 28704 | tf_op jit(solution)/shard_map/ppermute | solution.py:415
  58.8 0.0 collective-permute-done.5.refs_12_.refs_13_.refs_2_
  58.8 0.0 collective-permute-done.4.refs_10_.refs_11_.refs_1_
  58.8 0.0 collective-permute-done.2.refs_6_.refs_7_.refs_0_
  58.8 0.0 copy-start.3
  58.8 2.2 %pack.1 = (bf16[32,544,128]{2,1,0:T(8,128)(2,1)S(1)}, f32[24,128]{1,0:T(8,128)S(1)}) custom-call(s32[1]{0:T(128)S(6)} %mul.18.base_ref, s32[8,128]{1,0:T(8,128)S(1)} %pad.4.meta_ref, f32[8,128]{1,0:T(8,128)S(1)} %slice.8.list_ref, bf16[1024,256]{1,0:T(8,128)(2,1)S(1)} %copy-done.1, bf16[1024,256]{1,0:T(8,128)(2,1)S(1)} %collective-permute-done.3.refs_8_.refs_9_.other_ref, ...), custom_call_target="tpu_custom_call" | custom-call | bytes 3145728 | tf_op jit(solution)/shard_map/pack/pallas_call | solution.py:203
  61.1 0.0 copy-done.3
  61.1 2.1 %copy-done.2 = bf16[32,544,128]{2,1,0:T(8,128)(2,1)} copy-done((bf16[32,544,128]{2,1,0:T(8,128)(2,1)}, bf16[32,544,128]{2,1,0:T(8,128)(2,1)S(1)}, u32[]{:S(2)}) %copy-start.2) | copy-done | bytes 4456472
  63.2 4.9 %all-to-all-start = ((bf16[32,544,128]{2,1,0:T(8,128)(2,1)}), bf16[32,544,128]{2,1,0:T(8,128)(2,1)}, u32[]{:S(2)}, u32[]{:S(2)}) async-start(bf16[32,544,128]{2,1,0:T(8,128)(2,1)} %copy-done.2), calls=%async_computation | async-start | bytes 8912896 | tf_op jit(solution)/shard_map/all_to_all | solution.py:396
  68.0 0.0 copy-start.4
  68.0 1.0 copy-done.4
  69.1 1.2 copy-done.5
  70.3 19.8 %attend.1 = bf16[512,1024]{1,0:T(8,128)(2,1)} custom-call(s32[1]{0:T(128)} %bitcast.pos_ref, bf16[512,1024]{1,0:T(8,128)(2,1)S(1)} %copy-done.5, bf16[1024,256]{1,0:T(8,128)(2,1)S(1)} %copy-done.1, bf16[1024,256]{1,0:T(8,128)(2,1)S(1)} %copy-done.1, bf16[1024,256]{1,0:T(8,128)(2,1)S(1)} %collective-permute-done.refs_2_.refs_3_.refs_0_, ...), custom_call_target="tpu_custom_call" | custom-call | flops 4294967296 | bytes 4194304 | tf_op jit(solution)/shard_map/attend/pallas_call | solution.py:87
  90.1 34.7 %all-to-all-done.got_ref = bf16[32,544,128]{2,1,0:T(8,128)(2,1)} async-done(((bf16[32,544,128]{2,1,0:T(8,128)(2,1)}), bf16[32,544,128]{2,1,0:T(8,128)(2,1)}, u32[]{:S(2)}, u32[]{:S(2)}) %all-to-all-start) | async-done | bytes 4456480 | tf_op jit(solution)/shard_map/all_to_all | solution.py:396
  124.7 4.9 %place.1 = (bf16[64,128,128]{2,1,0:T(8,128)(2,1)}, bf16[64,128,128]{2,1,0:T(8,128)(2,1)}, bf16[1,64]{1,0:T(2,128)(2,1)}, f32[4,8]{1,0:T(4,128)}) custom-call(s32[1]{0:T(128)} %bitcast.1.half_ref, bf16[32,544,128]{2,1,0:T(8,128)(2,1)} %all-to-all-done.got_ref, f32[24,128]{1,0:T(8,128)S(1)} %get-tuple-element.12.stats_ref), custom_call_target="tpu_custom_call" | custom-call | bytes 4194304 | tf_op jit(solution)/shard_map/place/pallas_call | solution.py:344
  (7 shorter events, 0.1 us)
Async XLA Ops:
  2.5 56.3 %copy-start.1 = (bf16[1024,256]{1,0:T(8,128)(2,1)S(1)}, bf16[1024,256]{1,0:T(8,128)(2,1)}, u32[]{:S(2)}) copy-start(bf16[1024,256]{1,0:T(8,128)(2,1)} %join.1.refs_0_.refs_1_.k_ref.pair_ref) | copy-start | bytes 1572868
  2.5 33.3 %collective-permute-start.3 = (bf16[1024,256]{1,0:T(8,128)(2,1)}, bf16[1024,256]{1,0:T(8,128)(2,1)S(1)}, u32[]{:S(2)}, u32[]{:S(2)}) collective-permute-start(bf16[1024,256]{1,0:T(8,128)(2,1)} %join.1.refs_0_.refs_1_.k_ref.pair_ref), channel_id=1, source_target_pairs={{0,136},{136,0},{4,140},{140,4},{8,144},{144,8},{12,148},{148,12},... | collective-permute-start | bytes 1572872 | tf_op jit(solution)/shard_map/ppermute | solution.py:408
  7.8 31.3 %collective-permute-start.1 = (bf16[1024,256]{1,0:T(8,128)(2,1)}, bf16[1024,256]{1,0:T(8,128)(2,1)S(1)}, u32[]{:S(2)}, u32[]{:S(2)}) collective-permute-start(bf16[1024,256]{1,0:T(8,128)(2,1)} %join.1.refs_0_.refs_1_.k_ref.pair_ref), channel_id=1, source_target_pairs={{0,8},{4,12},{8,16},{12,20},{16,24},{20,28},{24,32},{28,36},{32,40... | collective-permute-start | bytes 1572872 | tf_op jit(solution)/shard_map/ppermute | solution.py:400
  10.0 2.0 %collective-permute-start.7 = (bf16[64,1024]{1,0:T(8,128)(2,1)S(1)}, bf16[64,1024]{1,0:T(8,128)(2,1)S(1)}, u32[]{:S(2)}, u32[]{:S(2)}) collective-permute-start(bf16[64,1024]{1,0:T(8,128)(2,1)S(1)} %slice_select_fusion), channel_id=1, source_target_pairs={{252,188},{253,189},{254,190},{255,191}} | collective-permute-start | bytes 393224 | tf_op jit(solution)/shard_map/ppermute | solution.py:376
  10.7 1.4 %collective-permute-start.8 = (bf16[64,1024]{1,0:T(8,128)(2,1)S(1)}, bf16[64,1024]{1,0:T(8,128)(2,1)S(1)}, u32[]{:S(2)}, u32[]{:S(2)}) collective-permute-start(bf16[64,1024]{1,0:T(8,128)(2,1)S(1)} %slice_select_fusion), channel_id=1, source_target_pairs={{252,220},{253,221},{254,222},{255,223}} | collective-permute-start | bytes 393224 | tf_op jit(solution)/shard_map/ppermute | solution.py:376
  11.4 0.7 collective-permute-start.6
  13.0 2.0 %collective-permute-start.11 = (bf16[64,1024]{1,0:T(8,128)(2,1)S(1)}, bf16[64,1024]{1,0:T(8,128)(2,1)S(1)}, u32[]{:S(2)}, u32[]{:S(2)}) collective-permute-start(bf16[64,1024]{1,0:T(8,128)(2,1)S(1)} %add_add_fusion.1), channel_id=1, source_target_pairs={{156,148},{188,180},{220,212},{252,244},{157,149},{189,181},{221,2... | collective-permute-start | bytes 393224 | tf_op jit(solution)/shard_map/ppermute | solution.py:376
  13.7 23.4 %collective-permute-start.10 = (bf16[64,1024]{1,0:T(8,128)(2,1)S(1)}, bf16[64,1024]{1,0:T(8,128)(2,1)S(1)}, u32[]{:S(2)}, u32[]{:S(2)}) collective-permute-start(bf16[64,1024]{1,0:T(8,128)(2,1)S(1)} %add_add_fusion.1), channel_id=1, source_target_pairs={{156,140},{188,172},{220,204},{252,236},{157,141},{189,173},{221,2... | collective-permute-start | bytes 393224 | tf_op jit(solution)/shard_map/ppermute | solution.py:376
  14.4 27.1 %collective-permute-start.9 = (bf16[64,1024]{1,0:T(8,128)(2,1)S(1)}, bf16[64,1024]{1,0:T(8,128)(2,1)S(1)}, u32[]{:S(2)}, u32[]{:S(2)}) collective-permute-start(bf16[64,1024]{1,0:T(8,128)(2,1)S(1)} %add_add_fusion.1), channel_id=1, source_target_pairs={{156,132},{188,164},{220,196},{252,228},{157,133},{189,165},{221,1... | collective-permute-start | bytes 393224 | tf_op jit(solution)/shard_map/ppermute | solution.py:376
  15.1 29.8 %collective-permute-start = (bf16[1024,256]{1,0:T(8,128)(2,1)}, bf16[1024,256]{1,0:T(8,128)(2,1)S(1)}, u32[]{:S(2)}, u32[]{:S(2)}) collective-permute-start(bf16[1024,256]{1,0:T(8,128)(2,1)} %join.1.refs_0_.refs_1_.k_ref.pair_ref), channel_id=1, source_target_pairs={{0,4},{4,8},{8,12},{12,16},{16,20},{20,24},{24,28},{28,32},{32,36}... | collective-permute-start | bytes 1572872 | tf_op jit(solution)/shard_map/ppermute | solution.py:400
  35.8 23.0 %collective-permute-start.5 = (bf16[1024,256]{1,0:T(8,128)(2,1)S(1)}, bf16[1024,256]{1,0:T(8,128)(2,1)S(1)}, u32[]{:S(2)}, u32[]{:S(2)}) collective-permute-start(bf16[1024,256]{1,0:T(8,128)(2,1)S(1)} %collective-permute-done.3.refs_8_.refs_9_.other_ref), channel_id=1, source_target_pairs={{132,136},{252,128},{133,137},{253,129},{134,138},{254,130},{135,1... | collective-permute-start | bytes 1572872 | tf_op jit(solution)/shard_map/ppermute | solution.py:412
  37.1 21.7 %collective-permute-start.4 = (bf16[1024,256]{1,0:T(8,128)(2,1)S(1)}, bf16[1024,256]{1,0:T(8,128)(2,1)S(1)}, u32[]{:S(2)}, u32[]{:S(2)}) collective-permute-start(bf16[1024,256]{1,0:T(8,128)(2,1)S(1)} %collective-permute-done.3.refs_8_.refs_9_.other_ref), channel_id=1, source_target_pairs={{128,132},{132,128},{129,133},{133,129},{130,134},{134,130},{131,1... | collective-permute-start | bytes 1572872 | tf_op jit(solution)/shard_map/ppermute | solution.py:411
  39.0 19.7 %collective-permute-start.2 = (bf16[1024,256]{1,0:T(8,128)(2,1)S(1)}, bf16[1024,256]{1,0:T(8,128)(2,1)S(1)}, u32[]{:S(2)}, u32[]{:S(2)}) collective-permute-start(bf16[1024,256]{1,0:T(8,128)(2,1)S(1)} %collective-permute-done.1.refs_4_.refs_5_.refs_1_), channel_id=1, source_target_pairs={{0,4},{4,8},{8,12},{12,16},{16,20},{20,24},{24,28},{28,32},{32,36}... | collective-permute-start | bytes 1572872 | tf_op jit(solution)/shard_map/ppermute | solution.py:400
  41.5 3.2 %collective-permute-start.12 = (bf16[64,1024]{1,0:T(8,128)(2,1)S(1)}, bf16[64,1024]{1,0:T(8,128)(2,1)S(1)}, u32[]{:S(2)}, u32[]{:S(2)}) collective-permute-start(bf16[64,1024]{1,0:T(8,128)(2,1)S(1)} %add_add_fusion), channel_id=1, source_target_pairs={{132,128},{140,136},{148,144},{156,152},{164,160},{172,168},{180,1... | collective-permute-start | bytes 393224 | tf_op jit(solution)/shard_map/ppermute | solution.py:376
  44.8 1.0 copy-start
  46.7 12.1 %collective-permute-start.13 = (f32[56,128]{1,0:T(8,128)S(1)}, f32[56,128]{1,0:T(8,128)S(1)}, u32[]{:S(2)}, u32[]{:S(2)}) collective-permute-start(f32[56,128]{1,0:T(8,128)S(1)} %observe.1.mail_ref), channel_id=1, source_target_pairs={{0,136},{136,0},{4,140},{140,4},{8,144},{144,8},{12,148},{148,12},... | collective-permute-start | bytes 86024 | tf_op jit(solution)/shard_map/ppermute | solution.py:415
  58.8 2.2 %copy-start.3 = (bf16[1024,256]{1,0:T(8,128)(2,1)}, bf16[1024,256]{1,0:T(8,128)(2,1)S(1)}, u32[]{:S(2)}) copy-start(bf16[1024,256]{1,0:T(8,128)(2,1)S(1)} %collective-permute-done.2.refs_6_.refs_7_.refs_0_) | copy-start | bytes 1572868
  61.1 2.1 %copy-start.2 = (bf16[32,544,128]{2,1,0:T(8,128)(2,1)}, bf16[32,544,128]{2,1,0:T(8,128)(2,1)S(1)}, u32[]{:S(2)}) copy-start(bf16[32,544,128]{2,1,0:T(8,128)(2,1)S(1)} %get-tuple-element.11) | copy-start | bytes 13369348
  63.2 61.6 %all-to-all-start = ((bf16[32,544,128]{2,1,0:T(8,128)(2,1)}), bf16[32,544,128]{2,1,0:T(8,128)(2,1)}, u32[]{:S(2)}, u32[]{:S(2)}) async-start(bf16[32,544,128]{2,1,0:T(8,128)(2,1)} %copy-done.2), calls=%async_computation | async-start | bytes 8912896 | tf_op jit(solution)/shard_map/all_to_all | solution.py:396
  68.0 1.0 copy-start.4
  69.1 1.2 copy-start.5

commit v5 on v4

--- a/solution.py
+++ b/solution.py
@@ -22,7 +22,8 @@
 HALF = 32
 SEQ = ("zh", "y", "x", "c")
 PLANE = ("y", "x", "c")
-LEAD = 4 * BLOCK
+PAIRS = 7
+LEAD = 2 * BLOCK
 SHIFT = 2
 LOG2E = 1.4426950408889634
 COEF = LOG2E / math.sqrt(HD)
@@ -36,10 +37,27 @@
     return lax.dot_general(a, b, dims, preferred_element_type=jnp.float32)
 
 
-def attend_kernel(pos_ref, q_ref, *refs):
-    o_ref = refs[-1]
+def attend_kernel(pos_ref, q_from, *refs):
+    o_ref, q_all, held_all, sems = refs[-4:]
     pos = pos_ref[0]
-    p0, p1, p2, p3, held, ea, eb = [refs[2 * i : 2 * i + 2] for i in range(7)]
+    head = pl.program_id(0)
+
+    @pl.when(head == 0)
+    def _():
+        copies = [pltpu.make_async_copy(q_from, q_all, sems.at[PAIRS])]
+        for i in range(PAIRS):
+            copies.append(pltpu.make_async_copy(refs[i], held_all.at[i], sems.at[i]))
+        for copy in copies:
+            copy.start()
+        for copy in copies:
+            copy.wait()
+
+    cols = pl.ds(pl.multiple_of((head // GROUP) * HD, HD), HD)
+    sides = (slice(0, SHARD), slice(SHARD, 2 * SHARD))
+    p0, p1, p2, p3, held, ea, eb = [
+        [held_all.at[i, side, cols] for side in sides] for i in range(PAIRS)
+    ]
+    q_ref = q_all.at[:, pl.ds(pl.multiple_of(head * HD, HD), HD)]
     first = pos - NSEQ // 2
     keys, values = [p0[0][...]], [p0[1][...]]
     for side, out in ((0, keys), (1, values)):
@@ -82,26 +100,26 @@
 
 
 def attend(position, queries, pairs):
-    key_spec = pl.BlockSpec((SHARD, HD), lambda h: (0, h // GROUP))
-    value_spec = pl.BlockSpec((SHARD, HD), lambda h: (1, h // GROUP))
     return pl.pallas_call(
         attend_kernel,
         grid=(HEADS,),
         out_shape=jax.ShapeDtypeStruct((SHARD, HEADS * HD), jnp.bfloat16),
-        in_specs=[
-            pl.BlockSpec(memory_space=pltpu.SMEM),
-            pl.BlockSpec((SHARD, HD), lambda h: (0, h)),
-        ]
-        + [key_spec, value_spec] * len(pairs),
+        in_specs=[pl.BlockSpec(memory_space=pltpu.SMEM)]
+        + [pl.BlockSpec(memory_space=pl.ANY)] * (1 + PAIRS),
         out_specs=pl.BlockSpec((SHARD, HD), lambda h: (0, h)),
-        compiler_params=pltpu.CompilerParams(vmem_limit_bytes=32 * 1024 * 1024),
+        scratch_shapes=[
+            pltpu.VMEM((SHARD, HEADS * HD), jnp.bfloat16),
+            pltpu.VMEM((PAIRS, 2 * SHARD, KVS * HD), jnp.bfloat16),
+            pltpu.SemaphoreType.DMA((PAIRS + 1,)),
+        ],
+        compiler_params=pltpu.CompilerParams(vmem_limit_bytes=60 * 1024 * 1024),
         cost_estimate=pl.CostEstimate(
             flops=HEADS * SHARD * SHARD * 4 * HD * 4,
             bytes_accessed=4 * 1024 * 1024,
             transcendentals=HEADS * SHARD * SHARD * 4,
         ),
         name="attend",
-    )(position, queries, *[pair for pair in pairs for _ in range(2)])
+    )(position, queries, *pairs)
 
 
 SMEM = pl.BlockSpec(memory_space=pltpu.SMEM)
@@ -143,6 +161,33 @@
     return pl.ds(pl.multiple_of(unit * BLOCK + start, BLOCK), BLOCK)
 
 
+def near_kernel(base_ref, meta_ref, pair_ref, *refs):
+    out_ref = refs[-1]
+    out_ref[...] = jnp.zeros_like(out_ref)
+
+    def entry(c, head):
+        return meta_ref[c, head] - base_ref[0], meta_ref[KEEP + c, head]
+
+    def put(seat, unit, head):
+        cols = slice((head // GROUP) * HD, (head // GROUP + 1) * HD)
+        out_ref[seat, :BLOCK] = pair_ref[block_rows(unit, 0), cols]
+        out_ref[seat, BLOCK:] = pair_ref[block_rows(unit, SHARD), cols]
+
+    seats(entry, put)
+
+
+def pack_near(base, meta, pair, after):
+    return pl.pallas_call(
+        near_kernel,
+        out_shape=jax.ShapeDtypeStruct((HALF, 2 * BLOCK, HD), jnp.bfloat16),
+        in_specs=[SMEM, SMEM, VMEM] + [ANY] * len(after),
+        out_specs=VMEM,
+        compiler_params=pltpu.CompilerParams(vmem_limit_bytes=60 * 1024 * 1024),
+        cost_estimate=pl.CostEstimate(flops=0, bytes_accessed=3 * 1024 * 1024, transcendentals=0),
+        name="pack_near",
+    )(base, meta, pair, *after)
+
+
 def terms(value, count):
     parts = []
     for _ in range(count):
@@ -152,7 +197,7 @@
     return parts
 
 
-def pack_kernel(base_ref, meta_ref, list_ref, pair_ref, other_ref, mail_ref, got_ref, *refs):
+def far_kernel(base_ref, meta_ref, list_ref, held_ref, mail_ref, got_ref, *refs):
     out_ref, stats_ref, tile_ref = refs[-3:]
     last = base_ref[0] > 0
     mine = jnp.where(last, mail_ref[0:24], got_ref[24:48])
@@ -188,31 +233,30 @@
         picked = jnp.where(which == head, tile_ref[source, unit], 0.0).astype(jnp.bfloat16)
         out_ref[seat, tail] = out_ref[seat, tail] + picked
 
-    def put(source, held_ref, seat, unit, head):
+    def put(seat, unit, head):
         cols = slice((head // GROUP) * HD, (head // GROUP + 1) * HD)
-        start = 2 * BLOCK * source
-        out_ref[seat, start : start + BLOCK] = held_ref[block_rows(unit, 0), cols]
-        out_ref[seat, start + BLOCK : start + 2 * BLOCK] = held_ref[block_rows(unit, SHARD), cols]
-        add_score(source, seat, unit, head)
-
-    seats(my_entry, functools.partial(put, 0, pair_ref))
-    seats(other_entry, functools.partial(put, 1, other_ref))
-
-
-def pack(base, meta, pair, other_pair, mail, got, after):
-    return pl.pallas_call(
-        pack_kernel,
+        out_ref[seat, :BLOCK] = held_ref[block_rows(unit, 0), cols]
+        out_ref[seat, BLOCK:LEAD] = held_ref[block_rows(unit, SHARD), cols]
+        add_score(1, seat, unit, head)
+
+    seats(my_entry, functools.partial(add_score, 0))
+    seats(other_entry, put)
+
+
+def pack_far(base, meta, other_pair, mail, got, after):
+    return pl.pallas_call(
+        far_kernel,
         out_shape=(
             jax.ShapeDtypeStruct((HALF, LEAD + 32, HD), jnp.bfloat16),
             jax.ShapeDtypeStruct((24, 128), jnp.float32),
         ),
-        in_specs=[SMEM, SMEM, SMEM, VMEM, VMEM, VMEM, VMEM] + [ANY] * len(after),
+        in_specs=[SMEM, SMEM, SMEM, VMEM, VMEM, VMEM] + [ANY] * len(after),
         out_specs=(VMEM, VMEM),
         scratch_shapes=[pltpu.VMEM((2, BLKS, 16, 128), jnp.float32)],
         compiler_params=pltpu.CompilerParams(vmem_limit_bytes=16 * 1024 * 1024),
         cost_estimate=pl.CostEstimate(flops=0, bytes_accessed=3 * 1024 * 1024, transcendentals=0),
-        name="pack",
-    )(base, meta, got[48:56], pair, other_pair, mail, got, *after)
+        name="pack_far",
+    )(base, meta, got[48:56], other_pair, mail, got, *after)
 
 
 def score_keys(pos, q_ref, k_ref, mail_ref, start):
@@ -264,32 +308,52 @@
     )(position, observers, keys, other_keys, meta, *after)
 
 
-def sends(half, buf_ref, key_ref, value_ref, sems):
-    own, other = half * HALF, (1 - half) * HALF
-    most = HALF - SHIFT
-    pieces = (
-        (0, 0, own, HALF),
-        (1, SHIFT * half, other + SHIFT * (1 - half), most),
-        (1, most * (1 - half), other + most * half, SHIFT),
-    )
+def sends(pieces, buf_ref, outs, sems):
     copies = []
-    for number, (source, start, row, count) in enumerate(pieces):
-        for side, out_ref in enumerate((key_ref, value_ref)):
-            at_ = (2 * source + side) * BLOCK
+    for start, row, count in pieces:
+        for side, out_ref in enumerate(outs):
             copies.append(
                 pltpu.make_async_copy(
-                    buf_ref.at[pl.ds(start, count), at_ : at_ + BLOCK],
+                    buf_ref.at[pl.ds(start, count), side * BLOCK : (side + 1) * BLOCK],
                     out_ref.at[pl.ds(row, count)],
-                    sems.at[2 * number + side],
+                    sems.at[len(copies)],
                 )
             )
     return copies
 
 
+def place_kernel(half_ref, got_ref, key_ref, value_ref, sems):
+    copies = sends(((0, half_ref[0] * HALF, HALF),), got_ref, (key_ref, value_ref), sems)
+    for copy in copies:
+        copy.start()
+    for copy in copies:
+        copy.wait()
+
+
+def place_near(half, got):
+    shape = jax.ShapeDtypeStruct((NSEQ, BLOCK, HD), jnp.bfloat16)
+    return pl.pallas_call(
+        place_kernel,
+        out_shape=(shape, shape),
+        in_specs=[SMEM, VMEM],
+        out_specs=(ANY, ANY),
+        scratch_shapes=[pltpu.SemaphoreType.DMA((2,))],
+        compiler_params=pltpu.CompilerParams(vmem_limit_bytes=60 * 1024 * 1024),
+        cost_estimate=pl.CostEstimate(flops=0, bytes_accessed=4 * 1024 * 1024, transcendentals=0),
+        name="place_near",
+    )(half, got)
+
+
 def last_kernel(
-    half_ref, got_ref, stats_ref, key_ref, value_ref, recv_ref, block_ref, sems
+    half_ref, got_ref, stats_ref, _k, _v, key_ref, value_ref, recv_ref, block_ref, sems
 ):
-    copies = sends(half_ref[0], got_ref, key_ref, value_ref, sems)
+    half, most = half_ref[0], HALF - SHIFT
+    other = (1 - half) * HALF
+    pieces = (
+        (SHIFT * half, other + SHIFT * (1 - half), most),
+        (most * (1 - half), other + most * half, SHIFT),
+    )
+    copies = sends(pieces, got_ref, (key_ref, value_ref), sems)
     for copy in copies:
         copy.start()
     factor = BLKS * NSEQ / OBS
@@ -339,7 +403,7 @@
         copy.wait()
 
 
-def place(half, got, stats):
+def place_last(half, got, stats, earlier):
     shape = jax.ShapeDtypeStruct((NSEQ, BLOCK, HD), jnp.bfloat16)
     return pl.pallas_call(
         last_kernel,
@@ -349,13 +413,14 @@
             jax.ShapeDtypeStruct((1, NSEQ), jnp.bfloat16),
             jax.ShapeDtypeStruct((BLKS, HEADS), jnp.float32),
         ),
-        in_specs=[SMEM, VMEM, VMEM],
+        in_specs=[SMEM, VMEM, VMEM, ANY, ANY],
         out_specs=(ANY, ANY, VMEM, VMEM),
-        scratch_shapes=[pltpu.SemaphoreType.DMA((6,))],
+        scratch_shapes=[pltpu.SemaphoreType.DMA((4,))],
+        input_output_aliases={3: 0, 4: 1},
         compiler_params=pltpu.CompilerParams(vmem_limit_bytes=16 * 1024 * 1024),
         cost_estimate=pl.CostEstimate(flops=0, bytes_accessed=4 * 1024 * 1024, transcendentals=0),
-        name="place",
-    )(half, got, stats)
+        name="place_last",
+    )(half, got, stats, *earlier)
 
 
 def at(zh, y, x, c):
@@ -411,12 +476,14 @@
     edge_a = lax.ppermute(other_pair, SEQ, [(32, 33), (33, 32)])
     edge_b = lax.ppermute(other_pair, SEQ, [(33, 34), (63, 32)])
 
-    mail = observe(pos, levels[-1], pair, other_pair, meta, (one, two))
+    near = exchange(pack_near(base, meta, pair, (other_pair, one, two, three, levels[2], edge_a, edge_b)))
+    mail = observe(pos, levels[-1], pair, other_pair, meta, ())
     got = lax.ppermute(mail, SEQ, swap)
-    packed, stats = pack(base, meta, pair, other_pair, mail, got, (three, edge_a, edge_b))
-    arrived = exchange(packed)
+    packed, stats = pack_far(base, meta, other_pair, mail, got, ())
+    far = exchange(packed)
     attended = attend(pos, queries, [pair, one, two, three, other_pair, edge_a, edge_b])
-    recv_keys, recv_values, recv_scores, scores_here = place(near_half, arrived, stats)
+    first = place_near(near_half, near)
+    recv_keys, recv_values, recv_scores, scores_here = place_last(near_half, far, stats, first)
     return (
         attended,
         scores_here.T,

time: 130 us -> 130 us (level)
  waiting for transfers between devices: 65.1 us -> 55.8 us
  starting transfers between devices: 25.4 us -> 32.3 us
  Pallas kernels: 29.5 us -> 33.5 us
  local copies, waits for them, and re-layouts: 5.4 us -> 3.79 us
    all_to_all x1 -> x2, waiting for transfers between devices: 34.7 us -> 22.9 us  [exchange(): lax.all_to_all(packed, PLANE, split_axis=0, concat_axis=0, tiled=True)]
    ppermute x1, waiting for transfers between devices: 0.01 us -> 4.13 us  [shards(): edge_b = lax.ppermute(other_pair, SEQ, [(33, 34), (63, 32)])]
    all_to_all x1 -> x2, starting transfers between devices: 4.85 us -> 8.97 us  [exchange(): lax.all_to_all(packed, PLANE, split_axis=0, concat_axis=0, tiled=True)]
    ppermute x1, starting transfers between devices: 0.87 us -> 3.66 us  [shards(): got = lax.ppermute(mail, SEQ, swap)]
    pallas_call x2 -> x4, Pallas kernels: 7.11 us -> 9.86 us  [the longest x1 3.08 us: pack_near(): pl.pallas_call(near_kernel, out_shape=jax.ShapeDtypeStruct((HALF, 2 * BLO...]
    ppermute x1, waiting for transfers between devices: 11.2 us -> 8.92 us  [shards(): got = lax.ppermute(mail, SEQ, swap)]
    unnamed x12 -> x28, local copies, waits for them, and re-layouts: 5.39 us -> 3.19 us
  transfers between devices with their start and end apart: 15 -> 16, of which waited for: 4 -> 6; matrix products, arithmetic and copies ran while one was open for 3% -> 2% of each run, Pallas kernels for 16% -> 21%
where the time goes in v5:
time: 130 us; the launch traced here: 129 us
  waiting for transfers between devices  55.8 us (43%)
  Pallas kernels  33.5 us (26%)
  starting transfers between devices  32.3 us (25%)
  local copies, waits for them, and re-layouts  3.79 us (3%)
  other arithmetic  2.61 us (2%)
    all_to_all x2, waiting for transfers between devices, exchange(): lax.all_to_all(packed, PLANE, split_axis=0, concat_axis=0, tiled=True)  22.9 us
    pallas_call x1, Pallas kernels, attend(): pl.pallas_call(attend_kernel, grid=(HEADS,), out_shape=jax.ShapeDtypeStru...  20.9 us
    ppermute x1, waiting for transfers between devices, shards(): other_pair = lax.ppermute(pair, SEQ, swap)  18.6 us
    all_to_all x2, starting transfers between devices, exchange(): lax.all_to_all(packed, PLANE, split_axis=0, concat_axis=0, tiled=True)  8.97 us
    ppermute x1, waiting for transfers between devices, shards(): got = lax.ppermute(mail, SEQ, swap)  8.92 us
    ppermute x3, starting transfers between devices, hop(): return lax.ppermute(pair, SEQ, steps)  5.86 us
    ppermute x7, starting transfers between devices, spread(): came = [lax.ppermute(held, SEQ, pairs) for pairs in step]  5.3 us
    ppermute x1, starting transfers between devices, shards(): other_pair = lax.ppermute(pair, SEQ, swap)  5.27 us
  transfers between devices with their start and end apart: 16, of which 6 were waited for; matrix products, arithmetic and copies ran while one was open for 2% of the time, Pallas kernels for 21%

profile of v5, /device:TPU:192, one launch (start us, length us, event | category | flops | bytes accessed | tf_op | source)
XLA Modules:
  0.0 129.0 jit_solution(11916931384945665865)
XLA Ops:
  0.6 0.0 copy-start.11
  0.7 1.9 %join.1.refs_0_.k_ref.pair_ref = bf16[1024,256]{1,0:T(8,128)(2,1)} custom-call(bf16[512,256]{1,0:T(8,128)(2,1)} %k_ref.1, bf16[512,256]{1,0:T(8,128)(2,1)} %v_ref.1), custom_call_target="tpu_custom_call" | custom-call | bytes 1048576 | tf_op jit(solution)/shard_map/join/pallas_call | solution.py:142
  2.5 5.3 %collective-permute-start.3 = (bf16[1024,256]{1,0:T(8,128)(2,1)}, bf16[1024,256]{1,0:T(8,128)(2,1)S(1)}, u32[]{:S(2)}, u32[]{:S(2)}) collective-permute-start(bf16[1024,256]{1,0:T(8,128)(2,1)} %join.1.refs_0_.k_ref.pair_ref), channel_id=1, source_target_pairs={{0,136},{136,0},{4,140},{140,4},{8,144},{144,8},{12,148},{148,12},... | collective-permute-start | bytes 1572872 | tf_op jit(solution)/shard_map/ppermute | solution.py:473
  7.8 1.3 %collective-permute-start.1 = (bf16[1024,256]{1,0:T(8,128)(2,1)}, bf16[1024,256]{1,0:T(8,128)(2,1)S(1)}, u32[]{:S(2)}, u32[]{:S(2)}) collective-permute-start(bf16[1024,256]{1,0:T(8,128)(2,1)} %join.1.refs_0_.k_ref.pair_ref), channel_id=1, source_target_pairs={{0,8},{4,12},{8,16},{12,20},{16,24},{20,28},{24,32},{28,36},{32,40... | collective-permute-start | bytes 1572872 | tf_op jit(solution)/shard_map/ppermute | solution.py:465
  9.1 0.9 slice_select_fusion
  10.1 0.7 collective-permute-start.7
  10.7 0.7 collective-permute-start.8
  11.4 0.7 collective-permute-start.6
  12.1 0.0 collective-permute-done.7
  12.1 0.0 collective-permute-done.8
  12.1 0.0 collective-permute-done.6
  12.1 1.0 add_add_fusion.1
  13.1 0.7 collective-permute-start.11
  13.7 0.7 collective-permute-start.10
  14.4 0.7 collective-permute-start.9
  15.1 0.0 collective-permute-done.11
  15.1 2.1 %collective-permute-start = (bf16[1024,256]{1,0:T(8,128)(2,1)}, bf16[1024,256]{1,0:T(8,128)(2,1)S(1)}, u32[]{:S(2)}, u32[]{:S(2)}) collective-permute-start(bf16[1024,256]{1,0:T(8,128)(2,1)} %join.1.refs_0_.k_ref.pair_ref), channel_id=1, source_target_pairs={{0,4},{4,8},{8,12},{12,16},{16,20},{20,24},{24,28},{28,32},{32,36}... | collective-permute-start | bytes 1572872 | tf_op jit(solution)/shard_map/ppermute | solution.py:465
  17.2 18.6 %collective-permute-done.3.refs_4_.other_ref.held_ref.refs_0_ = bf16[1024,256]{1,0:T(8,128)(2,1)S(1)} collective-permute-done((bf16[1024,256]{1,0:T(8,128)(2,1)}, bf16[1024,256]{1,0:T(8,128)(2,1)S(1)}, u32[]{:S(2)}, u32[]{:S(2)}) %collective-permute-start.3) | collective-permute-done | bytes 524320 | tf_op jit(solution)/shard_map/ppermute | solution.py:473
  35.9 1.3 collective-permute-start.5
  37.1 0.0 collective-permute-done.10
  37.1 1.9 %collective-permute-start.4 = (bf16[1024,256]{1,0:T(8,128)(2,1)S(1)}, bf16[1024,256]{1,0:T(8,128)(2,1)S(1)}, u32[]{:S(2)}, u32[]{:S(2)}) collective-permute-start(bf16[1024,256]{1,0:T(8,128)(2,1)S(1)} %collective-permute-done.3.refs_4_.other_ref.held_ref.refs_0_), channel_id=1, source_target_pairs={{128,132},{132,128},{129,133},{133,129},{130,134},{134,130},{131,1... | collective-permute-start | bytes 1572872 | tf_op jit(solution)/shard_map/ppermute | solution.py:476
  39.1 0.0 collective-permute-done.1.refs_2_
  39.1 2.4 %collective-permute-start.2 = (bf16[1024,256]{1,0:T(8,128)(2,1)S(1)}, bf16[1024,256]{1,0:T(8,128)(2,1)S(1)}, u32[]{:S(2)}, u32[]{:S(2)}) collective-permute-start(bf16[1024,256]{1,0:T(8,128)(2,1)S(1)} %collective-permute-done.1.refs_2_), channel_id=1, source_target_pairs={{0,4},{4,8},{8,12},{12,16},{16,20},{20,24},{24,28},{28,32},{32,36}... | collective-permute-start | bytes 1572872 | tf_op jit(solution)/shard_map/ppermute | solution.py:465
  41.5 0.0 collective-permute-done.9
  41.6 1.3 %collective-permute-start.12 = (bf16[64,1024]{1,0:T(8,128)(2,1)S(1)}, bf16[64,1024]{1,0:T(8,128)(2,1)S(1)}, u32[]{:S(2)}, u32[]{:S(2)}) collective-permute-start(bf16[64,1024]{1,0:T(8,128)(2,1)S(1)} %add_add_fusion), channel_id=1, source_target_pairs={{132,128},{140,136},{148,144},{156,152},{164,160},{172,168},{180,1... | collective-permute-start | bytes 393224 | tf_op jit(solution)/shard_map/ppermute | solution.py:441
  42.9 0.6 pad.4.meta_ref
  43.5 1.3 collective-permute-done.12
  44.8 0.7 add.44.q_ref.refs_4_
  45.5 0.0 collective-permute-done.refs_1_
  45.5 4.1 %collective-permute-done.5.refs_6_ = bf16[1024,256]{1,0:T(8,128)(2,1)S(1)} collective-permute-done((bf16[1024,256]{1,0:T(8,128)(2,1)S(1)}, bf16[1024,256]{1,0:T(8,128)(2,1)S(1)}, u32[]{:S(2)}, u32[]{:S(2)}) %collective-permute-start.5) | collective-permute-done | bytes 524320 | tf_op jit(solution)/shard_map/ppermute | solution.py:477
  49.7 0.0 collective-permute-done.4.refs_5_
  49.7 0.0 collective-permute-done.2.refs_3_
  49.7 0.8 copy-done.8
  50.5 0.2 copy-done.9
  50.6 0.8 copy-done.10
  51.4 3.1 %pack_near.1 = bf16[32,256,128]{2,1,0:T(8,128)(2,1)} custom-call(s32[1]{0:T(128)S(6)} %mul.18.base_ref, s32[8,128]{1,0:T(8,128)} %pad.4.meta_ref, bf16[1024,256]{1,0:T(8,128)(2,1)} %join.1.refs_0_.k_ref.pair_ref, bf16[1024,256]{1,0:T(8,128)(2,1)} %copy-done.1, bf16[1024,256]{1,0:T(8,128)(2,1)} %copy-done.7, bf16[1024,256]{1,0:T(8,128)(2,1)} %copy-done.6, ...), custom_call_target="tpu_custom_call" | custom-call | bytes 3145728 | tf_op jit(solution)/shard_map/pack_near/pallas_call | solution.py:180
  54.5 4.9 %all-to-all-start.1 = ((bf16[32,256,128]{2,1,0:T(8,128)(2,1)}), bf16[32,256,128]{2,1,0:T(8,128)(2,1)}, u32[]{:S(2)}, u32[]{:S(2)}) async-start(bf16[32,256,128]{2,1,0:T(8,128)(2,1)} %pack_near.1), calls=%async_computation.1 | async-start | bytes 4194304 | tf_op jit(solution)/shard_map/all_to_all | solution.py:461
  59.5 0.8 observe.1.mail_ref
  60.3 3.7 %collective-permute-start.13 = (f32[56,128]{1,0:T(8,128)S(1)}, f32[56,128]{1,0:T(8,128)S(1)}, u32[]{:S(2)}, u32[]{:S(2)}) collective-permute-start(f32[56,128]{1,0:T(8,128)S(1)} %observe.1.mail_ref), channel_id=1, source_target_pairs={{0,136},{136,0},{4,140},{140,4},{8,144},{144,8},{12,148},{148,12},... | collective-permute-start | bytes 86024 | tf_op jit(solution)/shard_map/ppermute | solution.py:481
  64.0 8.9 %collective-permute-done.13.got_ref = f32[56,128]{1,0:T(8,128)S(1)} collective-permute-done((f32[56,128]{1,0:T(8,128)S(1)}, f32[56,128]{1,0:T(8,128)S(1)}, u32[]{:S(2)}, u32[]{:S(2)}) %collective-permute-start.13) | collective-permute-done | bytes 28704 | tf_op jit(solution)/shard_map/ppermute | solution.py:481
  72.9 1.8 %pack_far.1 = (bf16[32,288,128]{2,1,0:T(8,128)(2,1)S(1)}, f32[24,128]{1,0:T(8,128)S(1)}) custom-call(s32[1]{0:T(128)S(6)} %mul.18.base_ref, s32[8,128]{1,0:T(8,128)S(1)} %copy-done.5, f32[8,128]{1,0:T(8,128)S(1)} %slice.8.list_ref, bf16[1024,256]{1,0:T(8,128)(2,1)S(1)} %copy-done.2, f32[56,128]{1,0:T(8,128)S(1)} %observe.1.mail_ref, ...), custom_call_target="tpu_custom_call" | custom-call | bytes 3145728 | tf_op jit(solution)/shard_map/pack_far/pallas_call | solution.py:247
  74.7 1.4 %copy-done.3 = bf16[32,288,128]{2,1,0:T(8,128)(2,1)} copy-done((bf16[32,288,128]{2,1,0:T(8,128)(2,1)}, bf16[32,288,128]{2,1,0:T(8,128)(2,1)S(1)}, u32[]{:S(2)}) %copy-start.3) | copy-done | bytes 2359320
  76.1 13.7 %all-to-all-done.1.got_ref = bf16[32,256,128]{2,1,0:T(8,128)(2,1)} async-done(((bf16[32,256,128]{2,1,0:T(8,128)(2,1)}), bf16[32,256,128]{2,1,0:T(8,128)(2,1)}, u32[]{:S(2)}, u32[]{:S(2)}) %all-to-all-start.1) | async-done | bytes 2097184 | tf_op jit(solution)/shard_map/all_to_all | solution.py:461
  89.8 4.1 %all-to-all-start = ((bf16[32,288,128]{2,1,0:T(8,128)(2,1)}), bf16[32,288,128]{2,1,0:T(8,128)(2,1)S(1)}, u32[]{:S(2)}, u32[]{:S(2)}) async-start(bf16[32,288,128]{2,1,0:T(8,128)(2,1)} %copy-done.3), calls=%async_computation | async-start | bytes 4718592 | tf_op jit(solution)/shard_map/all_to_all | solution.py:461
  93.9 20.9 %attend.1 = bf16[512,1024]{1,0:T(8,128)(2,1)} custom-call(s32[1]{0:T(128)} %bitcast.pos_ref, bf16[512,1024]{1,0:T(8,128)(2,1)} %q_from.1, bf16[1024,256]{1,0:T(8,128)(2,1)} %join.1.refs_0_.k_ref.pair_ref, bf16[1024,256]{1,0:T(8,128)(2,1)} %copy-done.7, bf16[1024,256]{1,0:T(8,128)(2,1)} %copy-done.6, bf16[1024,256]{1,0:T(8,128)(2,1)} %copy-done.10, ...), custom_call_target="tpu_custom_call" | custom-call | flops 4294967296 | bytes 4194304 | tf_op jit(solution)/shard_map/attend/pallas_call | solution.py:103
  114.8 2.9 %place_near.1 = (bf16[64,128,128]{2,1,0:T(8,128)(2,1)}, bf16[64,128,128]{2,1,0:T(8,128)(2,1)}) custom-call(s32[1]{0:T(128)} %bitcast.1.half_ref, bf16[32,256,128]{2,1,0:T(8,128)(2,1)} %all-to-all-done.1.got_ref), custom_call_target="tpu_custom_call" | custom-call | bytes 4194304 | tf_op jit(solution)/shard_map/place_near/pallas_call | solution.py:335
  117.7 9.2 %all-to-all-done.got_ref = bf16[32,288,128]{2,1,0:T(8,128)(2,1)S(1)} async-done(((bf16[32,288,128]{2,1,0:T(8,128)(2,1)}), bf16[32,288,128]{2,1,0:T(8,128)(2,1)S(1)}, u32[]{:S(2)}, u32[]{:S(2)}) %all-to-all-start) | async-done | bytes 2359328 | tf_op jit(solution)/shard_map/all_to_all | solution.py:461
  126.9 2.1 %place_last.1 = (bf16[64,128,128]{2,1,0:T(8,128)(2,1)}, bf16[64,128,128]{2,1,0:T(8,128)(2,1)}, bf16[1,64]{1,0:T(2,128)(2,1)}, f32[4,8]{1,0:T(4,128)}) custom-call(s32[1]{0:T(128)} %bitcast.1.half_ref, bf16[32,288,128]{2,1,0:T(8,128)(2,1)S(1)} %all-to-all-done.got_ref, ...), custom_call_target="tpu_custom_call", output_to_operand_aliasing={{0}: (3, {}), {1}: (4, {})} | custom-call | bytes 4194304 | tf_op jit(solution)/shard_map/place_last/pallas_call | solution.py:408
  (27 shorter events, 0.1 us)
Async XLA Ops:
  0.6 42.3 %copy-start.11 = (s32[1,8,4]{1,2,0:T(4,128)S(1)}, s32[1,8,4]{1,2,0:T(4,128)}, u32[]{:S(2)}) copy-start(s32[1,8,4]{1,2,0:T(4,128)} %param.11) | copy-start | bytes 388
  0.6 42.3 %copy-start.13 = (s32[1,8]{1,0:T(1,128)S(1)}, s32[1,8]{1,0:T(1,128)}, u32[]{:S(2)}) copy-start(s32[1,8]{1,0:T(1,128)} %param.10) | copy-start | bytes 100
  0.7 42.3 %copy-start.12 = (s32[1,8,4]{1,2,0:T(4,128)S(1)}, s32[1,8,4]{1,2,0:T(4,128)}, u32[]{:S(2)}) copy-start(s32[1,8,4]{1,2,0:T(4,128)} %param.9) | copy-start | bytes 388
  2.5 33.3 %collective-permute-start.3 = (bf16[1024,256]{1,0:T(8,128)(2,1)}, bf16[1024,256]{1,0:T(8,128)(2,1)S(1)}, u32[]{:S(2)}, u32[]{:S(2)}) collective-permute-start(bf16[1024,256]{1,0:T(8,128)(2,1)} %join.1.refs_0_.k_ref.pair_ref), channel_id=1, source_target_pairs={{0,136},{136,0},{4,140},{140,4},{8,144},{144,8},{12,148},{148,12},... | collective-permute-start | bytes 1572872 | tf_op jit(solution)/shard_map/ppermute | solution.py:473
  7.8 31.3 %collective-permute-start.1 = (bf16[1024,256]{1,0:T(8,128)(2,1)}, bf16[1024,256]{1,0:T(8,128)(2,1)S(1)}, u32[]{:S(2)}, u32[]{:S(2)}) collective-permute-start(bf16[1024,256]{1,0:T(8,128)(2,1)} %join.1.refs_0_.k_ref.pair_ref), channel_id=1, source_target_pairs={{0,8},{4,12},{8,16},{12,20},{16,24},{20,28},{24,32},{28,36},{32,40... | collective-permute-start | bytes 1572872 | tf_op jit(solution)/shard_map/ppermute | solution.py:465
  10.1 2.0 %collective-permute-start.7 = (bf16[64,1024]{1,0:T(8,128)(2,1)S(1)}, bf16[64,1024]{1,0:T(8,128)(2,1)S(1)}, u32[]{:S(2)}, u32[]{:S(2)}) collective-permute-start(bf16[64,1024]{1,0:T(8,128)(2,1)S(1)} %slice_select_fusion), channel_id=1, source_target_pairs={{252,188},{253,189},{254,190},{255,191}} | collective-permute-start | bytes 393224 | tf_op jit(solution)/shard_map/ppermute | solution.py:441
  10.7 1.4 %collective-permute-start.8 = (bf16[64,1024]{1,0:T(8,128)(2,1)S(1)}, bf16[64,1024]{1,0:T(8,128)(2,1)S(1)}, u32[]{:S(2)}, u32[]{:S(2)}) collective-permute-start(bf16[64,1024]{1,0:T(8,128)(2,1)S(1)} %slice_select_fusion), channel_id=1, source_target_pairs={{252,220},{253,221},{254,222},{255,223}} | collective-permute-start | bytes 393224 | tf_op jit(solution)/shard_map/ppermute | solution.py:441
  11.4 0.7 collective-permute-start.6
  13.1 2.0 %collective-permute-start.11 = (bf16[64,1024]{1,0:T(8,128)(2,1)S(1)}, bf16[64,1024]{1,0:T(8,128)(2,1)S(1)}, u32[]{:S(2)}, u32[]{:S(2)}) collective-permute-start(bf16[64,1024]{1,0:T(8,128)(2,1)S(1)} %add_add_fusion.1), channel_id=1, source_target_pairs={{156,148},{188,180},{220,212},{252,244},{157,149},{189,181},{221,2... | collective-permute-start | bytes 393224 | tf_op jit(solution)/shard_map/ppermute | solution.py:441
  13.7 23.4 %collective-permute-start.10 = (bf16[64,1024]{1,0:T(8,128)(2,1)S(1)}, bf16[64,1024]{1,0:T(8,128)(2,1)S(1)}, u32[]{:S(2)}, u32[]{:S(2)}) collective-permute-start(bf16[64,1024]{1,0:T(8,128)(2,1)S(1)} %add_add_fusion.1), channel_id=1, source_target_pairs={{156,140},{188,172},{220,204},{252,236},{157,141},{189,173},{221,2... | collective-permute-start | bytes 393224 | tf_op jit(solution)/shard_map/ppermute | solution.py:441
  14.4 27.1 %collective-permute-start.9 = (bf16[64,1024]{1,0:T(8,128)(2,1)S(1)}, bf16[64,1024]{1,0:T(8,128)(2,1)S(1)}, u32[]{:S(2)}, u32[]{:S(2)}) collective-permute-start(bf16[64,1024]{1,0:T(8,128)(2,1)S(1)} %add_add_fusion.1), channel_id=1, source_target_pairs={{156,132},{188,164},{220,196},{252,228},{157,133},{189,165},{221,1... | collective-permute-start | bytes 393224 | tf_op jit(solution)/shard_map/ppermute | solution.py:441
  15.1 30.4 %collective-permute-start = (bf16[1024,256]{1,0:T(8,128)(2,1)}, bf16[1024,256]{1,0:T(8,128)(2,1)S(1)}, u32[]{:S(2)}, u32[]{:S(2)}) collective-permute-start(bf16[1024,256]{1,0:T(8,128)(2,1)} %join.1.refs_0_.k_ref.pair_ref), channel_id=1, source_target_pairs={{0,4},{4,8},{8,12},{12,16},{16,20},{20,24},{24,28},{28,32},{32,36}... | collective-permute-start | bytes 1572872 | tf_op jit(solution)/shard_map/ppermute | solution.py:465
  35.8 13.8 %copy-start.1 = (bf16[1024,256]{1,0:T(8,128)(2,1)}, bf16[1024,256]{1,0:T(8,128)(2,1)S(1)}, u32[]{:S(2)}) copy-start(bf16[1024,256]{1,0:T(8,128)(2,1)S(1)} %collective-permute-done.3.refs_4_.other_ref.held_ref.refs_0_) | copy-start | bytes 1572868
  35.9 13.8 %collective-permute-start.5 = (bf16[1024,256]{1,0:T(8,128)(2,1)S(1)}, bf16[1024,256]{1,0:T(8,128)(2,1)S(1)}, u32[]{:S(2)}, u32[]{:S(2)}) collective-permute-start(bf16[1024,256]{1,0:T(8,128)(2,1)S(1)} %collective-permute-done.3.refs_4_.other_ref.held_ref.refs_0_), channel_id=1, source_target_pairs={{132,136},{252,128},{133,137},{253,129},{134,138},{254,130},{135,1... | collective-permute-start | bytes 1572872 | tf_op jit(solution)/shard_map/ppermute | solution.py:477
  37.1 12.5 %collective-permute-start.4 = (bf16[1024,256]{1,0:T(8,128)(2,1)S(1)}, bf16[1024,256]{1,0:T(8,128)(2,1)S(1)}, u32[]{:S(2)}, u32[]{:S(2)}) collective-permute-start(bf16[1024,256]{1,0:T(8,128)(2,1)S(1)} %collective-permute-done.3.refs_4_.other_ref.held_ref.refs_0_), channel_id=1, source_target_pairs={{128,132},{132,128},{129,133},{133,129},{130,134},{134,130},{131,1... | collective-permute-start | bytes 1572872 | tf_op jit(solution)/shard_map/ppermute | solution.py:476
  39.1 10.6 %copy-start.6 = (bf16[1024,256]{1,0:T(8,128)(2,1)}, bf16[1024,256]{1,0:T(8,128)(2,1)S(1)}, u32[]{:S(2)}) copy-start(bf16[1024,256]{1,0:T(8,128)(2,1)S(1)} %collective-permute-done.1.refs_2_) | copy-start | bytes 1572868
  39.1 10.6 %collective-permute-start.2 = (bf16[1024,256]{1,0:T(8,128)(2,1)S(1)}, bf16[1024,256]{1,0:T(8,128)(2,1)S(1)}, u32[]{:S(2)}, u32[]{:S(2)}) collective-permute-start(bf16[1024,256]{1,0:T(8,128)(2,1)S(1)} %collective-permute-done.1.refs_2_), channel_id=1, source_target_pairs={{0,4},{4,8},{8,12},{12,16},{16,20},{20,24},{24,28},{28,32},{32,36}... | collective-permute-start | bytes 1572872 | tf_op jit(solution)/shard_map/ppermute | solution.py:465
  41.6 3.2 %collective-permute-start.12 = (bf16[64,1024]{1,0:T(8,128)(2,1)S(1)}, bf16[64,1024]{1,0:T(8,128)(2,1)S(1)}, u32[]{:S(2)}, u32[]{:S(2)}) collective-permute-start(bf16[64,1024]{1,0:T(8,128)(2,1)S(1)} %add_add_fusion), channel_id=1, source_target_pairs={{132,128},{140,136},{148,144},{156,152},{164,160},{172,168},{180,1... | collective-permute-start | bytes 393224 | tf_op jit(solution)/shard_map/ppermute | solution.py:441
  45.5 4.2 %copy-start.7 = (bf16[1024,256]{1,0:T(8,128)(2,1)}, bf16[1024,256]{1,0:T(8,128)(2,1)S(1)}, u32[]{:S(2)}) copy-start(bf16[1024,256]{1,0:T(8,128)(2,1)S(1)} %collective-permute-done.refs_1_) | copy-start | bytes 1572868
  49.7 0.8 copy-start.8
  49.7 1.0 copy-start.9
  50.6 0.8 copy-start.10
  54.5 4.9 %copy-start = (bf16[1024,256]{1,0:T(8,128)(2,1)S(1)}, bf16[1024,256]{1,0:T(8,128)(2,1)}, u32[]{:S(2)}) copy-start(bf16[1024,256]{1,0:T(8,128)(2,1)} %join.1.refs_0_.k_ref.pair_ref) | copy-start | bytes 1572868
  54.5 4.9 %copy-start.2 = (bf16[1024,256]{1,0:T(8,128)(2,1)S(1)}, bf16[1024,256]{1,0:T(8,128)(2,1)}, u32[]{:S(2)}) copy-start(bf16[1024,256]{1,0:T(8,128)(2,1)} %copy-done.1) | copy-start | bytes 1572868
  54.5 4.9 %copy-start.4 = (bf16[64,1024]{1,0:T(8,128)(2,1)S(1)}, bf16[64,1024]{1,0:T(8,128)(2,1)}, u32[]{:S(2)}) copy-start(bf16[64,1024]{1,0:T(8,128)(2,1)} %add.44.q_ref.refs_4_) | copy-start | bytes 393220
  54.5 5.0 %copy-start.5 = (s32[8,128]{1,0:T(8,128)S(1)}, s32[8,128]{1,0:T(8,128)}, u32[]{:S(2)}) copy-start(s32[8,128]{1,0:T(8,128)} %pad.4.meta_ref) | copy-start | bytes 12292
  54.5 35.3 %all-to-all-start.1 = ((bf16[32,256,128]{2,1,0:T(8,128)(2,1)}), bf16[32,256,128]{2,1,0:T(8,128)(2,1)}, u32[]{:S(2)}, u32[]{:S(2)}) async-start(bf16[32,256,128]{2,1,0:T(8,128)(2,1)} %pack_near.1), calls=%async_computation.1 | async-start | bytes 4194304 | tf_op jit(solution)/shard_map/all_to_all | solution.py:461
  60.3 12.6 %collective-permute-start.13 = (f32[56,128]{1,0:T(8,128)S(1)}, f32[56,128]{1,0:T(8,128)S(1)}, u32[]{:S(2)}, u32[]{:S(2)}) collective-permute-start(f32[56,128]{1,0:T(8,128)S(1)} %observe.1.mail_ref), channel_id=1, source_target_pairs={{0,136},{136,0},{4,140},{140,4},{8,144},{144,8},{12,148},{148,12},... | collective-permute-start | bytes 86024 | tf_op jit(solution)/shard_map/ppermute | solution.py:481
  74.7 1.4 %copy-start.3 = (bf16[32,288,128]{2,1,0:T(8,128)(2,1)}, bf16[32,288,128]{2,1,0:T(8,128)(2,1)S(1)}, u32[]{:S(2)}) copy-start(bf16[32,288,128]{2,1,0:T(8,128)(2,1)S(1)} %get-tuple-element.13) | copy-start | bytes 7077892
  89.8 37.2 %all-to-all-start = ((bf16[32,288,128]{2,1,0:T(8,128)(2,1)}), bf16[32,288,128]{2,1,0:T(8,128)(2,1)S(1)}, u32[]{:S(2)}, u32[]{:S(2)}) async-start(bf16[32,288,128]{2,1,0:T(8,128)(2,1)} %copy-done.3), calls=%async_computation | async-start | bytes 4718592 | tf_op jit(solution)/shard_map/all_to_all | solution.py:461

commit v6 on v5

--- a/solution.py
+++ b/solution.py
@@ -476,7 +476,7 @@
     edge_a = lax.ppermute(other_pair, SEQ, [(32, 33), (33, 32)])
     edge_b = lax.ppermute(other_pair, SEQ, [(33, 34), (63, 32)])
 
-    near = exchange(pack_near(base, meta, pair, (other_pair, one, two, three, levels[2], edge_a, edge_b)))
+    near = exchange(pack_near(base, meta, pair, (one, three, levels[2], edge_a, edge_b)))
     mail = observe(pos, levels[-1], pair, other_pair, meta, ())
     got = lax.ppermute(mail, SEQ, swap)
     packed, stats = pack_far(base, meta, other_pair, mail, got, ())

time: 130 us -> 130 us (level)
    unnamed x28 -> x26, local copies, waits for them, and re-layouts: 3.19 us -> 3.2 us
where the time goes in v6:
time: 130 us; the launch traced here: 129 us
  waiting for transfers between devices  55.9 us (43%)
  Pallas kernels  33.4 us (26%)
  starting transfers between devices  32.3 us (25%)
  local copies, waits for them, and re-layouts  3.8 us (3%)
  other arithmetic  2.6 us (2%)
    all_to_all x2, waiting for transfers between devices, exchange(): lax.all_to_all(packed, PLANE, split_axis=0, concat_axis=0, tiled=True)  22.9 us
    pallas_call x1, Pallas kernels, attend(): pl.pallas_call(attend_kernel, grid=(HEADS,), out_shape=jax.ShapeDtypeStru...  20.9 us
    ppermute x1, waiting for transfers between devices, shards(): other_pair = lax.ppermute(pair, SEQ, swap)  18.6 us
    all_to_all x2, starting transfers between devices, exchange(): lax.all_to_all(packed, PLANE, split_axis=0, concat_axis=0, tiled=True)  8.96 us
    ppermute x1, waiting for transfers between devices, shards(): got = lax.ppermute(mail, SEQ, swap)  8.88 us
    ppermute x3, starting transfers between devices, hop(): return lax.ppermute(pair, SEQ, steps)  5.86 us
    ppermute x7, starting transfers between devices, spread(): came = [lax.ppermute(held, SEQ, pairs) for pairs in step]  5.3 us
    ppermute x1, starting transfers between devices, shards(): other_pair = lax.ppermute(pair, SEQ, swap)  5.27 us
  transfers between devices with their start and end apart: 16, of which 6 were waited for; matrix products, arithmetic and copies ran while one was open for 2% of the time, Pallas kernels for 21%

profile of v6, /device:TPU:192, one launch (start us, length us, event | category | flops | bytes accessed | tf_op | source)
XLA Modules:
  0.0 129.0 jit_solution(3022365383239137720)
XLA Ops:
  0.6 0.0 copy-start.9
  0.7 1.9 %join.1.refs_0_.k_ref.pair_ref = bf16[1024,256]{1,0:T(8,128)(2,1)} custom-call(bf16[512,256]{1,0:T(8,128)(2,1)} %k_ref.1, bf16[512,256]{1,0:T(8,128)(2,1)} %v_ref.1), custom_call_target="tpu_custom_call" | custom-call | bytes 1048576 | tf_op jit(solution)/shard_map/join/pallas_call | solution.py:142
  2.5 5.3 %collective-permute-start.3 = (bf16[1024,256]{1,0:T(8,128)(2,1)}, bf16[1024,256]{1,0:T(8,128)(2,1)S(1)}, u32[]{:S(2)}, u32[]{:S(2)}) collective-permute-start(bf16[1024,256]{1,0:T(8,128)(2,1)} %join.1.refs_0_.k_ref.pair_ref), channel_id=1, source_target_pairs={{0,136},{136,0},{4,140},{140,4},{8,144},{144,8},{12,148},{148,12},... | collective-permute-start | bytes 1572872 | tf_op jit(solution)/shard_map/ppermute | solution.py:473
  7.8 1.3 %collective-permute-start.1 = (bf16[1024,256]{1,0:T(8,128)(2,1)}, bf16[1024,256]{1,0:T(8,128)(2,1)S(1)}, u32[]{:S(2)}, u32[]{:S(2)}) collective-permute-start(bf16[1024,256]{1,0:T(8,128)(2,1)} %join.1.refs_0_.k_ref.pair_ref), channel_id=1, source_target_pairs={{0,8},{4,12},{8,16},{12,20},{16,24},{20,28},{24,32},{28,36},{32,40... | collective-permute-start | bytes 1572872 | tf_op jit(solution)/shard_map/ppermute | solution.py:465
  9.1 0.9 slice_select_fusion
  10.1 0.7 collective-permute-start.7
  10.7 0.7 collective-permute-start.8
  11.4 0.7 collective-permute-start.6
  12.1 0.0 collective-permute-done.7
  12.1 0.0 collective-permute-done.8
  12.1 0.0 collective-permute-done.6
  12.1 1.0 add_add_fusion.1
  13.1 0.7 collective-permute-start.11
  13.7 0.7 collective-permute-start.10
  14.4 0.7 collective-permute-start.9
  15.1 0.0 collective-permute-done.11
  15.1 2.1 %collective-permute-start = (bf16[1024,256]{1,0:T(8,128)(2,1)}, bf16[1024,256]{1,0:T(8,128)(2,1)S(1)}, u32[]{:S(2)}, u32[]{:S(2)}) collective-permute-start(bf16[1024,256]{1,0:T(8,128)(2,1)} %join.1.refs_0_.k_ref.pair_ref), channel_id=1, source_target_pairs={{0,4},{4,8},{8,12},{12,16},{16,20},{20,24},{24,28},{28,32},{32,36}... | collective-permute-start | bytes 1572872 | tf_op jit(solution)/shard_map/ppermute | solution.py:465
  17.2 18.6 %collective-permute-done.3.refs_4_.other_ref.held_ref = bf16[1024,256]{1,0:T(8,128)(2,1)S(1)} collective-permute-done((bf16[1024,256]{1,0:T(8,128)(2,1)}, bf16[1024,256]{1,0:T(8,128)(2,1)S(1)}, u32[]{:S(2)}, u32[]{:S(2)}) %collective-permute-start.3) | collective-permute-done | bytes 524320 | tf_op jit(solution)/shard_map/ppermute | solution.py:473
  35.9 1.3 collective-permute-start.5
  37.1 0.0 collective-permute-done.10
  37.1 1.9 %collective-permute-start.4 = (bf16[1024,256]{1,0:T(8,128)(2,1)S(1)}, bf16[1024,256]{1,0:T(8,128)(2,1)S(1)}, u32[]{:S(2)}, u32[]{:S(2)}) collective-permute-start(bf16[1024,256]{1,0:T(8,128)(2,1)S(1)} %collective-permute-done.3.refs_4_.other_ref.held_ref), channel_id=1, source_target_pairs={{128,132},{132,128},{129,133},{133,129},{130,134},{134,130},{131,1... | collective-permute-start | bytes 1572872 | tf_op jit(solution)/shard_map/ppermute | solution.py:476
  39.1 0.0 collective-permute-done.1.refs_2_
  39.1 2.4 %collective-permute-start.2 = (bf16[1024,256]{1,0:T(8,128)(2,1)S(1)}, bf16[1024,256]{1,0:T(8,128)(2,1)S(1)}, u32[]{:S(2)}, u32[]{:S(2)}) collective-permute-start(bf16[1024,256]{1,0:T(8,128)(2,1)S(1)} %collective-permute-done.1.refs_2_), channel_id=1, source_target_pairs={{0,4},{4,8},{8,12},{12,16},{16,20},{20,24},{24,28},{28,32},{32,36}... | collective-permute-start | bytes 1572872 | tf_op jit(solution)/shard_map/ppermute | solution.py:465
  41.5 0.0 collective-permute-done.9
  41.6 1.3 %collective-permute-start.12 = (bf16[64,1024]{1,0:T(8,128)(2,1)S(1)}, bf16[64,1024]{1,0:T(8,128)(2,1)S(1)}, u32[]{:S(2)}, u32[]{:S(2)}) collective-permute-start(bf16[64,1024]{1,0:T(8,128)(2,1)S(1)} %add_add_fusion), channel_id=1, source_target_pairs={{132,128},{140,136},{148,144},{156,152},{164,160},{172,168},{180,1... | collective-permute-start | bytes 393224 | tf_op jit(solution)/shard_map/ppermute | solution.py:441
  42.9 0.6 pad.4.meta_ref
  43.5 1.3 collective-permute-done.12
  44.8 0.7 add.44.q_ref.refs_2_
  45.5 0.0 collective-permute-done.refs_1_.refs_0_
  45.5 4.1 %collective-permute-done.5.refs_6_.refs_4_ = bf16[1024,256]{1,0:T(8,128)(2,1)S(1)} collective-permute-done((bf16[1024,256]{1,0:T(8,128)(2,1)S(1)}, bf16[1024,256]{1,0:T(8,128)(2,1)S(1)}, u32[]{:S(2)}, u32[]{:S(2)}) %collective-permute-start.5) | collective-permute-done | bytes 524320 | tf_op jit(solution)/shard_map/ppermute | solution.py:477
  49.7 0.0 collective-permute-done.4.refs_5_.refs_3_
  49.7 0.0 collective-permute-done.2.refs_3_.refs_1_
  49.7 0.8 copy-done.6
  50.5 0.2 copy-done.7
  50.6 0.8 copy-done.8
  51.4 3.1 %pack_near.1 = bf16[32,256,128]{2,1,0:T(8,128)(2,1)} custom-call(s32[1]{0:T(128)S(6)} %mul.18.base_ref, s32[8,128]{1,0:T(8,128)} %pad.4.meta_ref, bf16[1024,256]{1,0:T(8,128)(2,1)} %join.1.refs_0_.k_ref.pair_ref, bf16[1024,256]{1,0:T(8,128)(2,1)} %copy-done.5, bf16[1024,256]{1,0:T(8,128)(2,1)} %copy-done.8, bf16[64,1024]{1,0:T(8,128)(2,1)} %add.44.q_ref.refs_2_, ...), custom_call_target="tpu_custom_call" | custom-call | bytes 3145728 | tf_op jit(solution)/shard_map/pack_near/pallas_call | solution.py:180
  54.5 4.9 %all-to-all-start.1 = ((bf16[32,256,128]{2,1,0:T(8,128)(2,1)}), bf16[32,256,128]{2,1,0:T(8,128)(2,1)}, u32[]{:S(2)}, u32[]{:S(2)}) async-start(bf16[32,256,128]{2,1,0:T(8,128)(2,1)} %pack_near.1), calls=%async_computation.1 | async-start | bytes 4194304 | tf_op jit(solution)/shard_map/all_to_all | solution.py:461
  59.5 0.8 observe.1.mail_ref
  60.3 3.7 %collective-permute-start.13 = (f32[56,128]{1,0:T(8,128)S(1)}, f32[56,128]{1,0:T(8,128)S(1)}, u32[]{:S(2)}, u32[]{:S(2)}) collective-permute-start(f32[56,128]{1,0:T(8,128)S(1)} %observe.1.mail_ref), channel_id=1, source_target_pairs={{0,136},{136,0},{4,140},{140,4},{8,144},{144,8},{12,148},{148,12},... | collective-permute-start | bytes 86024 | tf_op jit(solution)/shard_map/ppermute | solution.py:481
  64.0 8.9 %collective-permute-done.13.got_ref = f32[56,128]{1,0:T(8,128)S(1)} collective-permute-done((f32[56,128]{1,0:T(8,128)S(1)}, f32[56,128]{1,0:T(8,128)S(1)}, u32[]{:S(2)}, u32[]{:S(2)}) %collective-permute-start.13) | collective-permute-done | bytes 28704 | tf_op jit(solution)/shard_map/ppermute | solution.py:481
  72.9 1.8 %pack_far.1 = (bf16[32,288,128]{2,1,0:T(8,128)(2,1)S(1)}, f32[24,128]{1,0:T(8,128)S(1)}) custom-call(s32[1]{0:T(128)S(6)} %mul.18.base_ref, s32[8,128]{1,0:T(8,128)S(1)} %copy-done.4, f32[8,128]{1,0:T(8,128)S(1)} %slice.8.list_ref, bf16[1024,256]{1,0:T(8,128)(2,1)S(1)} %collective-permute-done.3.refs_4_.other_ref.held_ref, f32[56,128]{1,0:T(8,128)S(1)} %observe.1.mail_ref, ...), custom_call_target="tpu_custom_call" | custom-call | bytes 3145728 | tf_op jit(solution)/shard_map/pack_far/pallas_call | solution.py:247
  74.7 1.4 %copy-done.1 = bf16[32,288,128]{2,1,0:T(8,128)(2,1)} copy-done((bf16[32,288,128]{2,1,0:T(8,128)(2,1)}, bf16[32,288,128]{2,1,0:T(8,128)(2,1)S(1)}, u32[]{:S(2)}) %copy-start.1) | copy-done | bytes 2359320
  76.1 13.7 %all-to-all-done.1.got_ref = bf16[32,256,128]{2,1,0:T(8,128)(2,1)} async-done(((bf16[32,256,128]{2,1,0:T(8,128)(2,1)}), bf16[32,256,128]{2,1,0:T(8,128)(2,1)}, u32[]{:S(2)}, u32[]{:S(2)}) %all-to-all-start.1) | async-done | bytes 2097184 | tf_op jit(solution)/shard_map/all_to_all | solution.py:461
  89.8 4.1 %all-to-all-start = ((bf16[32,288,128]{2,1,0:T(8,128)(2,1)}), bf16[32,288,128]{2,1,0:T(8,128)(2,1)S(1)}, u32[]{:S(2)}, u32[]{:S(2)}) async-start(bf16[32,288,128]{2,1,0:T(8,128)(2,1)} %copy-done.1), calls=%async_computation | async-start | bytes 4718592 | tf_op jit(solution)/shard_map/all_to_all | solution.py:461
  93.8 20.9 %attend.1 = bf16[512,1024]{1,0:T(8,128)(2,1)} custom-call(s32[1]{0:T(128)} %bitcast.pos_ref, bf16[512,1024]{1,0:T(8,128)(2,1)} %q_from.1, bf16[1024,256]{1,0:T(8,128)(2,1)} %join.1.refs_0_.k_ref.pair_ref, bf16[1024,256]{1,0:T(8,128)(2,1)} %copy-done.5, bf16[1024,256]{1,0:T(8,128)(2,1)} %copy-done.12, bf16[1024,256]{1,0:T(8,128)(2,1)} %copy-done.8, ...), custom_call_target="tpu_custom_call" | custom-call | flops 4294967296 | bytes 4194304 | tf_op jit(solution)/shard_map/attend/pallas_call | solution.py:103
  114.8 2.9 %place_near.1 = (bf16[64,128,128]{2,1,0:T(8,128)(2,1)}, bf16[64,128,128]{2,1,0:T(8,128)(2,1)}) custom-call(s32[1]{0:T(128)} %bitcast.1.half_ref, bf16[32,256,128]{2,1,0:T(8,128)(2,1)} %all-to-all-done.1.got_ref), custom_call_target="tpu_custom_call" | custom-call | bytes 4194304 | tf_op jit(solution)/shard_map/place_near/pallas_call | solution.py:335
  117.7 9.2 %all-to-all-done.got_ref = bf16[32,288,128]{2,1,0:T(8,128)(2,1)S(1)} async-done(((bf16[32,288,128]{2,1,0:T(8,128)(2,1)}), bf16[32,288,128]{2,1,0:T(8,128)(2,1)S(1)}, u32[]{:S(2)}, u32[]{:S(2)}) %all-to-all-start) | async-done | bytes 2359328 | tf_op jit(solution)/shard_map/all_to_all | solution.py:461
  126.9 2.1 %place_last.1 = (bf16[64,128,128]{2,1,0:T(8,128)(2,1)}, bf16[64,128,128]{2,1,0:T(8,128)(2,1)}, bf16[1,64]{1,0:T(2,128)(2,1)}, f32[4,8]{1,0:T(4,128)}) custom-call(s32[1]{0:T(128)} %bitcast.1.half_ref, bf16[32,288,128]{2,1,0:T(8,128)(2,1)S(1)} %all-to-all-done.got_ref, ...), custom_call_target="tpu_custom_call", output_to_operand_aliasing={{0}: (3, {}), {1}: (4, {})} | custom-call | bytes 4194304 | tf_op jit(solution)/shard_map/place_last/pallas_call | solution.py:408
  (25 shorter events, 0.1 us)
Async XLA Ops:
  0.6 42.3 %copy-start.9 = (s32[1,8,4]{1,2,0:T(4,128)S(1)}, s32[1,8,4]{1,2,0:T(4,128)}, u32[]{:S(2)}) copy-start(s32[1,8,4]{1,2,0:T(4,128)} %param.11) | copy-start | bytes 388
  0.6 42.3 %copy-start.11 = (s32[1,8]{1,0:T(1,128)S(1)}, s32[1,8]{1,0:T(1,128)}, u32[]{:S(2)}) copy-start(s32[1,8]{1,0:T(1,128)} %param.10) | copy-start | bytes 100
  0.7 42.3 %copy-start.10 = (s32[1,8,4]{1,2,0:T(4,128)S(1)}, s32[1,8,4]{1,2,0:T(4,128)}, u32[]{:S(2)}) copy-start(s32[1,8,4]{1,2,0:T(4,128)} %param.9) | copy-start | bytes 388
  2.5 33.3 %collective-permute-start.3 = (bf16[1024,256]{1,0:T(8,128)(2,1)}, bf16[1024,256]{1,0:T(8,128)(2,1)S(1)}, u32[]{:S(2)}, u32[]{:S(2)}) collective-permute-start(bf16[1024,256]{1,0:T(8,128)(2,1)} %join.1.refs_0_.k_ref.pair_ref), channel_id=1, source_target_pairs={{0,136},{136,0},{4,140},{140,4},{8,144},{144,8},{12,148},{148,12},... | collective-permute-start | bytes 1572872 | tf_op jit(solution)/shard_map/ppermute | solution.py:473
  7.8 31.3 %collective-permute-start.1 = (bf16[1024,256]{1,0:T(8,128)(2,1)}, bf16[1024,256]{1,0:T(8,128)(2,1)S(1)}, u32[]{:S(2)}, u32[]{:S(2)}) collective-permute-start(bf16[1024,256]{1,0:T(8,128)(2,1)} %join.1.refs_0_.k_ref.pair_ref), channel_id=1, source_target_pairs={{0,8},{4,12},{8,16},{12,20},{16,24},{20,28},{24,32},{28,36},{32,40... | collective-permute-start | bytes 1572872 | tf_op jit(solution)/shard_map/ppermute | solution.py:465
  10.1 2.0 %collective-permute-start.7 = (bf16[64,1024]{1,0:T(8,128)(2,1)S(1)}, bf16[64,1024]{1,0:T(8,128)(2,1)S(1)}, u32[]{:S(2)}, u32[]{:S(2)}) collective-permute-start(bf16[64,1024]{1,0:T(8,128)(2,1)S(1)} %slice_select_fusion), channel_id=1, source_target_pairs={{252,188},{253,189},{254,190},{255,191}} | collective-permute-start | bytes 393224 | tf_op jit(solution)/shard_map/ppermute | solution.py:441
  10.7 1.4 %collective-permute-start.8 = (bf16[64,1024]{1,0:T(8,128)(2,1)S(1)}, bf16[64,1024]{1,0:T(8,128)(2,1)S(1)}, u32[]{:S(2)}, u32[]{:S(2)}) collective-permute-start(bf16[64,1024]{1,0:T(8,128)(2,1)S(1)} %slice_select_fusion), channel_id=1, source_target_pairs={{252,220},{253,221},{254,222},{255,223}} | collective-permute-start | bytes 393224 | tf_op jit(solution)/shard_map/ppermute | solution.py:441
  11.4 0.7 collective-permute-start.6
  13.1 2.0 %collective-permute-start.11 = (bf16[64,1024]{1,0:T(8,128)(2,1)S(1)}, bf16[64,1024]{1,0:T(8,128)(2,1)S(1)}, u32[]{:S(2)}, u32[]{:S(2)}) collective-permute-start(bf16[64,1024]{1,0:T(8,128)(2,1)S(1)} %add_add_fusion.1), channel_id=1, source_target_pairs={{156,148},{188,180},{220,212},{252,244},{157,149},{189,181},{221,2... | collective-permute-start | bytes 393224 | tf_op jit(solution)/shard_map/ppermute | solution.py:441
  13.7 23.4 %collective-permute-start.10 = (bf16[64,1024]{1,0:T(8,128)(2,1)S(1)}, bf16[64,1024]{1,0:T(8,128)(2,1)S(1)}, u32[]{:S(2)}, u32[]{:S(2)}) collective-permute-start(bf16[64,1024]{1,0:T(8,128)(2,1)S(1)} %add_add_fusion.1), channel_id=1, source_target_pairs={{156,140},{188,172},{220,204},{252,236},{157,141},{189,173},{221,2... | collective-permute-start | bytes 393224 | tf_op jit(solution)/shard_map/ppermute | solution.py:441
  14.4 27.1 %collective-permute-start.9 = (bf16[64,1024]{1,0:T(8,128)(2,1)S(1)}, bf16[64,1024]{1,0:T(8,128)(2,1)S(1)}, u32[]{:S(2)}, u32[]{:S(2)}) collective-permute-start(bf16[64,1024]{1,0:T(8,128)(2,1)S(1)} %add_add_fusion.1), channel_id=1, source_target_pairs={{156,132},{188,164},{220,196},{252,228},{157,133},{189,165},{221,1... | collective-permute-start | bytes 393224 | tf_op jit(solution)/shard_map/ppermute | solution.py:441
  15.1 30.4 %collective-permute-start = (bf16[1024,256]{1,0:T(8,128)(2,1)}, bf16[1024,256]{1,0:T(8,128)(2,1)S(1)}, u32[]{:S(2)}, u32[]{:S(2)}) collective-permute-start(bf16[1024,256]{1,0:T(8,128)(2,1)} %join.1.refs_0_.k_ref.pair_ref), channel_id=1, source_target_pairs={{0,4},{4,8},{8,12},{12,16},{16,20},{20,24},{24,28},{28,32},{32,36}... | collective-permute-start | bytes 1572872 | tf_op jit(solution)/shard_map/ppermute | solution.py:465
  35.8 37.0 %copy-start.2 = (bf16[1024,256]{1,0:T(8,128)(2,1)}, bf16[1024,256]{1,0:T(8,128)(2,1)S(1)}, u32[]{:S(2)}) copy-start(bf16[1024,256]{1,0:T(8,128)(2,1)S(1)} %collective-permute-done.3.refs_4_.other_ref.held_ref) | copy-start | bytes 1572868
  35.9 13.8 %collective-permute-start.5 = (bf16[1024,256]{1,0:T(8,128)(2,1)S(1)}, bf16[1024,256]{1,0:T(8,128)(2,1)S(1)}, u32[]{:S(2)}, u32[]{:S(2)}) collective-permute-start(bf16[1024,256]{1,0:T(8,128)(2,1)S(1)} %collective-permute-done.3.refs_4_.other_ref.held_ref), channel_id=1, source_target_pairs={{132,136},{252,128},{133,137},{253,129},{134,138},{254,130},{135,1... | collective-permute-start | bytes 1572872 | tf_op jit(solution)/shard_map/ppermute | solution.py:477
  37.1 12.5 %collective-permute-start.4 = (bf16[1024,256]{1,0:T(8,128)(2,1)S(1)}, bf16[1024,256]{1,0:T(8,128)(2,1)S(1)}, u32[]{:S(2)}, u32[]{:S(2)}) collective-permute-start(bf16[1024,256]{1,0:T(8,128)(2,1)S(1)} %collective-permute-done.3.refs_4_.other_ref.held_ref), channel_id=1, source_target_pairs={{128,132},{132,128},{129,133},{133,129},{130,134},{134,130},{131,1... | collective-permute-start | bytes 1572872 | tf_op jit(solution)/shard_map/ppermute | solution.py:476
  39.1 15.4 %copy-start.12 = (bf16[1024,256]{1,0:T(8,128)(2,1)}, bf16[1024,256]{1,0:T(8,128)(2,1)S(1)}, u32[]{:S(2)}) copy-start(bf16[1024,256]{1,0:T(8,128)(2,1)S(1)} %collective-permute-done.1.refs_2_) | copy-start | bytes 1572868
  39.1 10.6 %collective-permute-start.2 = (bf16[1024,256]{1,0:T(8,128)(2,1)S(1)}, bf16[1024,256]{1,0:T(8,128)(2,1)S(1)}, u32[]{:S(2)}, u32[]{:S(2)}) collective-permute-start(bf16[1024,256]{1,0:T(8,128)(2,1)S(1)} %collective-permute-done.1.refs_2_), channel_id=1, source_target_pairs={{0,4},{4,8},{8,12},{12,16},{16,20},{20,24},{24,28},{28,32},{32,36}... | collective-permute-start | bytes 1572872 | tf_op jit(solution)/shard_map/ppermute | solution.py:465
  41.6 3.2 %collective-permute-start.12 = (bf16[64,1024]{1,0:T(8,128)(2,1)S(1)}, bf16[64,1024]{1,0:T(8,128)(2,1)S(1)}, u32[]{:S(2)}, u32[]{:S(2)}) collective-permute-start(bf16[64,1024]{1,0:T(8,128)(2,1)S(1)} %add_add_fusion), channel_id=1, source_target_pairs={{132,128},{140,136},{148,144},{156,152},{164,160},{172,168},{180,1... | collective-permute-start | bytes 393224 | tf_op jit(solution)/shard_map/ppermute | solution.py:441
  45.5 4.2 %copy-start.5 = (bf16[1024,256]{1,0:T(8,128)(2,1)}, bf16[1024,256]{1,0:T(8,128)(2,1)S(1)}, u32[]{:S(2)}) copy-start(bf16[1024,256]{1,0:T(8,128)(2,1)S(1)} %collective-permute-done.refs_1_.refs_0_) | copy-start | bytes 1572868
  49.7 0.8 copy-start.6
  49.7 1.0 copy-start.7
  50.6 0.8 copy-start.8
  54.5 4.9 %copy-start = (bf16[1024,256]{1,0:T(8,128)(2,1)S(1)}, bf16[1024,256]{1,0:T(8,128)(2,1)}, u32[]{:S(2)}) copy-start(bf16[1024,256]{1,0:T(8,128)(2,1)} %join.1.refs_0_.k_ref.pair_ref) | copy-start | bytes 1572868
  54.5 4.9 %copy-start.3 = (bf16[64,1024]{1,0:T(8,128)(2,1)S(1)}, bf16[64,1024]{1,0:T(8,128)(2,1)}, u32[]{:S(2)}) copy-start(bf16[64,1024]{1,0:T(8,128)(2,1)} %add.44.q_ref.refs_2_) | copy-start | bytes 393220
  54.5 4.9 %copy-start.4 = (s32[8,128]{1,0:T(8,128)S(1)}, s32[8,128]{1,0:T(8,128)}, u32[]{:S(2)}) copy-start(s32[8,128]{1,0:T(8,128)} %pad.4.meta_ref) | copy-start | bytes 12292
  54.5 35.2 %all-to-all-start.1 = ((bf16[32,256,128]{2,1,0:T(8,128)(2,1)}), bf16[32,256,128]{2,1,0:T(8,128)(2,1)}, u32[]{:S(2)}, u32[]{:S(2)}) async-start(bf16[32,256,128]{2,1,0:T(8,128)(2,1)} %pack_near.1), calls=%async_computation.1 | async-start | bytes 4194304 | tf_op jit(solution)/shard_map/all_to_all | solution.py:461
  60.3 12.6 %collective-permute-start.13 = (f32[56,128]{1,0:T(8,128)S(1)}, f32[56,128]{1,0:T(8,128)S(1)}, u32[]{:S(2)}, u32[]{:S(2)}) collective-permute-start(f32[56,128]{1,0:T(8,128)S(1)} %observe.1.mail_ref), channel_id=1, source_target_pairs={{0,136},{136,0},{4,140},{140,4},{8,144},{144,8},{12,148},{148,12},... | collective-permute-start | bytes 86024 | tf_op jit(solution)/shard_map/ppermute | solution.py:481
  74.6 1.4 %copy-start.1 = (bf16[32,288,128]{2,1,0:T(8,128)(2,1)}, bf16[32,288,128]{2,1,0:T(8,128)(2,1)S(1)}, u32[]{:S(2)}) copy-start(bf16[32,288,128]{2,1,0:T(8,128)(2,1)S(1)} %get-tuple-element.13) | copy-start | bytes 7077892
  89.8 37.2 %all-to-all-start = ((bf16[32,288,128]{2,1,0:T(8,128)(2,1)}), bf16[32,288,128]{2,1,0:T(8,128)(2,1)S(1)}, u32[]{:S(2)}, u32[]{:S(2)}) async-start(bf16[32,288,128]{2,1,0:T(8,128)(2,1)} %copy-done.1), calls=%async_computation | async-start | bytes 4718592 | tf_op jit(solution)/shard_map/all_to_all | solution.py:461
